TPU v7x, 32 devices: a whole 2x2x4 slice. The times are simulated.
32 devices in a mesh: guide: 2 (over core), kv: 4 (over y, x), seq: 4 (over z).
Axes of the slice: x: 2, y: 2, z: 4, core: 2. Of those that a mesh axis runs over, the one named last changes fastest.
Arguments:
- hidden: bfloat16 [2, 8, 4608], P(None, None, ('guide', 'seq')), may hold values from -50 to 50
- lengths: int32 [2, 8], replicated, may hold values from 1 to 8192, as said below
- slot_owner: int32 [2, 8], replicated, may hold values from 0 to 7, each once within a row
- allowed_ids: int32 [65536], P(('kv', 'seq')), may hold values from 0 to 131071, as said below
- guidance: float32 [8], replicated, may hold values from 1 to 4
- pre_attn_gain: float32 [4608], P(('guide', 'seq')), may hold values from 0.1 to 1.9
- post_attn_gain: float32 [4608], P(('guide', 'seq')), may hold values from 0.4 to 2.1
- pre_ffw_gain: float32 [4608], P(('guide', 'seq')), may hold values from 0.1 to 1.9
- post_ffw_gain: float32 [4608], P(('guide', 'seq')), may hold values from 0.4 to 2.1
- final_gain: float32 [4608], P(('guide', 'seq')), may hold values from 0.1 to 1.9
- query_weight: bfloat16 [4608, 4096], P(('guide', 'seq'), 'kv'), may hold values from -0.09375 to 0.09375
- key_weight: bfloat16 [4608, 2048], P(('guide', 'seq'), 'kv'), may hold values from -0.09375 to 0.09375
- value_weight: bfloat16 [4608, 2048], P(('guide', 'seq'), 'kv'), may hold values from -0.09375 to 0.09375
- output_weight: bfloat16 [4096, 4608], P('kv', ('guide', 'seq')), may hold values from -1 to 1
- gate_weight: bfloat16 [4608, 36864], P(('guide', 'seq'), 'kv'), may hold values from -1 to 1
- up_weight: bfloat16 [4608, 36864], P(('guide', 'seq'), 'kv'), may hold values from -1 to 1
- down_weight: bfloat16 [36864, 4608], P('kv', ('guide', 'seq')), may hold values from -1 to 1
- embedding: bfloat16 [131072, 4608], P(('kv', 'seq'), 'guide'), may hold values from -1 to 1
- cond_keys: bfloat16 [8, 8192, 2048], P(None, ('guide', 'seq'), 'kv'), may hold values from -6 to 6
- cond_values: bfloat16 [8, 8192, 2048], P(None, ('guide', 'seq'), 'kv'), may hold values from -6 to 6
- uncond_keys: bfloat16 [8, 2048, 2048], P(None, ('guide', 'seq'), 'kv'), may hold values from -6 to 6
- uncond_values: bfloat16 [8, 2048, 2048], P(None, ('guide', 'seq'), 'kv'), may hold values from -6 to 6
Outputs:
- mixed: float32 [8, 65536], P('guide', ('kv', 'seq'))
Inputs may be any that keep to these rules, and one draw needn't show every extreme that they name: lengths[0] lies in 1 to 8192 and some request has exactly 8192; lengths[1] lies in 1 to 2048 and some request has exactly 2048. `slot_owner`: each row is a permutation of the 8 requests. `allowed_ids`: the ids of the i-th aligned block of 4096 entries are distinct and lie in rows i * 8192 to (i + 1) * 8192 - 1 of the table.
All inputs are finite; a program needn't handle non-finite values.
Results may differ from a plain program's by a relative error of at most 0.0039.
Values may be sent and summed in bfloat16 or wider, within the bound.
No kernel may reach another device: no remote copies, remote signals or barrier semaphores. Data moves between devices by JAX's collectives and lax.ppermute only.
A program may use at most 192 MiB of HBM per device.

v0:
```python
import jax
import jax.numpy as jnp
from jax import lax
from jax.sharding import PartitionSpec as P

D = 4608
H = 32
HD = 128


EPS = 1e-06
ATTN_CAP = 50.0
LOGIT_CAP = 30.0
THETA = 10000.0
HIGHEST = lax.Precision.HIGHEST


def rotary(values, position):
    half_size = values.shape[-1] // 2
    frequency = THETA ** (-2.0 * jnp.arange(half_size, dtype=jnp.float32) / values.shape[-1])
    angles = position[:, None, None] * frequency
    first_half = values[..., :half_size]
    second_half = values[..., half_size:]
    cosine = jnp.cos(angles)
    sine_part = jnp.sin(angles)
    return jnp.concatenate(
        [
            first_half * cosine - second_half * sine_part,
            second_half * cosine + first_half * sine_part,
        ],
        axis=-1,
    )


def to_slots(slot_pick, array):
    flat = array.astype(jnp.float32).reshape(array.shape[0], array.shape[1], -1)
    moved = jnp.einsum("gsr,gre->gse", slot_pick, flat, precision=HIGHEST)
    return moved.reshape(array.shape).astype(array.dtype)


def to_requests(slot_pick, array):
    flat = array.astype(jnp.float32).reshape(array.shape[0], array.shape[1], -1)
    moved = jnp.einsum("gsr,gse->gre", slot_pick, flat, precision=HIGHEST)
    return moved.reshape(array.shape).astype(array.dtype)


def attend_block(queries, key_block, value_block, slot_len, first_pos, tile_len):
    slot_count, block_len = (key_block.shape[0], key_block.shape[1])
    local_kv, group_size, head_size = (queries.shape[1], queries.shape[2], queries.shape[3])
    live_len = jnp.clip(jnp.max(slot_len) - first_pos, 0, block_len)
    tile_count = (live_len + tile_len - 1) // tile_len

    def one_tile(tile_index, carry):
        numer, denom = carry
        tile_start = tile_index * tile_len
        key_tile = lax.dynamic_slice_in_dim(key_block, tile_start, tile_len, 1).reshape(
            slot_count, tile_len, local_kv, head_size
        )
        value_tile = lax.dynamic_slice_in_dim(value_block, tile_start, tile_len, 1).reshape(
            slot_count, tile_len, local_kv, head_size
        )
        scores = jnp.einsum(
            "rkgd,rtkd->rkgt", queries, key_tile, preferred_element_type=jnp.float32
        )
        places = first_pos + tile_start + jnp.arange(tile_len, dtype=jnp.int32)
        visible = places[None, None, None, :] < slot_len[:, None, None, None]
        probs = jnp.where(visible, jnp.exp(ATTN_CAP * jnp.tanh(scores / ATTN_CAP)), 0.0)
        numer = numer + jnp.einsum(
            "rkgt,rtkd->rkgd",
            probs.astype(jnp.bfloat16),
            value_tile,
            preferred_element_type=jnp.float32,
        )
        denom = denom + jnp.sum(probs, axis=-1)
        return (numer, denom)

    start_numer = jnp.zeros((slot_count, local_kv, group_size, head_size), jnp.float32)
    start_denom = jnp.zeros((slot_count, local_kv, group_size), jnp.float32)
    return lax.fori_loop(0, tile_count, one_tile, (start_numer, start_denom))


def on_device(
    hidden,
    lengths,
    slot_owner,
    allowed_ids,
    guidance,
    pre_attn_gain,
    post_attn_gain,
    pre_ffw_gain,
    post_ffw_gain,
    final_gain,
    query_weight,
    key_weight,
    value_weight,
    output_weight,
    gate_weight,
    up_weight,
    down_weight,
    embedding,
    cond_keys,
    cond_values,
    uncond_keys,
    uncond_values,
):
    kinds, requests, width_local = hidden.shape
    stream_count = kinds * requests
    local_heads = query_weight.shape[1] // HD
    local_kv = key_weight.shape[1] // HD
    group_size = local_heads // local_kv
    streams = hidden.astype(jnp.float32)
    normed = (streams * pre_attn_gain).astype(jnp.bfloat16).reshape(stream_count, width_local)
    query_part = jnp.dot(normed, query_weight, preferred_element_type=jnp.float32)
    key_part = jnp.dot(normed, key_weight, preferred_element_type=jnp.float32)
    value_part = jnp.dot(normed, value_weight, preferred_element_type=jnp.float32)
    square_part = jnp.sum(streams * streams, axis=-1)
    square_sum, query_sum, key_sum, value_sum = lax.psum(
        (square_part, query_part, key_part, value_part), ("guide", "seq")
    )
    row_scale = lax.rsqrt(square_sum / D + EPS).reshape(stream_count, 1)
    position = lengths.astype(jnp.float32).reshape(stream_count)
    queries = (
        rotary((query_sum * row_scale).reshape(stream_count, local_heads, HD), position)
        * (D // H) ** (-0.5)
    ).astype(jnp.bfloat16)
    new_keys = rotary((key_sum * row_scale).reshape(stream_count, local_kv, HD), position).astype(
        jnp.bfloat16
    )
    new_values = (value_sum * row_scale).astype(jnp.bfloat16)
    queries = queries.reshape(kinds, requests, local_kv, group_size, HD)
    new_keys = new_keys.reshape(kinds, requests, local_kv, HD)
    new_values = new_values.reshape(kinds, requests, local_kv, HD)
    matches = slot_owner[:, :, None] == jnp.arange(requests, dtype=jnp.int32)[None, None, :]
    slot_pick = matches.astype(jnp.float32)
    slot_len = jnp.sum(jnp.where(matches, lengths[:, None, :], 0), axis=-1)
    slot_queries = to_slots(slot_pick, queries)
    slot_keys = to_slots(slot_pick, new_keys)
    slot_values = to_slots(slot_pick, new_values)
    guide_index = lax.axis_index("guide")
    seq_index = lax.axis_index("seq")
    block_index = guide_index * lax.axis_size("seq") + seq_index
    cond_len = cond_keys.shape[1]
    uncond_len = uncond_keys.shape[1]
    cond_numer, cond_denom = attend_block(
        slot_queries[0],
        cond_keys,
        cond_values,
        slot_len[0],
        block_index * cond_len,
        min(256, cond_len),
    )
    uncond_numer, uncond_denom = attend_block(
        slot_queries[1],
        uncond_keys,
        uncond_values,
        slot_len[1],
        block_index * uncond_len,
        min(256, uncond_len),
    )
    numer_part = jnp.stack([cond_numer, uncond_numer])
    denom_part = jnp.stack([cond_denom, uncond_denom])
    numer_sum, denom_sum = lax.psum((numer_part, denom_part), ("guide", "seq"))
    own_score = jnp.einsum(
        "gskjd,gskd->gskj", slot_queries, slot_keys, preferred_element_type=jnp.float32
    )
    own_prob = jnp.exp(ATTN_CAP * jnp.tanh(own_score / ATTN_CAP))
    own_weight = own_prob.astype(jnp.bfloat16).astype(jnp.float32)
    numer_total = (
        numer_sum + own_weight[..., None] * slot_values.astype(jnp.float32)[:, :, :, None, :]
    )
    denom_total = denom_sum + own_prob
    attended_slots = (numer_total / denom_total[..., None]).astype(jnp.bfloat16)
    attended = to_requests(slot_pick, attended_slots).reshape(stream_count, local_heads * HD)
    out_part = jnp.dot(attended, output_weight, preferred_element_type=jnp.float32)
    projected = lax.psum(out_part, "kv").reshape(kinds, requests, width_local)
    branch_sq = lax.psum(jnp.sum(projected * projected, axis=-1), ("guide", "seq"))
    out_scale = lax.rsqrt(branch_sq / D + EPS)
    middle = streams + projected * out_scale[..., None] * post_attn_gain
    middle_sq = lax.psum(jnp.sum(middle * middle, axis=-1), ("guide", "seq"))
    ffw_in = (middle * pre_ffw_gain).astype(jnp.bfloat16).reshape(stream_count, width_local)
    ffw_scale = lax.rsqrt(middle_sq / D + EPS).reshape(stream_count, 1)
    gate_part = jnp.dot(ffw_in, gate_weight, preferred_element_type=jnp.float32)
    upward_part = jnp.dot(ffw_in, up_weight, preferred_element_type=jnp.float32)
    gate_sum, upward_sum = lax.psum((gate_part, upward_part), ("guide", "seq"))
    activ = (jax.nn.gelu(gate_sum * ffw_scale, approximate=True) * (upward_sum * ffw_scale)).astype(
        jnp.bfloat16
    )
    down_part = jnp.dot(activ, down_weight, preferred_element_type=jnp.float32)
    ffw_out = lax.psum(down_part, "kv").reshape(kinds, requests, width_local)
    ffw_sq = lax.psum(jnp.sum(ffw_out * ffw_out, axis=-1), ("guide", "seq"))
    branch_scale = lax.rsqrt(ffw_sq / D + EPS)
    last = middle + ffw_out * branch_scale[..., None] * post_ffw_gain
    last_sq = lax.psum(jnp.sum(last * last, axis=-1), ("guide", "seq"))
    final_scale = lax.rsqrt(last_sq / D + EPS)
    final_rows = (last * final_gain).astype(jnp.bfloat16)
    half_rows = lax.all_gather(final_rows, "seq", axis=2, tiled=True)
    table_rows = embedding.shape[0]
    block_first = (lax.axis_index("kv") * lax.axis_size("seq") + seq_index) * table_rows
    picked = jnp.take(embedding, allowed_ids - block_first, axis=0)
    logit_part = jnp.einsum(
        "sd,ad->sa",
        half_rows.reshape(stream_count, half_rows.shape[2]),
        picked,
        preferred_element_type=jnp.float32,
    )
    logit_term = jnp.transpose(logit_part.reshape(kinds, requests, picked.shape[0]), (1, 0, 2))
    logit_share = lax.psum_scatter(logit_term, "guide", scatter_dimension=0, tiled=True)
    half_req = requests // 2
    first_req = guide_index * half_req
    share_scale = jnp.transpose(
        lax.dynamic_slice_in_dim(final_scale, first_req, half_req, 1), (1, 0)
    )
    capped = LOGIT_CAP * jnp.tanh(logit_share * share_scale[:, :, None] / LOGIT_CAP)
    share_weight = lax.dynamic_slice_in_dim(guidance, first_req, half_req, 0)
    return capped[:, 1] + share_weight[:, None] * (capped[:, 0] - capped[:, 1])


def solution(mesh):
    return jax.shard_map(
        on_device,
        mesh=mesh,
        in_specs=(
            P(None, None, ("guide", "seq")),
            P(),
            P(),
            P(("kv", "seq")),
            P(),
            P(("guide", "seq")),
            P(("guide", "seq")),
            P(("guide", "seq")),
            P(("guide", "seq")),
            P(("guide", "seq")),
            P(("guide", "seq"), "kv"),
            P(("guide", "seq"), "kv"),
            P(("guide", "seq"), "kv"),
            P("kv", ("guide", "seq")),
            P(("guide", "seq"), "kv"),
            P(("guide", "seq"), "kv"),
            P("kv", ("guide", "seq")),
            P(("kv", "seq"), "guide"),
            P(None, ("guide", "seq"), "kv"),
            P(None, ("guide", "seq"), "kv"),
            P(None, ("guide", "seq"), "kv"),
            P(None, ("guide", "seq"), "kv"),
        ),
        out_specs=P("guide", ("kv", "seq")),
        check_vma=False,
    )
```

profile of v0, /device:TPU:0, one launch (start us, length us, event | category | flops | bytes accessed | tf_op | source)
XLA Modules:
  0.0 487.2 jit_solution(18035551585057274717)
XLA Ops:
  6.5 2.4 fusion.73
  9.0 0.8 fusion.55
  10.5 0.8 select_reduce_fusion
  11.9 18.5 %psum.99 = f32[2,8]{1,0:T(2,128)S(1)} all-reduce(f32[2,8]{1,0:T(2,128)S(1)} %fusion.55), channel_id=1, replica_groups=mesh['guide'=2,'kv'=4,'seq'=4] {'guide','seq'}, use_global_device_ids=true, to_apply=%region_4.0 | all-reduce | flops 16 | bytes 128 | tf_op jit(solution)/shard_map/psum | solution.py:117
  30.5 1.9 fusion.69
  32.4 1.9 fusion.71
  35.7 30.4 %all-reduce.9.cloned.1.call-done = f32[16,1024]{1,0:T(8,128)} async-done(((f32[16,1024]{1,0:T(8,128)}), f32[16,1024]{1,0:T(8,128)}) %all-reduce.9.cloned.1.call-update) | async-done | bytes 65552 | tf_op jit(solution)/shard_map/psum | solution.py:117
  66.1 0.9 multiply_bitcast_fusion
  68.2 2.3 while.27
  68.3 2.0 fusion.132
  70.6 48.5 %while.26 = (s32[]{:T(128)}, f32[8,4,2,128]{3,2,1,0:T(2,128)S(1)}, f32[8,4,2]{2,1,0:T(4,128)S(1)}, s32[]{:T(128)}, s32[]{:T(128)}, /*index=5*/s32[1,8]{1,0:T(1,1...) while((s32[]{:T(128)}, f32[8,4,2,128]{3,2,1,0:T(2,128)S(1)}, ...), condition=%wide.region_7.8_spmd, body=%wide.region_5.0_spmd.sunk | while | flops 8481031 | bytes 21126368 | solution.py:79
  70.7 4.0 constant_dynamic-slice_fusion.3
  74.7 2.4 copy.126
  77.2 2.1 fusion.128
  79.3 2.9 copy.125
  82.8 4.0 constant_dynamic-slice_fusion.3
  86.8 2.4 copy.126
  89.3 2.1 fusion.128
  91.4 2.9 copy.125
  95.0 4.0 constant_dynamic-slice_fusion.3
  98.9 2.4 copy.126
  101.4 2.1 fusion.128
  103.5 2.9 copy.125
  107.1 4.0 constant_dynamic-slice_fusion.3
  111.0 2.4 copy.126
  113.5 2.1 fusion.128
  115.6 2.9 copy.125
  120.7 48.2 %all-reduce.15.cloned.1.call-done = (f32[2,8,4,2]{1,2,3,0:T(4,128)}, f32[16,512]{1,0:T(8,128)}, f32[16,512]{1,0:T(8,128)}) async-done(((f32[2,8,4,2]{1,2,3,0:T(4,128)}, f32[16,512]{1,0:T(8,128)}, f32[16,512]{1,0:T(8,128)}), (f32[2,8,4,2]{1,2,3,0:T(4,128)}, f32[16,512]{1,0:T(8,128)}, f32[16,512]{1,0:T(8,128)})) %all-reduce.15.cloned.1.call-update) | async-done | bytes 66064 | tf_op jit(solution)/shard_map/psum | solution.py:162
  168.9 0.8 broadcast_multiply_fusion
  170.4 1.0 fusion.29
  171.4 0.7 fusion.84
  172.4 54.7 %all-reduce.11.cloned.1.call-done = f32[2,8,4,2,128]{4,3,2,1,0:T(2,128)} async-done(((f32[2,8,4,2,128]{4,3,2,1,0:T(2,128)}), f32[2,8,4,2,128]{4,3,2,1,0:T(2,128)}) %all-reduce.11.cloned.1.call-update) | async-done | bytes 65552 | tf_op jit(solution)/shard_map/psum | solution.py:162
  227.1 1.0 fusion.53
  228.7 16.6 %psum.104 = f32[16,576]{1,0:T(8,128)S(1)} all-reduce(f32[16,576]{1,0:T(8,128)S(1)} %fusion.96), channel_id=1, replica_groups=mesh['guide'=2,'kv'=4,'seq'=4] {'kv'}, use_global_device_ids=true, to_apply=%region_16.17 | all-reduce | flops 9216 | bytes 73728 | tf_op jit(solution)/shard_map/psum | solution.py:175
  245.6 14.2 %psum.105 = f32[2,8]{1,0:T(2,128)S(1)} all-reduce(f32[2,8]{1,0:T(2,128)S(1)} %reduce_sum.81), channel_id=1, replica_groups=mesh['guide'=2,'kv'=4,'seq'=4] {'guide','seq'}, use_global_device_ids=true, to_apply=%region_18.19 | all-reduce | flops 16 | bytes 128 | tf_op jit(solution)/shard_map/psum | solution.py:176
  260.0 6.5 %fusion.78 = f32[16,9216]{1,0:T(8,128)} fusion(bf16[576,9216]{1,0:T(8,128)(2,1)} %param.41, f32[2,8,576]{2,1,0:T(8,128)S(1)} %get-tuple-element.242, f32[576]{0:T(1024)S(1)} %copy-done.4), kind=kOutput, calls=%fused_computation.117 | convolution fusion | flops 169887744 | bytes 11245824 | tf_op jit(solution)/shard_map/dot_general | solution.py:183
  266.4 6.5 %fusion.80 = f32[16,9216]{1,0:T(8,128)} fusion(bf16[576,9216]{1,0:T(8,128)(2,1)} %param.40, f32[2,8,576]{2,1,0:T(8,128)S(1)} %get-tuple-element.242, f32[576]{0:T(1024)S(1)} %copy-done.4), kind=kOutput, calls=%fused_computation.118 | convolution fusion | flops 169887744 | bytes 11245824 | tf_op jit(solution)/shard_map/dot_general | solution.py:182
  273.0 100.6 %gather_fusion = bf16[4096,2304]{1,0:T(8,128)(2,1)} fusion(bf16[8192,2304]{1,0:T(8,128)(2,1)} %param.43, s32[4096]{0:T(1024)S(1)} %fusion.68), kind=kCustom, calls=%fused_computation | custom fusion | bytes 37765120 | tf_op jit(solution)/shard_map/jit(_take)/gather | solution.py:199
  374.9 15.5 %psum.107 = f32[2,8]{1,0:T(2,128)S(1)} all-reduce(f32[2,8]{1,0:T(2,128)S(1)} %get-tuple-element.241), channel_id=1, replica_groups=mesh['guide'=2,'kv'=4,'seq'=4] {'guide','seq'}, use_global_device_ids=true, to_apply=%region_21.22 | all-reduce | flops 16 | bytes 128 | tf_op jit(solution)/shard_map/psum | solution.py:179
  390.6 7.3 %fusion.39 = f32[16,576]{1,0:T(8,128)S(1)} fusion(bf16[9216,576]{0,1:T(8,128)(2,1)} %param.42, f32[16,9216]{1,0:T(8,128)} %get-tuple-element.239, f32[16,9216]{1,0:T(8,128)} %get-tuple-element.240, f32[16]{0:T(128)S(1)} %mul.344), kind=kOutput, calls=%fused_computation.50 | convolution fusion | flops 171638784 | bytes 11833408 | tf_op jit(solution)/shard_map/dot_general | solution.py:188
  397.8 14.6 %psum.109 = f32[16,576]{1,0:T(8,128)S(1)} all-reduce(f32[16,576]{1,0:T(8,128)S(1)} %fusion.39), channel_id=1, replica_groups=mesh['guide'=2,'kv'=4,'seq'=4] {'kv'}, use_global_device_ids=true, to_apply=%region_23.24 | all-reduce | flops 9216 | bytes 73728 | tf_op jit(solution)/shard_map/psum | solution.py:189
  412.7 14.2 %psum.110 = f32[2,8]{1,0:T(2,128)S(1)} all-reduce(f32[2,8]{1,0:T(2,128)S(1)} %reduce_sum.84), channel_id=1, replica_groups=mesh['guide'=2,'kv'=4,'seq'=4] {'guide','seq'}, use_global_device_ids=true, to_apply=%region_25.26 | all-reduce | flops 16 | bytes 128 | tf_op jit(solution)/shard_map/psum | solution.py:190
  427.3 23.9 %all_gather.3 = bf16[2,8,2304]{1,0,2:T(2,128)(2,1)S(1)} all-gather(bf16[2,8,576]{1,0,2:T(2,128)(2,1)S(1)} %copy.87), channel_id=1, replica_groups=mesh['guide'=2,'kv'=4,'seq'=4] {'seq'}, dimensions={2}, use_global_device_ids=true | all-gather | bytes 92160 | tf_op jit(solution)/shard_map/all_gather | solution.py:196
  451.2 10.8 %fusion.19 = f32[8,2,4096]{2,0,1:T(8,128)} fusion(bf16[4096,2304]{1,0:T(8,128)(2,1)} %gather_fusion, pred[4096]{0:T(1024)(128)(4,1)S(1)} %compare_and_fusion, bf16[2,8,2304]{1,0,2:T(2,128)(2,1)S(1)} %all_gather.3), kind=kOutput, calls=%fused_computation.27 | convolution fusion | flops 311427072 | bytes 19214336 | tf_op jit(solution)/shard_map/sd,ad->sa/dot_general | solution.py:200
  462.0 14.1 %psum.111 = f32[2,8]{1,0:T(2,128)S(1)} all-reduce(f32[2,8]{1,0:T(2,128)S(1)} %get-tuple-element.247), channel_id=1, replica_groups=mesh['guide'=2,'kv'=4,'seq'=4] {'guide','seq'}, use_global_device_ids=true, to_apply=%region_28.29 | all-reduce | flops 16 | bytes 128 | tf_op jit(solution)/shard_map/psum | solution.py:193
  476.2 2.6 all-reduce.13.cloned.1.call-done
  478.9 1.1 fusion.48
  479.9 0.7 fusion.51
  (108 shorter events, 11.2 us)
Async XLA Ops:
  6.5 60.9 %copy-start = (bf16[8,256,512]{2,1,0:T(8,128)(2,1)S(1)}, bf16[8,256,512]{2,1,0:T(8,128)(2,1)}, u32[]{:S(2)}) copy-start(bf16[8,256,512]{2,1,0:T(8,128)(2,1)} %param.46) | copy-start | bytes 6291460
  6.5 60.7 %copy-start.6 = (s32[2,8]{1,0:T(2,128)S(1)}, s32[2,8]{1,0:T(2,128)}, u32[]{:S(2)}) copy-start(s32[2,8]{1,0:T(2,128)} %param.28) | copy-start | bytes 196
  6.5 59.6 %all-reduce.9.cloned.1.call-start = ((), (), s32[]{:S(2)}) async-start(), calls=%async_computation | async-start | bytes 131072 | tf_op jit(solution)/shard_map/psum | solution.py:117
  8.9 159.9 %all-reduce.15.cloned.1.call-start = ((), (), s32[]{:S(2)}) async-start(), calls=%async_computation.3 | async-start | bytes 147456 | tf_op jit(solution)/shard_map/psum | solution.py:162
  70.6 157.7 %copy-start.2 = (bf16[1024,576]{0,1:T(8,128)(2,1)S(1)}, bf16[1024,576]{0,1:T(8,128)(2,1)}, u32[]{:S(2)}) copy-start(bf16[1024,576]{0,1:T(8,128)(2,1)} %param.39) | copy-start | bytes 3538948
  119.1 140.7 %copy-start.3 = (bf16[2,8,576]{2,1,0:T(8,128)(2,1)S(1)}, bf16[2,8,576]{2,1,0:T(8,128)(2,1)}, u32[]{:S(2)}) copy-start(bf16[2,8,576]{2,1,0:T(8,128)(2,1)} %param.26) | copy-start | bytes 55300
  119.2 140.6 %copy-start.9 = (f32[576]{0:T(1024)S(1)}, f32[576]{0:T(1024)}, u32[]{:S(2)}) copy-start(f32[576]{0:T(1024)} %param.32) | copy-start | bytes 6916
  119.2 140.8 %copy-start.4 = (f32[576]{0:T(1024)S(1)}, f32[576]{0:T(1024)}, u32[]{:S(2)}) copy-start(f32[576]{0:T(1024)} %param.33) | copy-start | bytes 6916
  119.9 107.2 %all-reduce.11.cloned.1.call-start = ((), (), s32[]{:S(2)}) async-start(), calls=%async_computation.1 | async-start | bytes 131072 | tf_op jit(solution)/shard_map/psum | solution.py:162
  120.6 269.9 %all-reduce.17.cloned.1.call-start = ((), (), s32[]{:S(2)}) async-start(), calls=%async_computation.4 | async-start | bytes 2359296 | tf_op jit(solution)/shard_map/psum | solution.py:184
  266.4 6.5 %copy-start.5 = (s32[4096]{0:T(1024)S(1)}, s32[4096]{0:T(1024)}, u32[]{:S(2)}) copy-start(s32[4096]{0:T(1024)} %param.29) | copy-start | bytes 49156
  272.9 205.9 %all-reduce.13.cloned.1.call-start = ((), (), s32[]{:S(2)}) async-start(), calls=%async_computation.2 | async-start | bytes 524288
  273.0 100.6 %copy-start.11 = (u32[32]{0:T(128)S(1)}, u32[32]{0:T(128)}, u32[]{:S(2)}) copy-start(u32[32]{0:T(128)} %constant.142) | copy-start | bytes 388
  273.0 101.8 %copy-start.10 = (f32[8]{0:T(128)S(1)}, f32[8]{0:T(128)}, u32[]{:S(2)}) copy-start(f32[8]{0:T(128)} %param.30) | copy-start | bytes 100
  390.5 36.4 %copy-start.7 = (f32[576]{0:T(1024)S(1)}, f32[576]{0:T(1024)}, u32[]{:S(2)}) copy-start(f32[576]{0:T(1024)} %param.34) | copy-start | bytes 6916
  390.6 36.4 %copy-start.8 = (f32[576]{0:T(1024)S(1)}, f32[576]{0:T(1024)}, u32[]{:S(2)}) copy-start(f32[576]{0:T(1024)} %param.35) | copy-start | bytes 6916
  451.2 29.4 %copy-start.1 = (bf16[8,256,512]{2,1,0:T(8,128)(2,1)S(1)}, bf16[8,256,512]{2,1,0:T(8,128)(2,1)}, u32[]{:S(2)}) copy-start(bf16[8,256,512]{2,1,0:T(8,128)(2,1)} %param.46) | copy-start | bytes 6291460
Sparse Core Ops, SparseCore 0:
  9.7 56.3 all-reduce.8
  120.0 48.8 all-reduce.14
  171.2 55.8 all-reduce.10
  273.0 57.1 all-reduce.16
  462.1 16.6 all-reduce.12
where the time goes:
time: 490 us; the launch traced here: 487 us
  local copies, waits for them, and re-layouts  140 us (29%)
  waiting for transfers between devices  136 us (28%)
  blocking collectives  132 us (27%)
  matrix products  52.8 us (11%)
  between operations  15.3 us (3%)
  other arithmetic  11.2 us (2%)
    psum x2, waiting for transfers between devices, on_device(): numer_sum, denom_sum = lax.psum((numer_part, denom_part), ('guide', 'seq'))  103 us
    gather x1, local copies, waits for them, and re-layouts, on_device(): picked = jnp.take(embedding, allowed_ids - block_first, axis=0)  101 us
    psum x1, waiting for transfers between devices, on_device(): lax.psum((square_part, query_part, key_part, value_part), ('guide', 'seq'))  30.4 us
    dynamic_slice x8, local copies, waits for them, and re-layouts, one_tile(): lax.dynamic_slice_in_dim(value_block, tile_start, tile_len, 1)  27.3 us
    all_gather x1, blocking collectives, on_device(): half_rows = lax.all_gather(final_rows, 'seq', axis=2, tiled=True)  23.9 us
    psum x1, blocking collectives, on_device(): lax.psum((square_part, query_part, key_part, value_part), ('guide', 'seq'))  18.5 us
    psum x1, blocking collectives, on_device(): projected = lax.psum(out_part, 'kv').reshape(kinds, requests, width_local)  16.6 us
    psum x1, blocking collectives, on_device(): middle_sq = lax.psum(jnp.sum(middle * middle, axis=-1), ('guide', 'seq'))  15.5 us
  transfers between devices with their start and end apart: 5, of which 4 were waited for; matrix products, arithmetic and copies ran while one was open for 23% of the time, Pallas kernels for 0%

commit v1 on v0

--- a/solution.py
+++ b/solution.py
@@ -1,6 +1,8 @@
 import jax
 import jax.numpy as jnp
 from jax import lax
+from jax.experimental import pallas as pl
+from jax.experimental.pallas import tpu as pltpu
 from jax.sharding import PartitionSpec as P
 
 D = 4608
@@ -79,7 +81,7 @@
     return lax.fori_loop(0, tile_count, one_tile, (start_numer, start_denom))
 
 
-def on_device(
+def plain_layer(
     hidden,
     lengths,
     slot_owner,
@@ -215,6 +217,637 @@
     return capped[:, 1] + share_weight[:, None] * (capped[:, 0] - capped[:, 1])
 
 
+BF = jnp.bfloat16
+F32 = jnp.float32
+LANES = 128
+VMEM = pl.BlockSpec(memory_space=pltpu.VMEM)
+SMEM = pl.BlockSpec(memory_space=pltpu.SMEM)
+MIB = 1 << 20
+
+
+def nt_dot(a, b):
+    return lax.dot_general(a, b, (((1,), (1,)), ((), ())), preferred_element_type=F32)
+
+
+def nn_dot(a, b):
+    return jnp.dot(a, b, preferred_element_type=F32)
+
+
+def limit(mib):
+    return pltpu.CompilerParams(vmem_limit_bytes=mib * MIB)
+
+
+def columns_tile(values, rows):
+    lane = lax.broadcasted_iota(jnp.int32, (rows, LANES), 1)
+    tile = jnp.zeros((rows, LANES), F32)
+    for place, value in enumerate(values):
+        tile = jnp.where(lane == place, value, tile)
+    return tile
+
+
+def split_tile(tile):
+    high = tile.astype(BF).astype(F32)
+    rest = tile - high
+    middle = rest.astype(BF).astype(F32)
+    low = (rest - middle).astype(BF).astype(F32)
+    return (high + pltpu.roll(middle, 32, 1) + pltpu.roll(low, 64, 1)).astype(BF)
+
+
+def joined_tile(tile):
+    terms = tile.astype(F32)
+    total = terms + pltpu.roll(terms, LANES - 32, 1) + pltpu.roll(terms, LANES - 64, 1)
+    lane = lax.broadcasted_iota(jnp.int32, total.shape, 1)
+    return jnp.where(lane < 32, total, 0.0)
+
+
+def project_kernel(meta, hidden, gain, wq, wk, wv, rows, keep, send):
+    count = hidden.shape[0]
+    half = count // 2
+    group = half // 2
+    row = lax.broadcasted_iota(jnp.int32, (count, count), 0)
+    column = lax.broadcasted_iota(jnp.int32, (count, count), 1)
+    source = (row // group) % 2 * half + row // half * group + row % group
+    pick = jnp.where(column == source, 1.0, 0.0).astype(BF)
+    streams = nn_dot(pick, hidden[...])
+    rows[...] = streams.astype(BF)
+    square = jnp.sum(streams * streams, axis=-1, keepdims=True)
+    normed = (streams * gain[...]).astype(BF)
+    first = meta[0] == 0
+    offset = 0
+    for weight in (wq, wk, wv):
+        product = nn_dot(normed, weight[...])
+        width = product.shape[1] // 2
+        low, high = product[:, :width], product[:, width:]
+        keep[:, offset : offset + width] = jnp.where(first, low, high)
+        send[:, offset : offset + width] = jnp.where(first, high, low)
+        offset += width
+    tile = columns_tile([square], count)
+    keep[:, offset:] = tile
+    send[:, offset:] = tile
+
+
+def rope_kernel(head_dim, scale, cosine, sine, *refs):
+    parts, (out, squares) = refs[:-2], refs[-2:]
+    total = parts[0][...]
+    for part in parts[1:]:
+        total = total + part[...]
+    blocks = (total.shape[1] - LANES) // head_dim
+    tile = total[:, blocks * head_dim :]
+    squares[...] = tile
+    row_scale = lax.rsqrt(tile[:, :1] / D + EPS)
+    cosines, sines = cosine[...], sine[...]
+    for block in range(blocks):
+        entry = total[:, block * head_dim : (block + 1) * head_dim] * row_scale
+        if block < blocks * 3 // 4:
+            entry = entry * cosines + pltpu.roll(entry, head_dim // 2, 1) * sines
+        if block < blocks // 2:
+            entry = entry * scale
+        out[:, block * head_dim : (block + 1) * head_dim] = entry.astype(BF)
+
+
+def attend_kernel(
+    meta, lengths, owners, mine, other, ck, cv, uk, uv, keep, send, queries, numer, denom
+):
+    slot = pl.program_id(0)
+    count, heads, wide = queries.shape
+    head_dim = numer.shape[2]
+    half = count // 2
+    group = half // 2
+    half_heads = heads // 2
+    half_kv = half_heads // 2
+    first = meta[0] == 0
+    block_index = meta[1]
+
+    def piece(index, at):
+        a = mine[:, at * head_dim : (at + 1) * head_dim].astype(F32)
+        b = other[:, at * head_dim : (at + 1) * head_dim].astype(F32)
+        return jnp.where(first, a, b) if index == 0 else jnp.where(first, b, a)
+
+    @pl.when(slot == 0)
+    def _():
+        queries[...] = jnp.zeros_like(queries)
+        for head in range(heads):
+            kv = head // 2
+            queries[:, head, kv * head_dim : (kv + 1) * head_dim] = piece(
+                head // half_heads, head % half_heads
+            )
+
+    head_row = lax.broadcasted_iota(jnp.int32, (heads, head_dim), 0)
+    for kind, (key_ref, value_ref) in enumerate(((ck, cv), (uk, uv))):
+        block_len = key_ref.shape[1]
+        request = owners[kind, slot]
+        length = lengths[kind, request]
+        row = request // group * half + kind * group + request % group
+        query = queries[row].astype(BF)
+        scores = nt_dot(query, key_ref[0])
+        place = block_index * block_len + lax.broadcasted_iota(jnp.int32, scores.shape, 1)
+        probs = jnp.where(
+            place < length, jnp.exp(ATTN_CAP * jnp.tanh(scores / ATTN_CAP)), 0.0
+        )
+        sums = nn_dot(probs.astype(BF), value_ref[0])
+        folded = jnp.zeros((heads, head_dim), F32)
+        for kv in range(heads // 2):
+            folded = jnp.where(
+                head_row // 2 == kv, sums[:, kv * head_dim : (kv + 1) * head_dim], folded
+            )
+        numer[row] = folded
+        denom[row] = jnp.broadcast_to(
+            jnp.sum(probs, axis=-1, keepdims=True), (heads, head_dim)
+        )
+
+    @pl.when(slot == pl.num_programs(0) - 1)
+    def _():
+        owned = jnp.where(block_index == 0, 1.0, 0.0)
+        sums, totals = [], []
+        for head in range(heads):
+            side = head // half_heads
+            kv = head % half_heads // 2
+            query = piece(side, head % half_heads)
+            key = piece(side, half_heads + kv)
+            value = piece(side, half_heads + half_kv + kv)
+            score = jnp.sum(query * key, axis=-1, keepdims=True)
+            own = jnp.exp(ATTN_CAP * jnp.tanh(score / ATTN_CAP))
+            weight = own.astype(BF).astype(F32)
+            sums.append(numer[:, head, :] + owned * weight * value)
+            totals.append(denom[:, head, :1] + owned * own)
+        for at in range(half_heads):
+            low, high = sums[at], sums[half_heads + at]
+            keep[:, at * head_dim : (at + 1) * head_dim] = jnp.where(first, low, high)
+            send[:, at * head_dim : (at + 1) * head_dim] = jnp.where(first, high, low)
+        low = columns_tile(totals[:half_heads], count)
+        high = columns_tile(totals[half_heads:], count)
+        keep[:, half_heads * head_dim :] = jnp.where(first, low, high)
+        send[:, half_heads * head_dim :] = jnp.where(first, high, low)
+
+
+def attended_kernel(*refs):
+    parts, out = refs[:-1], refs[-1]
+    total = parts[0][...]
+    for part in parts[1:]:
+        total = total + part[...]
+    width = out.shape[1]
+    heads = width // HD
+    for head in range(heads):
+        at = slice(head * HD, (head + 1) * HD)
+        out[:, at] = (total[:, at] / total[:, width + head : width + head + 1]).astype(BF)
+
+
+def output_kernel(meta, mine, other, weight, out):
+    first = meta[0] == 0
+    a, b = mine[...].astype(F32), other[...].astype(F32)
+    low = jnp.where(first, a, b).astype(BF)
+    high = jnp.where(first, b, a).astype(BF)
+    width = mine.shape[1]
+    out[...] = nt_dot(low, weight[:, :width]) + nt_dot(high, weight[:, width:])
+
+
+def gate_up_kernel(pieces, meta, hidden, post_gain, pre_gain, *refs):
+    parts, (gate_weight, up_weight, keep, send, branch, inputs, tile) = refs[:-7], refs[-7:]
+    step = pl.program_id(0)
+    count = hidden.shape[0]
+    guide, place = meta[0], meta[2]
+
+    @pl.when(step == 0)
+    def _():
+        projected = parts[0][...]
+        for part in parts[1:]:
+            projected = projected + part[...]
+        streams = hidden[...].astype(F32)
+        gained = projected * post_gain[...]
+        branch[...] = gained
+        inputs[:count, :] = (streams * pre_gain[...]).astype(BF)
+        inputs[count:, :] = (gained * pre_gain[...]).astype(BF)
+        tile[...] = columns_tile(
+            [
+                jnp.sum(projected * projected, axis=-1, keepdims=True),
+                jnp.sum(streams * gained, axis=-1, keepdims=True),
+                jnp.sum(gained * gained, axis=-1, keepdims=True),
+            ],
+            count,
+        )
+
+    operand = inputs[...]
+    gate = nn_dot(operand, gate_weight[...])
+    up = nn_dot(operand, up_weight[...])
+    width = gate.shape[1]
+    slot = lax.bitwise_xor(lax.rem(step, pieces), place)
+    mine = lax.div(step, pieces) == guide
+
+    @pl.when(mine)
+    def _():
+        keep[slot, :, :width] = gate
+        keep[slot, :, width : 2 * width] = up
+        keep[slot, :count, 2 * width :] = tile[...]
+        keep[slot, count:, 2 * width :] = jnp.zeros((count, LANES), F32)
+
+    @pl.when(jnp.logical_not(mine))
+    def _():
+        send[slot, :, :width] = gate.astype(BF)
+        send[slot, :, width : 2 * width] = up.astype(BF)
+        coded = split_tile(tile[...])
+        send[slot, :count, 2 * width :] = coded
+        send[slot, count:, 2 * width :] = jnp.zeros_like(coded)
+
+
+def share_kernel(keep, got, own, *outs):
+    width = keep.shape[2] - LANES
+    count = keep.shape[1] // 2
+    tile = keep[0, :count, width:] + joined_tile(got[0, :count, width:])
+    own[:, :width] = keep[0, :, :width] + got[0, :, :width].astype(F32)
+    own[:count, width:] = tile
+    own[count:, width:] = jnp.zeros((count, LANES), F32)
+    coded = split_tile(tile)
+    for at, out in enumerate(outs):
+        out[:, :width] = (
+            keep[at + 1, :, :width] + got[at + 1, :, :width].astype(F32)
+        ).astype(BF)
+        out[:count, width:] = coded
+        out[count:, width:] = jnp.zeros_like(coded)
+
+
+def active_kernel(squares, own, *refs):
+    parts, (out, scales) = refs[:-2], refs[-2:]
+    count = squares.shape[0]
+    width = out.shape[1]
+    tile = own[:count, 2 * width :]
+    for part in parts:
+        tile = tile + joined_tile(part[:count, 2 * width :])
+    branch_scale = lax.rsqrt(tile[:, 0:1] / D + EPS)
+    middle_sq = squares[:, 0:1] + branch_scale * (
+        2.0 * tile[:, 1:2] + branch_scale * tile[:, 2:3]
+    )
+    scale = lax.rsqrt(jnp.maximum(middle_sq, 0.0) / D + EPS)
+    scales[...] = jnp.broadcast_to(branch_scale, (count, LANES))
+
+    def summed(rows, at):
+        total = own[rows, at]
+        for part in parts:
+            total = total + part[rows, at].astype(F32)
+        return total
+
+    low, high = slice(0, count), slice(count, 2 * count)
+    gate_at, up_at = slice(0, width), slice(width, 2 * width)
+    gate = (summed(low, gate_at) + branch_scale * summed(high, gate_at)) * scale
+    up = (summed(low, up_at) + branch_scale * summed(high, up_at)) * scale
+    out[...] = (jax.nn.gelu(gate, approximate=True) * up).astype(BF)
+
+
+def down_kernel(pieces, meta, *refs):
+    mine, other = refs[:pieces], refs[pieces : 2 * pieces]
+    weight, out = refs[2 * pieces :]
+    step = pl.program_id(0)
+
+    @pl.when(step == 0)
+    def _():
+        out[...] = jnp.zeros_like(out)
+
+    for at, part in enumerate(mine + other):
+
+        @pl.when(step == at)
+        def _(part=part):
+            out[...] += nt_dot(part[...], weight[...])
+
+
+def last_kernel(hidden, branch, scales, post_gain, final_gain, *refs):
+    parts, out = refs[:-1], refs[-1]
+    ffw = parts[0][...]
+    for part in parts[1:]:
+        ffw = ffw + part[...]
+    count = ffw.shape[0]
+    middle = hidden[...].astype(F32) + branch[...] * scales[:, 0:1]
+    gained = ffw * post_gain[...]
+    out[:count, :] = (middle * final_gain[...]).astype(BF)
+    out[count : 2 * count, :] = (gained * final_gain[...]).astype(BF)
+    tile = columns_tile(
+        [
+            jnp.sum(ffw * ffw, axis=-1, keepdims=True),
+            jnp.sum(middle * gained, axis=-1, keepdims=True),
+            jnp.sum(gained * gained, axis=-1, keepdims=True),
+            jnp.sum(middle * middle, axis=-1, keepdims=True),
+        ],
+        count,
+    )
+    out[2 * count :, :LANES] = split_tile(tile)
+    out[2 * count :, LANES:] = jnp.zeros((count, out.shape[1] - LANES), BF)
+
+
+def table_kernel(pieces, meta, *refs):
+    parts, (table, keep, send, rows) = refs[:pieces], refs[pieces:]
+    step = pl.program_id(0)
+    count = parts[0].shape[0] // 3
+    half = count // 2
+    width = parts[0].shape[1]
+    first = meta[0] == 0
+    place = meta[2]
+    step_rows = table.shape[0]
+    total_rows = keep.shape[1] - LANES
+
+    @pl.when(step == 0)
+    def _():
+        for target in range(pieces):
+            block = parts[0][: 2 * count, :].astype(F32)
+            for at in range(1, pieces):
+                block = jnp.where(
+                    lax.bitwise_xor(place, at) == target,
+                    parts[at][: 2 * count, :].astype(F32),
+                    block,
+                )
+            rows[:, target * width : (target + 1) * width] = block
+        tile = joined_tile(parts[0][2 * count :, :LANES])
+        for at in range(1, pieces):
+            tile = tile + joined_tile(parts[at][2 * count :, :LANES])
+        low, high = tile[:half], tile[half:]
+        keep[:half, total_rows:] = jnp.where(first, low, high)
+        send[:half, total_rows:] = jnp.where(first, high, low)
+        keep[half:, total_rows:] = jnp.zeros((half, LANES), F32)
+        send[half:, total_rows:] = jnp.zeros((half, LANES), F32)
+
+    product = nt_dot(rows[...].astype(BF), table[...])
+    at = pl.ds(pl.multiple_of(step * step_rows, step_rows), step_rows)
+    for base in (0, half):
+        low = product[2 * base : 2 * base + half]
+        high = product[2 * base + half : 2 * base + 2 * half]
+        keep[base : base + half, at] = jnp.where(first, low, high)
+        send[base : base + half, at] = jnp.where(first, high, low)
+
+
+def logits_kernel(places, weights, keep, got, out, mixed):
+    rows = keep.shape[0] // 2
+    group = rows // 2
+    total_rows = keep.shape[1] - LANES
+    tile = keep[:rows, total_rows:] + got[:rows, total_rows:]
+    branch_scale = lax.rsqrt(tile[:, 0:1] / D + EPS)
+    last_sq = tile[:, 3:4] + branch_scale * (
+        2.0 * tile[:, 1:2] + branch_scale * tile[:, 2:3]
+    )
+    scale = lax.rsqrt(jnp.maximum(last_sq, 0.0) / D + EPS)
+    sums = keep[:, :total_rows] + got[:, :total_rows]
+    logits = LOGIT_CAP * jnp.tanh(
+        (sums[:rows] + branch_scale * sums[rows:]) * scale / LOGIT_CAP
+    )
+    turned = pltpu.roll(logits, group, 0)
+    top = lax.broadcasted_iota(jnp.int32, logits.shape, 0) < group
+    uncond = jnp.where(top, turned, logits)
+    cond = jnp.where(top, logits, turned)
+    mixed[...] = uncond + weights[:, 0:1] * (cond - uncond)
+    half = places.shape[1]
+    for start in range(0, half, LANES):
+        at = slice(start, start + LANES)
+        wanted = places[:, at]
+        lane = lax.bitwise_and(wanted, LANES - 1)
+        chunk = lax.shift_right_logical(wanted, 7)
+        found = jnp.zeros((rows, LANES), F32)
+        for block in range(total_rows // LANES):
+            values = mixed[:, block * LANES : (block + 1) * LANES]
+            found = jnp.where(
+                chunk == block, jnp.take_along_axis(values, lane, axis=1), found
+            )
+        out[:, start : start + LANES] = found[:group]
+        out[:, half + start : half + start + LANES] = found[group:]
+
+
+def from_peers(value, axis, size):
+    values = value if isinstance(value, (list, tuple)) else [value] * (size - 1)
+    return [
+        lax.ppermute(values[k - 1], axis, [(i, i ^ k) for i in range(size)])
+        for k in range(1, size)
+    ]
+
+
+def fast_layer(
+    hidden,
+    lengths,
+    slot_owner,
+    allowed_ids,
+    guidance,
+    pre_attn_gain,
+    post_attn_gain,
+    pre_ffw_gain,
+    post_ffw_gain,
+    final_gain,
+    query_weight,
+    key_weight,
+    value_weight,
+    output_weight,
+    gate_weight,
+    up_weight,
+    down_weight,
+    embedding,
+    cond_keys,
+    cond_values,
+    uncond_keys,
+    uncond_values,
+):
+    kinds, requests, width = hidden.shape
+    count = kinds * requests
+    half = count // 2
+    group = half // 2
+    heads = query_weight.shape[1] // HD
+    kv_heads = key_weight.shape[1] // HD
+    seq_size = lax.axis_size("seq")
+    kv_size = lax.axis_size("kv")
+    guide_index = lax.axis_index("guide")
+    seq_index = lax.axis_index("seq")
+    kv_index = lax.axis_index("kv")
+    meta = jnp.stack([guide_index, guide_index * seq_size + seq_index, seq_index]).astype(jnp.int32)
+    shape = jax.ShapeDtypeStruct
+    row = lambda gain: gain.reshape(1, -1)
+
+    position = (
+        lengths.astype(F32).reshape(kinds, 2, group).transpose(1, 0, 2).reshape(count)
+    )
+    half_dim = HD // 2
+    frequency = THETA ** (-2.0 * jnp.arange(half_dim, dtype=F32) / HD)
+    angles = position[:, None] * frequency
+    cosine = jnp.cos(angles)
+    sine = jnp.sin(angles)
+    cosine = jnp.concatenate([cosine, cosine], axis=-1)
+    sine = jnp.concatenate([-sine, sine], axis=-1)
+
+    with jax.named_scope("project"):
+        joint = (heads + 2 * kv_heads) * HD // 2 + LANES
+        rows, keep, send = pl.pallas_call(
+            project_kernel,
+            out_shape=(
+                shape((count, width), BF),
+                shape((count, joint), F32),
+                shape((count, joint), F32),
+            ),
+            in_specs=[SMEM] + [VMEM] * 5,
+            out_specs=(VMEM,) * 3,
+            compiler_params=limit(16),
+        )(meta, hidden.reshape(count, width), row(pre_attn_gain), query_weight, key_weight, value_weight)
+        total = keep + from_peers(send, "guide", 2)[0]
+        parts = [total] + from_peers(total, "seq", seq_size)
+        mine, squares = pl.pallas_call(
+            lambda *refs: rope_kernel(HD, (D // H) ** (-0.5), *refs),
+            out_shape=(shape((count, joint - LANES), BF), shape((count, LANES), F32)),
+            in_specs=[VMEM] * (2 + seq_size),
+            out_specs=(VMEM,) * 2,
+            compiler_params=limit(16),
+        )(cosine, sine, *parts)
+        other = from_peers(mine, "guide", 2)[0]
+
+    with jax.named_scope("attend"):
+        cond_len, uncond_len = cond_keys.shape[1], uncond_keys.shape[1]
+        kv_width = kv_heads * HD
+        block = lambda size: pl.BlockSpec((1, size, kv_width), lambda i, *_: (i, 0, 0))
+        whole = pl.BlockSpec((count, joint - LANES), lambda i, *_: (0, 0))
+        attend_width = heads // 2 * HD + LANES
+        out_block = pl.BlockSpec((count, attend_width), lambda i, *_: (0, 0))
+        keep, send = pl.pallas_call(
+            attend_kernel,
+            out_shape=(shape((count, attend_width), F32),) * 2,
+            grid_spec=pltpu.PrefetchScalarGridSpec(
+                num_scalar_prefetch=3,
+                grid=(requests,),
+                in_specs=[whole, whole] + [block(cond_len)] * 2 + [block(uncond_len)] * 2,
+                out_specs=(out_block,) * 2,
+                scratch_shapes=[
+                    pltpu.VMEM((count, heads, kv_width), F32),
+                    pltpu.VMEM((count, heads, HD), F32),
+                    pltpu.VMEM((count, heads, HD), F32),
+                ],
+            ),
+            compiler_params=limit(24),
+        )(meta, lengths, slot_owner, mine, other, cond_keys, cond_values, uncond_keys, uncond_values)
+        total = keep + from_peers(send, "guide", 2)[0]
+        parts = [total] + from_peers(total, "seq", seq_size)
+        mine = pl.pallas_call(
+            attended_kernel,
+            out_shape=shape((count, heads // 2 * HD), BF),
+            in_specs=[VMEM] * seq_size,
+            out_specs=VMEM,
+            compiler_params=limit(16),
+        )(*parts)
+        other = from_peers(mine, "guide", 2)[0]
+        part = pl.pallas_call(
+            output_kernel,
+            out_shape=shape((count, width), F32),
+            in_specs=[SMEM] + [VMEM] * 3,
+            out_specs=VMEM,
+            compiler_params=limit(16),
+        )(meta, mine, other, output_weight.T)
+        parts = [part] + from_peers(part, "kv", kv_size)
+
+    with jax.named_scope("gate_up"):
+        hidden_units = gate_weight.shape[1]
+        unit_block = hidden_units // (2 * seq_size)
+        share_width = 2 * unit_block + LANES
+        const2 = lambda i, *_: (0, 0)
+        small = pl.BlockSpec((count, width), const2)
+        gain_block = pl.BlockSpec((1, width), const2)
+        weight_block = pl.BlockSpec((width, unit_block), lambda i, *_: (0, i))
+        share_block = pl.BlockSpec((seq_size, 2 * count, share_width), lambda i, *_: (0, 0, 0))
+        keep, send, branch = pl.pallas_call(
+            lambda *refs: gate_up_kernel(seq_size, *refs),
+            out_shape=(
+                shape((seq_size, 2 * count, share_width), F32),
+                shape((seq_size, 2 * count, share_width), BF),
+                shape((count, width), F32),
+            ),
+            grid_spec=pltpu.PrefetchScalarGridSpec(
+                num_scalar_prefetch=1,
+                grid=(2 * seq_size,),
+                in_specs=[small, gain_block, gain_block] + [small] * kv_size + [weight_block] * 2,
+                out_specs=(share_block, share_block, small),
+                scratch_shapes=[
+                    pltpu.VMEM((2 * count, width), BF),
+                    pltpu.VMEM((count, LANES), F32),
+                ],
+            ),
+            compiler_params=limit(24),
+        )(meta, rows, row(post_attn_gain), row(pre_ffw_gain), *parts, gate_weight, up_weight)
+        got = from_peers(send, "guide", 2)[0]
+        own, *shares = pl.pallas_call(
+            share_kernel,
+            out_shape=(shape((2 * count, share_width), F32),)
+            + (shape((2 * count, share_width), BF),) * (seq_size - 1),
+            in_specs=[VMEM] * 2,
+            out_specs=(VMEM,) * seq_size,
+            compiler_params=limit(16),
+        )(keep, got)
+        parts = from_peers(shares, "seq", seq_size)
+        active, scales = pl.pallas_call(
+            active_kernel,
+            out_shape=(shape((count, unit_block), BF), shape((count, LANES), F32)),
+            in_specs=[VMEM] * (1 + seq_size),
+            out_specs=(VMEM,) * 2,
+            compiler_params=limit(16),
+        )(squares, own, *parts)
+
+    with jax.named_scope("down"):
+        mine = [active] + from_peers(active, "seq", seq_size)
+        other = [from_peers(value, "guide", 2)[0] for value in mine]
+
+        def weight_place(i, meta_ref):
+            side = jnp.where(i < seq_size, meta_ref[0], 1 - meta_ref[0])
+            return (0, side * seq_size + lax.bitwise_xor(lax.rem(i, seq_size), meta_ref[2]))
+
+        part = pl.pallas_call(
+            lambda *refs: down_kernel(seq_size, *refs),
+            out_shape=shape((count, width), F32),
+            grid_spec=pltpu.PrefetchScalarGridSpec(
+                num_scalar_prefetch=1,
+                grid=(2 * seq_size,),
+                in_specs=[pl.BlockSpec((count, unit_block), const2)] * (2 * seq_size)
+                + [pl.BlockSpec((width, unit_block), weight_place)],
+                out_specs=small,
+            ),
+            compiler_params=limit(16),
+        )(meta, *mine, *other, down_weight.T)
+        parts = [part] + from_peers(part, "kv", kv_size)
+
+    with jax.named_scope("head"):
+        mine = pl.pallas_call(
+            last_kernel,
+            out_shape=shape((3 * count, width), BF),
+            in_specs=[VMEM] * (5 + kv_size),
+            out_specs=VMEM,
+            compiler_params=limit(16),
+        )(rows, branch, scales, row(post_ffw_gain), row(final_gain), *parts)
+        parts = [mine] + from_peers(mine, "seq", seq_size)
+        table_rows, table_width = embedding.shape
+        step_rows = min(512, table_rows)
+        piece_block = pl.BlockSpec((3 * count, width), const2)
+        logit_block = pl.BlockSpec((count, table_rows + LANES), const2)
+        keep, send = pl.pallas_call(
+            lambda *refs: table_kernel(seq_size, *refs),
+            out_shape=(shape((count, table_rows + LANES), F32),) * 2,
+            grid_spec=pltpu.PrefetchScalarGridSpec(
+                num_scalar_prefetch=1,
+                grid=(table_rows // step_rows,),
+                in_specs=[piece_block] * seq_size
+                + [pl.BlockSpec((step_rows, table_width), lambda i, *_: (i, 0))],
+                out_specs=(logit_block,) * 2,
+                scratch_shapes=[pltpu.VMEM((2 * count, table_width), F32)],
+            ),
+            compiler_params=limit(24),
+        )(meta, *parts, embedding)
+        got = from_peers(send, "guide", 2)[0]
+        allowed = allowed_ids.shape[0]
+        places = allowed_ids - (kv_index * seq_size + seq_index) * table_rows
+        places = jnp.repeat(places.reshape(2, allowed // 2), group, axis=0)
+        weights = lax.dynamic_slice_in_dim(guidance, guide_index * group, group, 0)
+        weights = jnp.broadcast_to(jnp.concatenate([weights, weights])[:, None], (half, LANES))
+        return pl.pallas_call(
+            logits_kernel,
+            out_shape=shape((group, allowed), F32),
+            in_specs=[VMEM] * 4,
+            out_specs=VMEM,
+            scratch_shapes=[pltpu.VMEM((half, table_rows), F32)],
+            compiler_params=limit(24),
+        )(places, weights, keep, got)
+
+
+def on_device(*arrays):
+    units = arrays[14].shape[1] // (2 * lax.axis_size("seq"))
+    requests = arrays[0].shape[1]
+    if units % LANES or requests != 8 or lax.axis_size("guide") != 2:
+        return plain_layer(*arrays)
+    return fast_layer(*arrays)
+
+
 def solution(mesh):
     return jax.shard_map(
         on_device,

time: 490 us -> 152 us (0.31)
  blocking collectives: 132 us -> 0 us
  local copies, waits for them, and re-layouts: 140 us -> 25.4 us
  waiting for transfers between devices: 136 us -> 43.7 us
  matrix products: 52.8 us -> 0 us
  Pallas kernels: 0 us -> 47.9 us
  starting transfers between devices: 0.17 us -> 32.7 us
  between operations: 15.3 us -> 0.3 us
  other arithmetic: 11.2 us -> 1.07 us
    psum x4 -> x0, waiting for transfers between devices: 133 us -> none  [the longest x2 103 us: on_device(): numer_sum, denom_sum = lax.psum((numer_part, denom_part), ('guide', 'seq'))]
    psum x7 -> x0, blocking collectives: 108 us -> none  [the longest x1 18.5 us: on_device(): lax.psum((square_part, query_part, key_part, value_part), ('guide', 'seq'))]
    gather x1 -> x0, local copies, waits for them, and re-layouts: 101 us -> none  [on_device(): picked = jnp.take(embedding, allowed_ids - block_first, axis=0)]
    dot_general x23 -> x0, matrix products: 52.8 us -> none  [the longest x1 10.8 us: on_device(): jnp.einsum('sd,ad->sa', half_rows.reshape(stream_count, half_rows.shape[2...]
    pallas_call x0 -> x12, Pallas kernels: none -> 47.9 us  [the longest x1 22.1 us: fast_layer(): pl.pallas_call(lambda *refs: table_kernel(seq_size, *refs), out_shape=(sh...]
    ppermute x0 -> x31, waiting for transfers between devices: none -> 43.7 us  [from_peers(): lax.ppermute(values[k - 1], axis, [(i, i ^ k) for i in range(size)])]
    dynamic_slice x13 -> x1, local copies, waits for them, and re-layouts: 37.1 us -> 0.08 us  [fast_layer(): weights = lax.dynamic_slice_in_dim(guidance, guide_index * group, group, 0)]
    ppermute x0 -> x31, starting transfers between devices: none -> 32.7 us  [from_peers(): lax.ppermute(values[k - 1], axis, [(i, i ^ k) for i in range(size)])]
  transfers between devices with their start and end apart: 5 -> 31, of which waited for: 4 -> 21; matrix products, arithmetic and copies ran while one was open for 23% -> 1% of each run, Pallas kernels for 0% -> 0%
where the time goes in v1:
time: 152 us; the launch traced here: 151 us
  Pallas kernels  47.9 us (32%)
  waiting for transfers between devices  43.7 us (29%)
  starting transfers between devices  32.7 us (22%)
  local copies, waits for them, and re-layouts  25.4 us (17%)
    ppermute x31, waiting for transfers between devices, from_peers(): lax.ppermute(values[k - 1], axis, [(i, i ^ k) for i in range(size)])  43.7 us
    ppermute x31, starting transfers between devices, from_peers(): lax.ppermute(values[k - 1], axis, [(i, i ^ k) for i in range(size)])  32.7 us
    unnamed x44, local copies, waits for them, and re-layouts  24.3 us
    pallas_call x1, Pallas kernels, fast_layer(): pl.pallas_call(lambda *refs: table_kernel(seq_size, *refs), out_shape=(sh...  22.1 us
    pallas_call x1, Pallas kernels, fast_layer(): pl.pallas_call(attend_kernel, out_shape=(shape((count, attend_width), F32...  7.73 us
    pallas_call x1, Pallas kernels, fast_layer(): pl.pallas_call(lambda *refs: gate_up_kernel(seq_size, *refs), out_shape=(...  7.28 us
    pallas_call x1, Pallas kernels, fast_layer(): pl.pallas_call(lambda *refs: down_kernel(seq_size, *refs), out_shape=shap...  5.43 us
  transfers between devices with their start and end apart: 31, of which 21 were waited for; matrix products, arithmetic and copies ran while one was open for 1% of the time, Pallas kernels for 0%

profile of v1, /device:TPU:0, one launch (start us, length us, event | category | flops | bytes accessed | tf_op | source)
XLA Modules:
  0.0 151.0 jit_solution(14328183641897396772)
XLA Ops:
  0.8 1.3 copy-done.6
  2.0 1.1 copy-done.8
  3.1 1.1 copy-done.9
  4.9 1.1 project.2
  7.5 2.9 %collective-permute-start.1 = (f32[16,1152]{1,0:T(8,128)S(1)}, f32[16,1152]{1,0:T(8,128)S(1)}, u32[]{:S(2)}, u32[]{:S(2)}) collective-permute-start(f32[16,1152]{1,0:T(8,128)S(1)} %add.18.refs_2_), channel_id=1, source_target_pairs={{0,1},{1,0},{2,3},{3,2},{4,5},{5,4},{6,7},{7,6},{8,9},{9,8},{10,11... | collective-permute-start | bytes 221192 | tf_op jit(solution)/shard_map/project/ppermute | solution.py:612
  10.3 2.6 %collective-permute-start.2 = (f32[16,1152]{1,0:T(8,128)S(1)}, f32[16,1152]{1,0:T(8,128)S(1)}, u32[]{:S(2)}, u32[]{:S(2)}) collective-permute-start(f32[16,1152]{1,0:T(8,128)S(1)} %add.18.refs_2_), channel_id=1, source_target_pairs={{0,2},{1,3},{2,0},{3,1},{4,6},{5,7},{6,4},{7,5},{8,10},{9,11},{10,... | collective-permute-start | bytes 221192 | tf_op jit(solution)/shard_map/project/ppermute | solution.py:612
  13.0 6.2 %collective-permute-done.2.refs_4_ = f32[16,1152]{1,0:T(8,128)S(1)} collective-permute-done((f32[16,1152]{1,0:T(8,128)S(1)}, f32[16,1152]{1,0:T(8,128)S(1)}, u32[]{:S(2)}, u32[]{:S(2)}) %collective-permute-start.2) | collective-permute-done | bytes 73760 | tf_op jit(solution)/shard_map/project/ppermute | solution.py:612
  19.6 1.2 collective-permute-done.4.other
  20.8 4.0 %copy-done.2 = bf16[8,1024,512]{2,1,0:T(8,128)(2,1)S(1)} copy-done((bf16[8,1024,512]{2,1,0:T(8,128)(2,1)S(1)}, bf16[8,1024,512]{2,1,0:T(8,128)(2,1)}, u32[]{:S(2)}) %copy-start.2) | copy-done | bytes 8388632
  24.7 3.6 %copy-done.3 = bf16[8,1024,512]{2,1,0:T(8,128)(2,1)S(1)} copy-done((bf16[8,1024,512]{2,1,0:T(8,128)(2,1)S(1)}, bf16[8,1024,512]{2,1,0:T(8,128)(2,1)}, u32[]{:S(2)}) %copy-start.3) | copy-done | bytes 8388632
  28.3 1.6 %copy-done.4 = bf16[8,256,512]{2,1,0:T(8,128)(2,1)S(1)} copy-done((bf16[8,256,512]{2,1,0:T(8,128)(2,1)S(1)}, bf16[8,256,512]{2,1,0:T(8,128)(2,1)}, u32[]{:S(2)}) %copy-start.4) | copy-done | bytes 2097176
  29.9 1.6 %copy-done.5 = bf16[8,256,512]{2,1,0:T(8,128)(2,1)S(1)} copy-done((bf16[8,256,512]{2,1,0:T(8,128)(2,1)S(1)}, bf16[8,256,512]{2,1,0:T(8,128)(2,1)}, u32[]{:S(2)}) %copy-start.5) | copy-done | bytes 2097176
  32.9 7.7 %attend.3 = (f32[16,640]{1,0:T(8,128)S(1)}, f32[16,640]{1,0:T(8,128)S(1)}) custom-call(s32[3]{0:T(128)S(1)} %pad_add_fusion.meta.refs_0_, s32[2,8]{1,0:T(2,128)S(1)} %copy-done.11, s32[2,8]{1,0:T(2,128)S(1)} %copy-done.12, bf16[16,1024]{1,0:T(8,128)(2,1)S(1)} %get-tuple-element.26.mine, bf16[16,1024]{1,0:T(8,128)(2,1)S(1)} %collective-permute-done.4.other, ...), custom_call_target="tpu_custom_call" | custom-call | tf_op jit(solution)/shard_map/attend/pallas_call | solution.py:698
  40.7 1.2 collective-permute-done.5
  41.9 1.5 collective-permute-start.6
  43.4 1.6 %collective-permute-start.7 = (f32[16,640]{1,0:T(8,128)S(1)}, f32[16,640]{1,0:T(8,128)S(1)}, u32[]{:S(2)}, u32[]{:S(2)}) collective-permute-start(f32[16,640]{1,0:T(8,128)S(1)} %add.19.refs_0_), channel_id=1, source_target_pairs={{0,2},{1,3},{2,0},{3,1},{4,6},{5,7},{6,4},{7,5},{8,10},{9,11},{10,... | collective-permute-start | bytes 122888 | tf_op jit(solution)/shard_map/attend/ppermute | solution.py:612
  45.0 1.3 collective-permute-start.8
  46.3 3.3 %collective-permute-done.7.refs_2_ = f32[16,640]{1,0:T(8,128)S(1)} collective-permute-done((f32[16,640]{1,0:T(8,128)S(1)}, f32[16,640]{1,0:T(8,128)S(1)}, u32[]{:S(2)}, u32[]{:S(2)}) %collective-permute-start.7) | collective-permute-done | bytes 40992 | tf_op jit(solution)/shard_map/attend/ppermute | solution.py:612
  49.6 1.2 collective-permute-done.8.refs_3_
  51.0 1.2 collective-permute-done.9.other
  53.1 1.5 collective-permute-start.10
  54.6 1.5 %collective-permute-start.11 = (f32[16,576]{1,0:T(8,128)S(1)}, f32[16,576]{1,0:T(8,128)S(1)}, u32[]{:S(2)}, u32[]{:S(2)}) collective-permute-start(f32[16,576]{1,0:T(8,128)S(1)} %attend.5.refs_4_), channel_id=1, source_target_pairs={{0,8},{4,12},{8,0},{12,4},{1,9},{5,13},{9,1},{13,5},{2,10},{6,14},... | collective-permute-start | bytes 110600 | tf_op jit(solution)/shard_map/attend/ppermute | solution.py:612
  57.1 1.5 collective-permute-done.11.refs_6_
  58.6 2.4 %collective-permute-done.12.refs_7_ = f32[16,576]{1,0:T(8,128)S(1)} collective-permute-done((f32[16,576]{1,0:T(8,128)S(1)}, f32[16,576]{1,0:T(8,128)S(1)}, u32[]{:S(2)}, u32[]{:S(2)}) %collective-permute-start.12) | collective-permute-done | bytes 36896 | tf_op jit(solution)/shard_map/attend/ppermute | solution.py:612
  61.0 4.0 %copy-done = bf16[576,9216]{1,0:T(8,128)(2,1)S(1)} copy-done((bf16[576,9216]{1,0:T(8,128)(2,1)S(1)}, bf16[576,9216]{1,0:T(8,128)(2,1)}, u32[]{:S(2)}) %copy-start) | copy-done | bytes 10616856
  65.1 7.3 %gate_up.3 = (f32[4,32,2432]{2,1,0:T(8,128)S(1)}, bf16[4,32,2432]{2,1,0:T(8,128)(2,1)S(1)}, f32[16,576]{1,0:T(8,128)S(1)}) custom-call(s32[3]{0:T(128)S(1)} %pad_add_fusion.meta.refs_0_, bf16[16,576]{1,0:T(8,128)(2,1)S(1)} %get-tuple-element.23.refs_1_.hidden, f32[1,576]{1,0:T(1,128)S(1)} %reshape.38.refs_2_, f32[1,576]{1,0:T(1,128)S(1)} %reshape.39.refs_3_, ...), custom_call_target="tpu_custom_call" | custom-call | tf_op jit(solution)/shard_map/gate_up/pallas_call | solution.py:742
  72.4 2.0 %collective-permute-done.13.got = bf16[4,32,2432]{2,1,0:T(8,128)(2,1)S(1)} collective-permute-done((bf16[4,32,2432]{2,1,0:T(8,128)(2,1)S(1)}, bf16[4,32,2432]{2,1,0:T(8,128)(2,1)S(1)}, u32[]{:S(2)}, u32[]{:S(2)}) %collective-permute-start.13) | collective-permute-done | bytes 622624 | tf_op jit(solution)/shard_map/gate_up/ppermute | solution.py:612
  74.7 2.0 %collective-permute-start.15 = (bf16[32,2432]{1,0:T(8,128)(2,1)S(1)}, bf16[32,2432]{1,0:T(8,128)(2,1)S(1)}, u32[]{:S(2)}, u32[]{:S(2)}) collective-permute-start(bf16[32,2432]{1,0:T(8,128)(2,1)S(1)} %get-tuple-element.35), channel_id=1, source_target_pairs={{0,2},{1,3},{2,0},{3,1},{4,6},{5,7},{6,4},{7,5},{8,10},{9,11},{10,... | collective-permute-start | bytes 466952 | tf_op jit(solution)/shard_map/gate_up/ppermute | solution.py:612
  76.7 2.4 %collective-permute-start.16 = (bf16[32,2432]{1,0:T(8,128)(2,1)S(1)}, bf16[32,2432]{1,0:T(8,128)(2,1)S(1)}, u32[]{:S(2)}, u32[]{:S(2)}) collective-permute-start(bf16[32,2432]{1,0:T(8,128)(2,1)S(1)} %get-tuple-element.36), channel_id=1, source_target_pairs={{0,3},{1,2},{2,1},{3,0},{4,7},{5,6},{6,5},{7,4},{8,11},{9,10},{10,... | collective-permute-start | bytes 466952 | tf_op jit(solution)/shard_map/gate_up/ppermute | solution.py:612
  79.1 4.4 %collective-permute-done.14.refs_0_ = bf16[32,2432]{1,0:T(8,128)(2,1)S(1)} collective-permute-done((bf16[32,2432]{1,0:T(8,128)(2,1)S(1)}, bf16[32,2432]{1,0:T(8,128)(2,1)S(1)}, u32[]{:S(2)}, u32[]{:S(2)}) %collective-permute-start.14) | collective-permute-done | bytes 155680 | tf_op jit(solution)/shard_map/gate_up/ppermute | solution.py:612
  83.5 5.8 %collective-permute-done.15.refs_1_ = bf16[32,2432]{1,0:T(8,128)(2,1)S(1)} collective-permute-done((bf16[32,2432]{1,0:T(8,128)(2,1)S(1)}, bf16[32,2432]{1,0:T(8,128)(2,1)S(1)}, u32[]{:S(2)}, u32[]{:S(2)}) %collective-permute-start.15) | collective-permute-done | bytes 155680 | tf_op jit(solution)/shard_map/gate_up/ppermute | solution.py:612
  89.7 3.2 %collective-permute-start.17 = (bf16[16,1152]{1,0:T(8,128)(2,1)S(1)}, bf16[16,1152]{1,0:T(8,128)(2,1)S(1)}, u32[]{:S(2)}, u32[]{:S(2)}) collective-permute-start(bf16[16,1152]{1,0:T(8,128)(2,1)S(1)} %get-tuple-element.38.refs_1_), channel_id=1, source_target_pairs={{0,1},{1,0},{2,3},{3,2},{4,5},{5,4},{6,7},{7,6},{8,9},{9,8},{10,11... | collective-permute-start | bytes 110600 | tf_op jit(solution)/shard_map/down/ppermute | solution.py:612
  93.6 1.7 %collective-permute-start.19 = (bf16[16,1152]{1,0:T(8,128)(2,1)S(1)}, bf16[16,1152]{1,0:T(8,128)(2,1)S(1)}, u32[]{:S(2)}, u32[]{:S(2)}) collective-permute-start(bf16[16,1152]{1,0:T(8,128)(2,1)S(1)} %get-tuple-element.38.refs_1_), channel_id=1, source_target_pairs={{0,3},{1,2},{2,1},{3,0},{4,7},{5,6},{6,5},{7,4},{8,11},{9,10},{10,... | collective-permute-start | bytes 110600 | tf_op jit(solution)/shard_map/down/ppermute | solution.py:612
  95.8 2.2 %collective-permute-done.18.refs_3_ = bf16[16,1152]{1,0:T(8,128)(2,1)S(1)} collective-permute-done((bf16[16,1152]{1,0:T(8,128)(2,1)S(1)}, bf16[16,1152]{1,0:T(8,128)(2,1)S(1)}, u32[]{:S(2)}, u32[]{:S(2)}) %collective-permute-start.18) | collective-permute-done | bytes 36896 | tf_op jit(solution)/shard_map/down/ppermute | solution.py:612
  98.1 1.3 collective-permute-done.19.refs_4_
  99.3 1.2 collective-permute-done.23.refs_8_
  100.5 4.0 %copy-done.1 = bf16[9216,576]{0,1:T(8,128)(2,1)S(1)} copy-done((bf16[9216,576]{0,1:T(8,128)(2,1)S(1)}, bf16[9216,576]{0,1:T(8,128)(2,1)}, u32[]{:S(2)}) %copy-start.1) | copy-done | bytes 10616856
  104.5 5.4 %down.1.refs_0_ = f32[16,576]{1,0:T(8,128)S(1)} custom-call(s32[3]{0:T(128)S(1)} %pad_add_fusion.meta.refs_0_, bf16[16,1152]{1,0:T(8,128)(2,1)S(1)} %get-tuple-element.38.refs_1_, bf16[16,1152]{1,0:T(8,128)(2,1)S(1)} %collective-permute-done.17.refs_2_, bf16[16,1152]{1,0:T(8,128)(2,1)S(1)} %collective-permute-done.18.refs_3_, ...), custom_call_target="tpu_custom_call" | custom-call | tf_op jit(solution)/shard_map/down/pallas_call | solution.py:787
  111.1 2.4 %collective-permute-start.26 = (f32[16,576]{1,0:T(8,128)S(1)}, f32[16,576]{1,0:T(8,128)S(1)}, u32[]{:S(2)}, u32[]{:S(2)}) collective-permute-start(f32[16,576]{1,0:T(8,128)S(1)} %down.1.refs_0_), channel_id=1, source_target_pairs={{0,12},{4,8},{8,4},{12,0},{1,13},{5,9},{9,5},{13,1},{2,14},{6,10},... | collective-permute-start | bytes 110600 | tf_op jit(solution)/shard_map/down/ppermute | solution.py:612
  114.0 1.0 collective-permute-done.25.refs_2_
  115.0 1.0 collective-permute-done.26.refs_3_
  116.4 2.2 %collective-permute-start.28 = (bf16[48,576]{1,0:T(8,128)(2,1)S(1)}, bf16[48,576]{1,0:T(8,128)(2,1)S(1)}, u32[]{:S(2)}, u32[]{:S(2)}) collective-permute-start(bf16[48,576]{1,0:T(8,128)(2,1)S(1)} %head.3.refs_1_), channel_id=1, source_target_pairs={{0,2},{1,3},{2,0},{3,1},{4,6},{5,7},{6,4},{7,5},{8,10},{9,11},{10,... | collective-permute-start | bytes 165896 | tf_op jit(solution)/shard_map/head/ppermute | solution.py:612
  118.6 2.1 %collective-permute-start.29 = (bf16[48,576]{1,0:T(8,128)(2,1)S(1)}, bf16[48,576]{1,0:T(8,128)(2,1)S(1)}, u32[]{:S(2)}, u32[]{:S(2)}) collective-permute-start(bf16[48,576]{1,0:T(8,128)(2,1)S(1)} %head.3.refs_1_), channel_id=1, source_target_pairs={{0,3},{1,2},{2,1},{3,0},{4,7},{5,6},{6,5},{7,4},{8,11},{9,10},{10,... | collective-permute-start | bytes 165896 | tf_op jit(solution)/shard_map/head/ppermute | solution.py:612
  120.6 1.5 %collective-permute-done.28.refs_3_ = bf16[48,576]{1,0:T(8,128)(2,1)S(1)} collective-permute-done((bf16[48,576]{1,0:T(8,128)(2,1)S(1)}, bf16[48,576]{1,0:T(8,128)(2,1)S(1)}, u32[]{:S(2)}, u32[]{:S(2)}) %collective-permute-start.28) | collective-permute-done | bytes 55328 | tf_op jit(solution)/shard_map/head/ppermute | solution.py:612
  122.2 2.4 %collective-permute-done.29.refs_4_ = bf16[48,576]{1,0:T(8,128)(2,1)S(1)} collective-permute-done((bf16[48,576]{1,0:T(8,128)(2,1)S(1)}, bf16[48,576]{1,0:T(8,128)(2,1)S(1)}, u32[]{:S(2)}, u32[]{:S(2)}) %collective-permute-start.29) | collective-permute-done | bytes 55328 | tf_op jit(solution)/shard_map/head/ppermute | solution.py:612
  124.6 22.1 %head.4 = (f32[16,8320]{1,0:T(8,128)S(1)}, f32[16,8320]{1,0:T(8,128)S(1)}) custom-call(s32[3]{0:T(128)S(1)} %pad_add_fusion.meta.refs_0_, bf16[48,576]{1,0:T(8,128)(2,1)S(1)} %head.3.refs_1_, bf16[48,576]{1,0:T(8,128)(2,1)S(1)} %collective-permute-done.27.refs_2_, bf16[48,576]{1,0:T(8,128)(2,1)S(1)} %collective-permute-done.28.refs_3_, ...), custom_call_target="tpu_custom_call" | custom-call | tf_op jit(solution)/shard_map/head/pallas_call | solution.py:814
  147.1 1.6 %collective-permute-done.30.got = f32[16,8320]{1,0:T(8,128)S(1)} collective-permute-done((f32[16,8320]{1,0:T(8,128)S(1)}, f32[16,8320]{1,0:T(8,128)S(1)}, u32[]{:S(2)}, u32[]{:S(2)}) %collective-permute-start.30) | collective-permute-done | bytes 532512 | tf_op jit(solution)/shard_map/head/ppermute | solution.py:612
  148.8 2.2 %head.5 = f32[4,4096]{1,0:T(4,128)} custom-call(s32[8,2048]{1,0:T(8,128)S(1)} %reshape.35.places, f32[8,128]{1,0:T(8,128)S(1)} %broadcast_in_dim.5.weights, f32[16,8320]{1,0:T(8,128)S(1)} %get-tuple-element.39.keep, f32[16,8320]{1,0:T(8,128)S(1)} %collective-permute-done.30.got), custom_call_target="tpu_custom_call" | custom-call | tf_op jit(solution)/shard_map/head/pallas_call | solution.py:833
  (93 shorter events, 11.2 us)
Async XLA Ops:
  0.8 1.3 copy-start.6
  6.0 1.5 collective-permute-start
  7.5 5.6 %collective-permute-start.1 = (f32[16,1152]{1,0:T(8,128)S(1)}, f32[16,1152]{1,0:T(8,128)S(1)}, u32[]{:S(2)}, u32[]{:S(2)}) collective-permute-start(f32[16,1152]{1,0:T(8,128)S(1)} %add.18.refs_2_), channel_id=1, source_target_pairs={{0,1},{1,0},{2,3},{3,2},{4,5},{5,4},{6,7},{7,6},{8,9},{9,8},{10,11... | collective-permute-start | bytes 221192 | tf_op jit(solution)/shard_map/project/ppermute | solution.py:612
  10.3 8.9 %collective-permute-start.2 = (f32[16,1152]{1,0:T(8,128)S(1)}, f32[16,1152]{1,0:T(8,128)S(1)}, u32[]{:S(2)}, u32[]{:S(2)}) collective-permute-start(f32[16,1152]{1,0:T(8,128)S(1)} %add.18.refs_2_), channel_id=1, source_target_pairs={{0,2},{1,3},{2,0},{3,1},{4,6},{5,7},{6,4},{7,5},{8,10},{9,11},{10,... | collective-permute-start | bytes 221192 | tf_op jit(solution)/shard_map/project/ppermute | solution.py:612
  12.9 6.3 %collective-permute-start.3 = (f32[16,1152]{1,0:T(8,128)S(1)}, f32[16,1152]{1,0:T(8,128)S(1)}, u32[]{:S(2)}, u32[]{:S(2)}) collective-permute-start(f32[16,1152]{1,0:T(8,128)S(1)} %add.18.refs_2_), channel_id=1, source_target_pairs={{0,3},{1,2},{2,1},{3,0},{4,7},{5,6},{6,5},{7,4},{8,11},{9,10},{10,... | collective-permute-start | bytes 221192 | tf_op jit(solution)/shard_map/project/ppermute | solution.py:612
  19.4 41.6 %slice-start = ((s8[10616832]{0:T(1024)(128)(4,1)}), s8[4194304]{0:T(1024)(128)(4,1)S(1)}, s32[]{:S(2)}) async-start(s8[10616832]{0:T(1024)(128)(4,1)} %bitcast.7), calls=%async_computation | async-start | bytes 8388608
  19.5 41.6 %slice-start.1 = ((s8[10616832]{0:T(1024)(128)(4,1)}), s8[4194304]{0:T(1024)(128)(4,1)S(1)}, s32[]{:S(2)}) async-start(s8[10616832]{0:T(1024)(128)(4,1)} %bitcast.7), calls=%async_computation.1 | async-start | bytes 8388608
  19.5 41.6 %slice-start.2 = ((s8[10616832]{0:T(1024)(128)(4,1)}), s8[2228224]{0:T(1024)(128)(4,1)S(1)}, s32[]{:S(2)}) async-start(s8[10616832]{0:T(1024)(128)(4,1)} %bitcast.7), calls=%async_computation.2 | async-start | bytes 4456448
  19.5 1.3 collective-permute-start.4
  20.8 4.0 %copy-start.2 = (bf16[8,1024,512]{2,1,0:T(8,128)(2,1)S(1)}, bf16[8,1024,512]{2,1,0:T(8,128)(2,1)}, u32[]{:S(2)}) copy-start(bf16[8,1024,512]{2,1,0:T(8,128)(2,1)} %ck.1) | copy-start | bytes 25165828
  24.7 3.6 %copy-start.3 = (bf16[8,1024,512]{2,1,0:T(8,128)(2,1)S(1)}, bf16[8,1024,512]{2,1,0:T(8,128)(2,1)}, u32[]{:S(2)}) copy-start(bf16[8,1024,512]{2,1,0:T(8,128)(2,1)} %cv.1) | copy-start | bytes 25165828
  28.3 1.6 %copy-start.4 = (bf16[8,256,512]{2,1,0:T(8,128)(2,1)S(1)}, bf16[8,256,512]{2,1,0:T(8,128)(2,1)}, u32[]{:S(2)}) copy-start(bf16[8,256,512]{2,1,0:T(8,128)(2,1)} %uk.1) | copy-start | bytes 6291460
  29.9 1.6 %copy-start.5 = (bf16[8,256,512]{2,1,0:T(8,128)(2,1)S(1)}, bf16[8,256,512]{2,1,0:T(8,128)(2,1)}, u32[]{:S(2)}) copy-start(bf16[8,256,512]{2,1,0:T(8,128)(2,1)} %uv.1) | copy-start | bytes 6291460
  32.9 19.3 %copy-start.7 = (bf16[1024,576]{0,1:T(8,128)(2,1)S(1)}, bf16[1024,576]{0,1:T(8,128)(2,1)}, u32[]{:S(2)}) copy-start(bf16[1024,576]{0,1:T(8,128)(2,1)} %param.35) | copy-start | bytes 3538948
  32.9 23.8 %copy-start.14 = (f32[576]{0:T(1024)S(1)}, f32[576]{0:T(1024)}, u32[]{:S(2)}) copy-start(f32[576]{0:T(1024)} %param.28) | copy-start | bytes 6916
  32.9 23.8 %copy-start.15 = (f32[576]{0:T(1024)S(1)}, f32[576]{0:T(1024)}, u32[]{:S(2)}) copy-start(f32[576]{0:T(1024)} %param.29) | copy-start | bytes 6916
  40.6 1.3 collective-permute-start.5
  41.9 4.4 %collective-permute-start.6 = (f32[16,640]{1,0:T(8,128)S(1)}, f32[16,640]{1,0:T(8,128)S(1)}, u32[]{:S(2)}, u32[]{:S(2)}) collective-permute-start(f32[16,640]{1,0:T(8,128)S(1)} %add.19.refs_0_), channel_id=1, source_target_pairs={{0,1},{1,0},{2,3},{3,2},{4,5},{5,4},{6,7},{7,6},{8,9},{9,8},{10,11... | collective-permute-start | bytes 122888 | tf_op jit(solution)/shard_map/attend/ppermute | solution.py:612
  43.4 6.2 %collective-permute-start.7 = (f32[16,640]{1,0:T(8,128)S(1)}, f32[16,640]{1,0:T(8,128)S(1)}, u32[]{:S(2)}, u32[]{:S(2)}) collective-permute-start(f32[16,640]{1,0:T(8,128)S(1)} %add.19.refs_0_), channel_id=1, source_target_pairs={{0,2},{1,3},{2,0},{3,1},{4,6},{5,7},{6,4},{7,5},{8,10},{9,11},{10,... | collective-permute-start | bytes 122888 | tf_op jit(solution)/shard_map/attend/ppermute | solution.py:612
  45.0 5.8 %collective-permute-start.8 = (f32[16,640]{1,0:T(8,128)S(1)}, f32[16,640]{1,0:T(8,128)S(1)}, u32[]{:S(2)}, u32[]{:S(2)}) collective-permute-start(f32[16,640]{1,0:T(8,128)S(1)} %add.19.refs_0_), channel_id=1, source_target_pairs={{0,3},{1,2},{2,1},{3,0},{4,7},{5,6},{6,5},{7,4},{8,11},{9,10},{10,... | collective-permute-start | bytes 122888 | tf_op jit(solution)/shard_map/attend/ppermute | solution.py:612
  50.9 1.2 collective-permute-start.9
  53.1 4.0 %collective-permute-start.10 = (f32[16,576]{1,0:T(8,128)S(1)}, f32[16,576]{1,0:T(8,128)S(1)}, u32[]{:S(2)}, u32[]{:S(2)}) collective-permute-start(f32[16,576]{1,0:T(8,128)S(1)} %attend.5.refs_4_), channel_id=1, source_target_pairs={{0,4},{4,0},{8,12},{12,8},{1,5},{5,1},{9,13},{13,9},{2,6},{6,2},{1... | collective-permute-start | bytes 110600 | tf_op jit(solution)/shard_map/attend/ppermute | solution.py:612
  54.6 4.0 %collective-permute-start.11 = (f32[16,576]{1,0:T(8,128)S(1)}, f32[16,576]{1,0:T(8,128)S(1)}, u32[]{:S(2)}, u32[]{:S(2)}) collective-permute-start(f32[16,576]{1,0:T(8,128)S(1)} %attend.5.refs_4_), channel_id=1, source_target_pairs={{0,8},{4,12},{8,0},{12,4},{1,9},{5,13},{9,1},{13,5},{2,10},{6,14},... | collective-permute-start | bytes 110600 | tf_op jit(solution)/shard_map/attend/ppermute | solution.py:612
  56.1 4.9 %collective-permute-start.12 = (f32[16,576]{1,0:T(8,128)S(1)}, f32[16,576]{1,0:T(8,128)S(1)}, u32[]{:S(2)}, u32[]{:S(2)}) collective-permute-start(f32[16,576]{1,0:T(8,128)S(1)} %attend.5.refs_4_), channel_id=1, source_target_pairs={{0,12},{4,8},{8,4},{12,0},{1,13},{5,9},{9,5},{13,1},{2,14},{6,10},... | collective-permute-start | bytes 110600 | tf_op jit(solution)/shard_map/attend/ppermute | solution.py:612
  61.0 4.0 %copy-start = (bf16[576,9216]{1,0:T(8,128)(2,1)S(1)}, bf16[576,9216]{1,0:T(8,128)(2,1)}, u32[]{:S(2)}) copy-start(bf16[576,9216]{1,0:T(8,128)(2,1)} %refs_9_.1) | copy-start | bytes 31850500
  72.3 41.2 %copy-start.16 = (f32[576]{0:T(1024)S(1)}, f32[576]{0:T(1024)}, u32[]{:S(2)}) copy-start(f32[576]{0:T(1024)} %param.30) | copy-start | bytes 6916
  72.3 41.2 %copy-start.17 = (f32[576]{0:T(1024)S(1)}, f32[576]{0:T(1024)}, u32[]{:S(2)}) copy-start(f32[576]{0:T(1024)} %param.31) | copy-start | bytes 6916
  72.3 2.1 %collective-permute-start.13 = (bf16[4,32,2432]{2,1,0:T(8,128)(2,1)S(1)}, bf16[4,32,2432]{2,1,0:T(8,128)(2,1)S(1)}, u32[]{:S(2)}, u32[]{:S(2)}) collective-permute-start(bf16[4,32,2432]{2,1,0:T(8,128)(2,1)S(1)} %get-tuple-element.32), channel_id=1, source_target_pairs={{0,16},{16,0},{1,17},{17,1},{2,18},{18,2},{3,19},{19,3},{4,20},{20... | collective-permute-start | bytes 1867784 | tf_op jit(solution)/shard_map/gate_up/ppermute | solution.py:612
  74.7 8.8 %collective-permute-start.14 = (bf16[32,2432]{1,0:T(8,128)(2,1)S(1)}, bf16[32,2432]{1,0:T(8,128)(2,1)S(1)}, u32[]{:S(2)}, u32[]{:S(2)}) collective-permute-start(bf16[32,2432]{1,0:T(8,128)(2,1)S(1)} %get-tuple-element.34), channel_id=1, source_target_pairs={{0,1},{1,0},{2,3},{3,2},{4,5},{5,4},{6,7},{7,6},{8,9},{9,8},{10,11... | collective-permute-start | bytes 466952 | tf_op jit(solution)/shard_map/gate_up/ppermute | solution.py:612
  74.7 14.5 %collective-permute-start.15 = (bf16[32,2432]{1,0:T(8,128)(2,1)S(1)}, bf16[32,2432]{1,0:T(8,128)(2,1)S(1)}, u32[]{:S(2)}, u32[]{:S(2)}) collective-permute-start(bf16[32,2432]{1,0:T(8,128)(2,1)S(1)} %get-tuple-element.35), channel_id=1, source_target_pairs={{0,2},{1,3},{2,0},{3,1},{4,6},{5,7},{6,4},{7,5},{8,10},{9,11},{10,... | collective-permute-start | bytes 466952 | tf_op jit(solution)/shard_map/gate_up/ppermute | solution.py:612
  76.7 12.6 %collective-permute-start.16 = (bf16[32,2432]{1,0:T(8,128)(2,1)S(1)}, bf16[32,2432]{1,0:T(8,128)(2,1)S(1)}, u32[]{:S(2)}, u32[]{:S(2)}) collective-permute-start(bf16[32,2432]{1,0:T(8,128)(2,1)S(1)} %get-tuple-element.36), channel_id=1, source_target_pairs={{0,3},{1,2},{2,1},{3,0},{4,7},{5,6},{6,5},{7,4},{8,11},{9,10},{10,... | collective-permute-start | bytes 466952 | tf_op jit(solution)/shard_map/gate_up/ppermute | solution.py:612
  89.7 5.6 %collective-permute-start.17 = (bf16[16,1152]{1,0:T(8,128)(2,1)S(1)}, bf16[16,1152]{1,0:T(8,128)(2,1)S(1)}, u32[]{:S(2)}, u32[]{:S(2)}) collective-permute-start(bf16[16,1152]{1,0:T(8,128)(2,1)S(1)} %get-tuple-element.38.refs_1_), channel_id=1, source_target_pairs={{0,1},{1,0},{2,3},{3,2},{4,5},{5,4},{6,7},{7,6},{8,9},{9,8},{10,11... | collective-permute-start | bytes 110600 | tf_op jit(solution)/shard_map/down/ppermute | solution.py:612
  92.9 5.2 %collective-permute-start.18 = (bf16[16,1152]{1,0:T(8,128)(2,1)S(1)}, bf16[16,1152]{1,0:T(8,128)(2,1)S(1)}, u32[]{:S(2)}, u32[]{:S(2)}) collective-permute-start(bf16[16,1152]{1,0:T(8,128)(2,1)S(1)} %get-tuple-element.38.refs_1_), channel_id=1, source_target_pairs={{0,2},{1,3},{2,0},{3,1},{4,6},{5,7},{6,4},{7,5},{8,10},{9,11},{10,... | collective-permute-start | bytes 110600 | tf_op jit(solution)/shard_map/down/ppermute | solution.py:612
  93.6 5.8 %collective-permute-start.19 = (bf16[16,1152]{1,0:T(8,128)(2,1)S(1)}, bf16[16,1152]{1,0:T(8,128)(2,1)S(1)}, u32[]{:S(2)}, u32[]{:S(2)}) collective-permute-start(bf16[16,1152]{1,0:T(8,128)(2,1)S(1)} %get-tuple-element.38.refs_1_), channel_id=1, source_target_pairs={{0,3},{1,2},{2,1},{3,0},{4,7},{5,6},{6,5},{7,4},{8,11},{9,10},{10,... | collective-permute-start | bytes 110600 | tf_op jit(solution)/shard_map/down/ppermute | solution.py:612
  95.3 4.0 %collective-permute-start.20 = (bf16[16,1152]{1,0:T(8,128)(2,1)S(1)}, bf16[16,1152]{1,0:T(8,128)(2,1)S(1)}, u32[]{:S(2)}, u32[]{:S(2)}) collective-permute-start(bf16[16,1152]{1,0:T(8,128)(2,1)S(1)} %get-tuple-element.38.refs_1_), channel_id=1, source_target_pairs={{0,16},{16,0},{1,17},{17,1},{2,18},{18,2},{3,19},{19,3},{4,20},{20... | collective-permute-start | bytes 110600 | tf_op jit(solution)/shard_map/down/ppermute | solution.py:612
  95.3 4.0 %collective-permute-start.21 = (bf16[16,1152]{1,0:T(8,128)(2,1)S(1)}, bf16[16,1152]{1,0:T(8,128)(2,1)S(1)}, u32[]{:S(2)}, u32[]{:S(2)}) collective-permute-start(bf16[16,1152]{1,0:T(8,128)(2,1)S(1)} %collective-permute-done.17.refs_2_), channel_id=1, source_target_pairs={{0,16},{16,0},{1,17},{17,1},{2,18},{18,2},{3,19},{19,3},{4,20},{20... | collective-permute-start | bytes 110600 | tf_op jit(solution)/shard_map/down/ppermute | solution.py:612
  98.1 1.3 collective-permute-start.22
  99.3 1.2 collective-permute-start.23
  100.5 4.0 %copy-start.1 = (bf16[9216,576]{0,1:T(8,128)(2,1)S(1)}, bf16[9216,576]{0,1:T(8,128)(2,1)}, u32[]{:S(2)}) copy-start(bf16[9216,576]{0,1:T(8,128)(2,1)} %param.38) | copy-start | bytes 31850500
  110.0 4.1 %collective-permute-start.24 = (f32[16,576]{1,0:T(8,128)S(1)}, f32[16,576]{1,0:T(8,128)S(1)}, u32[]{:S(2)}, u32[]{:S(2)}) collective-permute-start(f32[16,576]{1,0:T(8,128)S(1)} %down.1.refs_0_), channel_id=1, source_target_pairs={{0,4},{4,0},{8,12},{12,8},{1,5},{5,1},{9,13},{13,9},{2,6},{6,2},{1... | collective-permute-start | bytes 110600 | tf_op jit(solution)/shard_map/down/ppermute | solution.py:612
  110.6 4.4 %collective-permute-start.25 = (f32[16,576]{1,0:T(8,128)S(1)}, f32[16,576]{1,0:T(8,128)S(1)}, u32[]{:S(2)}, u32[]{:S(2)}) collective-permute-start(f32[16,576]{1,0:T(8,128)S(1)} %down.1.refs_0_), channel_id=1, source_target_pairs={{0,8},{4,12},{8,0},{12,4},{1,9},{5,13},{9,1},{13,5},{2,10},{6,14},... | collective-permute-start | bytes 110600 | tf_op jit(solution)/shard_map/down/ppermute | solution.py:612
  111.1 4.9 %collective-permute-start.26 = (f32[16,576]{1,0:T(8,128)S(1)}, f32[16,576]{1,0:T(8,128)S(1)}, u32[]{:S(2)}, u32[]{:S(2)}) collective-permute-start(f32[16,576]{1,0:T(8,128)S(1)} %down.1.refs_0_), channel_id=1, source_target_pairs={{0,12},{4,8},{8,4},{12,0},{1,13},{5,9},{9,5},{13,1},{2,14},{6,10},... | collective-permute-start | bytes 110600 | tf_op jit(solution)/shard_map/down/ppermute | solution.py:612
  116.2 30.6 %copy-start.13 = (s32[4096]{0:T(1024)S(1)}, s32[4096]{0:T(1024)}, u32[]{:S(2)}) copy-start(s32[4096]{0:T(1024)} %param.25) | copy-start | bytes 49156
  116.2 30.7 %copy-start.18 = (f32[8]{0:T(128)S(1)}, f32[8]{0:T(128)}, u32[]{:S(2)}) copy-start(f32[8]{0:T(128)} %param.26) | copy-start | bytes 100
  116.2 4.4 %collective-permute-start.27 = (bf16[48,576]{1,0:T(8,128)(2,1)S(1)}, bf16[48,576]{1,0:T(8,128)(2,1)S(1)}, u32[]{:S(2)}, u32[]{:S(2)}) collective-permute-start(bf16[48,576]{1,0:T(8,128)(2,1)S(1)} %head.3.refs_1_), channel_id=1, source_target_pairs={{0,1},{1,0},{2,3},{3,2},{4,5},{5,4},{6,7},{7,6},{8,9},{9,8},{10,11... | collective-permute-start | bytes 165896 | tf_op jit(solution)/shard_map/head/ppermute | solution.py:612
  116.4 5.8 %collective-permute-start.28 = (bf16[48,576]{1,0:T(8,128)(2,1)S(1)}, bf16[48,576]{1,0:T(8,128)(2,1)S(1)}, u32[]{:S(2)}, u32[]{:S(2)}) collective-permute-start(bf16[48,576]{1,0:T(8,128)(2,1)S(1)} %head.3.refs_1_), channel_id=1, source_target_pairs={{0,2},{1,3},{2,0},{3,1},{4,6},{5,7},{6,4},{7,5},{8,10},{9,11},{10,... | collective-permute-start | bytes 165896 | tf_op jit(solution)/shard_map/head/ppermute | solution.py:612
  118.6 6.0 %collective-permute-start.29 = (bf16[48,576]{1,0:T(8,128)(2,1)S(1)}, bf16[48,576]{1,0:T(8,128)(2,1)S(1)}, u32[]{:S(2)}, u32[]{:S(2)}) collective-permute-start(bf16[48,576]{1,0:T(8,128)(2,1)S(1)} %head.3.refs_1_), channel_id=1, source_target_pairs={{0,3},{1,2},{2,1},{3,0},{4,7},{5,6},{6,5},{7,4},{8,11},{9,10},{10,... | collective-permute-start | bytes 165896 | tf_op jit(solution)/shard_map/head/ppermute | solution.py:612
  146.7 2.0 %collective-permute-start.30 = (f32[16,8320]{1,0:T(8,128)S(1)}, f32[16,8320]{1,0:T(8,128)S(1)}, u32[]{:S(2)}, u32[]{:S(2)}) collective-permute-start(f32[16,8320]{1,0:T(8,128)S(1)} %get-tuple-element.40), channel_id=1, source_target_pairs={{0,16},{16,0},{1,17},{17,1},{2,18},{18,2},{3,19},{19,3},{4,20},{20... | collective-permute-start | bytes 1597448 | tf_op jit(solution)/shard_map/head/ppermute | solution.py:612
  (5 other events, 4.2 us)

commit v2 on v1

--- a/solution.py
+++ b/solution.py
@@ -220,9 +220,11 @@
 BF = jnp.bfloat16
 F32 = jnp.float32
 LANES = 128
+ANY = pl.BlockSpec(memory_space=pl.ANY)
 VMEM = pl.BlockSpec(memory_space=pltpu.VMEM)
 SMEM = pl.BlockSpec(memory_space=pltpu.SMEM)
 MIB = 1 << 20
+COPIES = 4
 
 
 def nt_dot(a, b):
@@ -231,6 +233,20 @@
 
 def nn_dot(a, b):
     return jnp.dot(a, b, preferred_element_type=F32)
+
+
+def in_hbm(value):
+    return pltpu.with_memory_space_constraint(value, pltpu.HBM)
+
+
+def started(sources, targets, done):
+    copies = [
+        pltpu.make_async_copy(source, target, done.at[at])
+        for at, (source, target) in enumerate(zip(sources, targets))
+    ]
+    for copy in copies:
+        copy.start()
+    return copies
 
 
 def limit(mib):
@@ -260,7 +276,12 @@
     return jnp.where(lane < 32, total, 0.0)
 
 
-def project_kernel(meta, hidden, gain, wq, wk, wv, rows, keep, send):
+def project_kernel(meta, *refs):
+    sources, (rows, keep, send), held, done = refs[:5], refs[5:8], refs[8:13], refs[13]
+    copies = started(sources, held, done)
+    hidden, gain, *weights = held
+    for copy in copies[:2]:
+        copy.wait()
     count = hidden.shape[0]
     half = count // 2
     group = half // 2
@@ -271,10 +292,11 @@
     streams = nn_dot(pick, hidden[...])
     rows[...] = streams.astype(BF)
     square = jnp.sum(streams * streams, axis=-1, keepdims=True)
-    normed = (streams * gain[...]).astype(BF)
+    normed = (streams * gain[...].reshape(1, -1)).astype(BF)
     first = meta[0] == 0
     offset = 0
-    for weight in (wq, wk, wv):
+    for copy, weight in zip(copies[2:], weights):
+        copy.wait()
         product = nn_dot(normed, weight[...])
         width = product.shape[1] // 2
         low, high = product[:, :width], product[:, width:]
@@ -286,13 +308,59 @@
     send[:, offset:] = tile
 
 
+def hold_kernel(starts, *refs):
+    count = len(starts)
+    sources, (*targets, token, done) = refs[1 : count + 1], refs[count + 1 :]
+    token[...] = jnp.zeros_like(token)
+    pieces = []
+    for start, source, target in zip(starts, sources, targets):
+        size = target.shape[0] // COPIES
+        pieces += [
+            (source.at[pl.ds(start + at * size, size)], target.at[pl.ds(at * size, size)])
+            for at in range(COPIES)
+        ]
+    for copy in started(*zip(*pieces), done):
+        copy.wait()
+
+
+def held_near(after, *values):
+    arrays = [array for array, _, _ in values]
+    starts = [start for _, start, _ in values]
+    shapes = [(rows,) + array.shape[1:] for array, _, rows in values]
+    size = sum(rows * array.shape[-1] * 2 for array, _, rows in values)
+    return pl.pallas_call(
+        lambda *refs: hold_kernel(starts, *refs),
+        out_shape=[pltpu.VMEM(held, array.dtype) for held, array in zip(shapes, arrays)]
+        + [jax.ShapeDtypeStruct((8, LANES), F32)],
+        in_specs=[ANY] * (1 + len(values)),
+        out_specs=[VMEM] * (1 + len(values)),
+        scratch_shapes=[pltpu.SemaphoreType.DMA((COPIES * len(values),))],
+        cost_estimate=pl.CostEstimate(flops=0, bytes_accessed=2 * size, transcendentals=0),
+        compiler_params=limit(2),
+    )(after, *map(in_hbm, arrays))
+
+
+def pair_kernel(keep, got, own, coded):
+    total = keep[...] + got[...]
+    own[...] = total
+    width = total.shape[1] - LANES
+    coded[:, :width] = total[:, :width].astype(BF)
+    coded[:, width:] = split_tile(total[:, width:])
+
+
+def added_parts(own, parts):
+    width = own.shape[1] - LANES
+    total, tile = own[:, :width], own[:, width:]
+    for part in parts:
+        total = total + part[:, :width].astype(F32)
+        tile = tile + joined_tile(part[:, width:])
+    return total, tile
+
+
 def rope_kernel(head_dim, scale, cosine, sine, *refs):
     parts, (out, squares) = refs[:-2], refs[-2:]
-    total = parts[0][...]
-    for part in parts[1:]:
-        total = total + part[...]
-    blocks = (total.shape[1] - LANES) // head_dim
-    tile = total[:, blocks * head_dim :]
+    total, tile = added_parts(parts[0], parts[1:])
+    blocks = total.shape[1] // head_dim
     squares[...] = tile
     row_scale = lax.rsqrt(tile[:, :1] / D + EPS)
     cosines, sines = cosine[...], sine[...]
@@ -305,10 +373,17 @@
         out[:, block * head_dim : (block + 1) * head_dim] = entry.astype(BF)
 
 
-def attend_kernel(
-    meta, lengths, owners, mine, other, ck, cv, uk, uv, keep, send, queries, numer, denom
-):
-    slot = pl.program_id(0)
+def attend_kernel(meta, mine, other, *refs):
+    sources, (keep, send), held = refs[:4], refs[4:6], refs[6:10]
+    queries, numer, denom, done = refs[10:]
+    slots = sources[0].shape[0]
+    order = [(slot, which) for slot in range(slots) for which in (0, 2, 1, 3)]
+    copies = started(
+        [sources[which].at[slot] for slot, which in order],
+        [held[which].at[slot] for slot, which in order],
+        done,
+    )
+    arrived = dict(zip(order, copies))
     count, heads, wide = queries.shape
     head_dim = numer.shape[2]
     half = count // 2
@@ -323,28 +398,32 @@
         b = other[:, at * head_dim : (at + 1) * head_dim].astype(F32)
         return jnp.where(first, a, b) if index == 0 else jnp.where(first, b, a)
 
-    @pl.when(slot == 0)
-    def _():
-        queries[...] = jnp.zeros_like(queries)
-        for head in range(heads):
-            kv = head // 2
-            queries[:, head, kv * head_dim : (kv + 1) * head_dim] = piece(
-                head // half_heads, head % half_heads
-            )
-
-    head_row = lax.broadcasted_iota(jnp.int32, (heads, head_dim), 0)
-    for kind, (key_ref, value_ref) in enumerate(((ck, cv), (uk, uv))):
-        block_len = key_ref.shape[1]
-        request = owners[kind, slot]
-        length = lengths[kind, request]
+    queries[...] = jnp.zeros_like(queries)
+    for head in range(heads):
+        kv = head // 2
+        queries[:, head, kv * head_dim : (kv + 1) * head_dim] = piece(
+            head // half_heads, head % half_heads
+        )
+
+    def place_of(kind, slot):
+        request = meta[3 + (2 + kind) * half + slot]
         row = request // group * half + kind * group + request % group
+        return row, meta[3 + kind * half + request]
+
+    def scores_of(kind, slot):
+        row, length = place_of(kind, slot)
         query = queries[row].astype(BF)
-        scores = nt_dot(query, key_ref[0])
-        place = block_index * block_len + lax.broadcasted_iota(jnp.int32, scores.shape, 1)
-        probs = jnp.where(
+        scores = nt_dot(query, held[2 * kind][slot])
+        place = block_index * scores.shape[1] + lax.broadcasted_iota(jnp.int32, scores.shape, 1)
+        return jnp.where(
             place < length, jnp.exp(ATTN_CAP * jnp.tanh(scores / ATTN_CAP)), 0.0
         )
-        sums = nn_dot(probs.astype(BF), value_ref[0])
+
+    head_row = lax.broadcasted_iota(jnp.int32, (heads, head_dim), 0)
+
+    def weigh(kind, slot, probs):
+        row, _ = place_of(kind, slot)
+        sums = nn_dot(probs.astype(BF), held[2 * kind + 1][slot])
         folded = jnp.zeros((heads, head_dim), F32)
         for kv in range(heads // 2):
             folded = jnp.where(
@@ -355,41 +434,49 @@
             jnp.sum(probs, axis=-1, keepdims=True), (heads, head_dim)
         )
 
-    @pl.when(slot == pl.num_programs(0) - 1)
-    def _():
-        owned = jnp.where(block_index == 0, 1.0, 0.0)
-        sums, totals = [], []
-        for head in range(heads):
-            side = head // half_heads
-            kv = head % half_heads // 2
-            query = piece(side, head % half_heads)
-            key = piece(side, half_heads + kv)
-            value = piece(side, half_heads + half_kv + kv)
-            score = jnp.sum(query * key, axis=-1, keepdims=True)
-            own = jnp.exp(ATTN_CAP * jnp.tanh(score / ATTN_CAP))
-            weight = own.astype(BF).astype(F32)
-            sums.append(numer[:, head, :] + owned * weight * value)
-            totals.append(denom[:, head, :1] + owned * own)
-        for at in range(half_heads):
-            low, high = sums[at], sums[half_heads + at]
-            keep[:, at * head_dim : (at + 1) * head_dim] = jnp.where(first, low, high)
-            send[:, at * head_dim : (at + 1) * head_dim] = jnp.where(first, high, low)
-        low = columns_tile(totals[:half_heads], count)
-        high = columns_tile(totals[half_heads:], count)
-        keep[:, half_heads * head_dim :] = jnp.where(first, low, high)
-        send[:, half_heads * head_dim :] = jnp.where(first, high, low)
+    ready = None
+    for slot in range(slots + 1):
+        if slot < slots:
+            arrived[slot, 0].wait()
+            arrived[slot, 2].wait()
+        if slot > 0:
+            arrived[slot - 1, 1].wait()
+            arrived[slot - 1, 3].wait()
+        following = [scores_of(kind, slot) for kind in (0, 1)] if slot < slots else None
+        if ready is not None:
+            for kind in (0, 1):
+                weigh(kind, slot - 1, ready[kind])
+        ready = following
+
+    owned = jnp.where(block_index == 0, 1.0, 0.0)
+    sums, totals = [], []
+    for head in range(heads):
+        side = head // half_heads
+        kv = head % half_heads // 2
+        query = piece(side, head % half_heads)
+        key = piece(side, half_heads + kv)
+        value = piece(side, half_heads + half_kv + kv)
+        score = jnp.sum(query * key, axis=-1, keepdims=True)
+        own = jnp.exp(ATTN_CAP * jnp.tanh(score / ATTN_CAP))
+        weight = own.astype(BF).astype(F32)
+        sums.append(numer[:, head, :] + owned * weight * value)
+        totals.append(denom[:, head, :1] + owned * own)
+    for at in range(half_heads):
+        low, high = sums[at], sums[half_heads + at]
+        keep[:, at * head_dim : (at + 1) * head_dim] = jnp.where(first, low, high)
+        send[:, at * head_dim : (at + 1) * head_dim] = jnp.where(first, high, low)
+    low = columns_tile(totals[:half_heads], count)
+    high = columns_tile(totals[half_heads:], count)
+    keep[:, half_heads * head_dim :] = jnp.where(first, low, high)
+    send[:, half_heads * head_dim :] = jnp.where(first, high, low)
 
 
 def attended_kernel(*refs):
     parts, out = refs[:-1], refs[-1]
-    total = parts[0][...]
-    for part in parts[1:]:
-        total = total + part[...]
-    width = out.shape[1]
-    heads = width // HD
-    for head in range(heads):
+    total, tile = added_parts(parts[0], parts[1:])
+    for head in range(out.shape[1] // HD):
         at = slice(head * HD, (head + 1) * HD)
-        out[:, at] = (total[:, at] / total[:, width + head : width + head + 1]).astype(BF)
+        out[:, at] = (total[:, at] / tile[:, head : head + 1]).astype(BF)
 
 
 def output_kernel(meta, mine, other, weight, out):
@@ -402,51 +489,55 @@
 
 
 def gate_up_kernel(pieces, meta, hidden, post_gain, pre_gain, *refs):
-    parts, (gate_weight, up_weight, keep, send, branch, inputs, tile) = refs[:-7], refs[-7:]
-    step = pl.program_id(0)
+    parts, (gate_weight, up_weight, keep, send, branch, ups, done) = refs[:-7], refs[-7:]
     count = hidden.shape[0]
+    width = ups.shape[2]
     guide, place = meta[0], meta[2]
-
-    @pl.when(step == 0)
-    def _():
-        projected = parts[0][...]
-        for part in parts[1:]:
-            projected = projected + part[...]
-        streams = hidden[...].astype(F32)
-        gained = projected * post_gain[...]
-        branch[...] = gained
-        inputs[:count, :] = (streams * pre_gain[...]).astype(BF)
-        inputs[count:, :] = (gained * pre_gain[...]).astype(BF)
-        tile[...] = columns_tile(
-            [
-                jnp.sum(projected * projected, axis=-1, keepdims=True),
-                jnp.sum(streams * gained, axis=-1, keepdims=True),
-                jnp.sum(gained * gained, axis=-1, keepdims=True),
-            ],
-            count,
-        )
-
-    operand = inputs[...]
-    gate = nn_dot(operand, gate_weight[...])
-    up = nn_dot(operand, up_weight[...])
-    width = gate.shape[1]
-    slot = lax.bitwise_xor(lax.rem(step, pieces), place)
-    mine = lax.div(step, pieces) == guide
-
-    @pl.when(mine)
-    def _():
-        keep[slot, :, :width] = gate
-        keep[slot, :, width : 2 * width] = up
-        keep[slot, :count, 2 * width :] = tile[...]
-        keep[slot, count:, 2 * width :] = jnp.zeros((count, LANES), F32)
-
-    @pl.when(jnp.logical_not(mine))
-    def _():
-        send[slot, :, :width] = gate.astype(BF)
-        send[slot, :, width : 2 * width] = up.astype(BF)
-        coded = split_tile(tile[...])
+    blocks = [pl.ds(step * width, width) for step in range(2 * pieces)]
+    copies = started(
+        [up_weight.at[:, block] for block in blocks],
+        [ups.at[step] for step in range(2 * pieces)],
+        done,
+    )
+    projected = parts[0][...]
+    for part in parts[1:]:
+        projected = projected + part[...]
+    streams = hidden[...].astype(F32)
+    gained = projected * post_gain[...].reshape(1, -1)
+    branch[...] = gained
+    scale = pre_gain[...].reshape(1, -1)
+    operand = jnp.concatenate([(streams * scale).astype(BF), (gained * scale).astype(BF)])
+    tile = columns_tile(
+        [
+            jnp.sum(projected * projected, axis=-1, keepdims=True),
+            jnp.sum(streams * gained, axis=-1, keepdims=True),
+            jnp.sum(gained * gained, axis=-1, keepdims=True),
+        ],
+        count,
+    )
+    coded = split_tile(tile)
+    for slot in range(pieces):
+        keep[slot, :count, 2 * width :] = tile
+        keep[slot, count:, 2 * width :] = jnp.zeros_like(tile)
         send[slot, :count, 2 * width :] = coded
         send[slot, count:, 2 * width :] = jnp.zeros_like(coded)
+    for part in range(4 * pieces):
+        step, offset = part % (2 * pieces), part // (2 * pieces) * width
+        slot = lax.bitwise_xor(place, step % pieces)
+        mine = guide == step // pieces
+        if offset:
+            copies[step].wait()
+            product = nn_dot(operand, ups[step])
+        else:
+            product = nn_dot(operand, gate_weight[:, step * width : (step + 1) * width])
+
+        @pl.when(mine)
+        def _(product=product, slot=slot, offset=offset):
+            keep[slot, :, offset : offset + width] = product
+
+        @pl.when(jnp.logical_not(mine))
+        def _(product=product, slot=slot, offset=offset):
+            send[slot, :, offset : offset + width] = product.astype(BF)
 
 
 def share_kernel(keep, got, own, *outs):
@@ -493,19 +584,16 @@
 
 
 def down_kernel(pieces, meta, *refs):
-    mine, other = refs[:pieces], refs[pieces : 2 * pieces]
-    weight, out = refs[2 * pieces :]
-    step = pl.program_id(0)
-
-    @pl.when(step == 0)
-    def _():
-        out[...] = jnp.zeros_like(out)
-
-    for at, part in enumerate(mine + other):
-
-        @pl.when(step == at)
-        def _(part=part):
-            out[...] += nt_dot(part[...], weight[...])
+    parts, (weight, out) = refs[: 2 * pieces], refs[2 * pieces :]
+    units = parts[0].shape[1]
+    guide, place = meta[0], meta[2]
+    total = jnp.zeros(out.shape, F32)
+    for step, part in enumerate(parts):
+        side = guide if step < pieces else 1 - guide
+        block = side * pieces + lax.bitwise_xor(place, step % pieces)
+        held = weight[:, pl.ds(pl.multiple_of(block * units, LANES), units)]
+        total = total + nt_dot(part[...], held)
+    out[...] = total
 
 
 def last_kernel(hidden, branch, scales, post_gain, final_gain, *refs):
@@ -515,9 +603,10 @@
         ffw = ffw + part[...]
     count = ffw.shape[0]
     middle = hidden[...].astype(F32) + branch[...] * scales[:, 0:1]
-    gained = ffw * post_gain[...]
-    out[:count, :] = (middle * final_gain[...]).astype(BF)
-    out[count : 2 * count, :] = (gained * final_gain[...]).astype(BF)
+    gained = ffw * post_gain[...].reshape(1, -1)
+    scale = final_gain[...].reshape(1, -1)
+    out[:count, :] = (middle * scale).astype(BF)
+    out[count : 2 * count, :] = (gained * scale).astype(BF)
     tile = columns_tile(
         [
             jnp.sum(ffw * ffw, axis=-1, keepdims=True),
@@ -532,43 +621,46 @@
 
 
 def table_kernel(pieces, meta, *refs):
-    parts, (table, keep, send, rows) = refs[:pieces], refs[pieces:]
-    step = pl.program_id(0)
+    parts, (lower, upper, table, keep, send, last, rows, done) = refs[:pieces], refs[pieces:]
+    quarter = last.shape[0]
+    copies = started([table.at[pl.ds(3 * quarter, quarter)]], [last], done)
     count = parts[0].shape[0] // 3
     half = count // 2
     width = parts[0].shape[1]
     first = meta[0] == 0
     place = meta[2]
-    step_rows = table.shape[0]
-    total_rows = keep.shape[1] - LANES
-
-    @pl.when(step == 0)
-    def _():
-        for target in range(pieces):
-            block = parts[0][: 2 * count, :].astype(F32)
-            for at in range(1, pieces):
-                block = jnp.where(
-                    lax.bitwise_xor(place, at) == target,
-                    parts[at][: 2 * count, :].astype(F32),
-                    block,
-                )
-            rows[:, target * width : (target + 1) * width] = block
-        tile = joined_tile(parts[0][2 * count :, :LANES])
+    total_rows = 4 * quarter
+    for target in range(pieces):
+        block = parts[0][: 2 * count, :].astype(F32)
         for at in range(1, pieces):
-            tile = tile + joined_tile(parts[at][2 * count :, :LANES])
-        low, high = tile[:half], tile[half:]
-        keep[:half, total_rows:] = jnp.where(first, low, high)
-        send[:half, total_rows:] = jnp.where(first, high, low)
-        keep[half:, total_rows:] = jnp.zeros((half, LANES), F32)
-        send[half:, total_rows:] = jnp.zeros((half, LANES), F32)
-
-    product = nt_dot(rows[...].astype(BF), table[...])
-    at = pl.ds(pl.multiple_of(step * step_rows, step_rows), step_rows)
-    for base in (0, half):
-        low = product[2 * base : 2 * base + half]
-        high = product[2 * base + half : 2 * base + 2 * half]
-        keep[base : base + half, at] = jnp.where(first, low, high)
-        send[base : base + half, at] = jnp.where(first, high, low)
+            block = jnp.where(
+                lax.bitwise_xor(place, at) == target,
+                parts[at][: 2 * count, :].astype(F32),
+                block,
+            )
+        rows[:, target * width : (target + 1) * width] = block
+    tile = joined_tile(parts[0][2 * count :, :LANES])
+    for at in range(1, pieces):
+        tile = tile + joined_tile(parts[at][2 * count :, :LANES])
+    low, high = tile[:half], tile[half:]
+    keep[:half, total_rows:] = jnp.where(first, low, high)
+    send[:half, total_rows:] = jnp.where(first, high, low)
+    keep[half:, total_rows:] = jnp.zeros((half, LANES), F32)
+    send[half:, total_rows:] = jnp.zeros((half, LANES), F32)
+    operand = rows[...].astype(BF)
+    step_rows = quarter // 2
+    for block in range(8):
+        ref, first_row = ((lower, 0), (upper, 4), (last, 6))[(block >= 4) + (block >= 6)]
+        if block == 6:
+            copies[0].wait()
+        start = (block - first_row) * step_rows
+        product = nt_dot(ref[start : start + step_rows, :], operand).T
+        at = slice(block * step_rows, (block + 1) * step_rows)
+        for base in (0, half):
+            low = product[2 * base : 2 * base + half]
+            high = product[2 * base + half : 2 * base + 2 * half]
+            keep[base : base + half, at] = jnp.where(first, low, high)
+            send[base : base + half, at] = jnp.where(first, high, low)
 
 
 def logits_kernel(places, weights, keep, got, out, mixed):
@@ -612,6 +704,19 @@
         lax.ppermute(values[k - 1], axis, [(i, i ^ k) for i in range(size)])
         for k in range(1, size)
     ]
+
+
+def pair_summed(keep, send):
+    return pl.pallas_call(
+        pair_kernel,
+        out_shape=(
+            jax.ShapeDtypeStruct(keep.shape, F32),
+            jax.ShapeDtypeStruct(keep.shape, BF),
+        ),
+        in_specs=[VMEM] * 2,
+        out_specs=(VMEM,) * 2,
+        compiler_params=limit(16),
+    )(keep, from_peers(send, "guide", 2)[0])
 
 
 def fast_layer(
@@ -649,9 +754,15 @@
     guide_index = lax.axis_index("guide")
     seq_index = lax.axis_index("seq")
     kv_index = lax.axis_index("kv")
-    meta = jnp.stack([guide_index, guide_index * seq_size + seq_index, seq_index]).astype(jnp.int32)
+    place = jnp.stack([guide_index, guide_index * seq_size + seq_index, seq_index]).astype(jnp.int32)
+    meta = jnp.concatenate(
+        [
+            place,
+            lengths.reshape(-1),
+            slot_owner.reshape(-1),
+        ]
+    )
     shape = jax.ShapeDtypeStruct
-    row = lambda gain: gain.reshape(1, -1)
 
     position = (
         lengths.astype(F32).reshape(kinds, 2, group).transpose(1, 0, 2).reshape(count)
@@ -673,12 +784,17 @@
                 shape((count, joint), F32),
                 shape((count, joint), F32),
             ),
-            in_specs=[SMEM] + [VMEM] * 5,
+            in_specs=[SMEM] + [ANY] * 5,
             out_specs=(VMEM,) * 3,
-            compiler_params=limit(16),
-        )(meta, hidden.reshape(count, width), row(pre_attn_gain), query_weight, key_weight, value_weight)
-        total = keep + from_peers(send, "guide", 2)[0]
-        parts = [total] + from_peers(total, "seq", seq_size)
+            scratch_shapes=[
+                pltpu.VMEM(source.shape, source.dtype)
+                for source in (hidden.reshape(count, width), pre_attn_gain, query_weight, key_weight, value_weight)
+            ]
+            + [pltpu.SemaphoreType.DMA((5,))],
+            compiler_params=limit(8),
+        )(place, *map(in_hbm, (hidden.reshape(count, width), pre_attn_gain, query_weight, key_weight, value_weight)))
+        own, coded = pair_summed(keep, send)
+        parts = [own] + from_peers(coded, "seq", seq_size)
         mine, squares = pl.pallas_call(
             lambda *refs: rope_kernel(HD, (D // H) ** (-0.5), *refs),
             out_shape=(shape((count, joint - LANES), BF), shape((count, LANES), F32)),
@@ -689,30 +805,24 @@
         other = from_peers(mine, "guide", 2)[0]
 
     with jax.named_scope("attend"):
-        cond_len, uncond_len = cond_keys.shape[1], uncond_keys.shape[1]
-        kv_width = kv_heads * HD
-        block = lambda size: pl.BlockSpec((1, size, kv_width), lambda i, *_: (i, 0, 0))
-        whole = pl.BlockSpec((count, joint - LANES), lambda i, *_: (0, 0))
         attend_width = heads // 2 * HD + LANES
-        out_block = pl.BlockSpec((count, attend_width), lambda i, *_: (0, 0))
+        caches = [cond_keys, cond_values, uncond_keys, uncond_values]
         keep, send = pl.pallas_call(
             attend_kernel,
             out_shape=(shape((count, attend_width), F32),) * 2,
-            grid_spec=pltpu.PrefetchScalarGridSpec(
-                num_scalar_prefetch=3,
-                grid=(requests,),
-                in_specs=[whole, whole] + [block(cond_len)] * 2 + [block(uncond_len)] * 2,
-                out_specs=(out_block,) * 2,
-                scratch_shapes=[
-                    pltpu.VMEM((count, heads, kv_width), F32),
-                    pltpu.VMEM((count, heads, HD), F32),
-                    pltpu.VMEM((count, heads, HD), F32),
-                ],
-            ),
-            compiler_params=limit(24),
-        )(meta, lengths, slot_owner, mine, other, cond_keys, cond_values, uncond_keys, uncond_values)
-        total = keep + from_peers(send, "guide", 2)[0]
-        parts = [total] + from_peers(total, "seq", seq_size)
+            in_specs=[SMEM] + [VMEM] * 2 + [ANY] * 4,
+            out_specs=(VMEM,) * 2,
+            scratch_shapes=[pltpu.VMEM(cache.shape, cache.dtype) for cache in caches]
+            + [
+                pltpu.VMEM((count, heads, kv_heads * HD), F32),
+                pltpu.VMEM((count, heads, HD), F32),
+                pltpu.VMEM((count, heads, HD), F32),
+            ]
+            + [pltpu.SemaphoreType.DMA((4 * requests,))],
+            compiler_params=limit(28),
+        )(meta, mine, other, *map(in_hbm, caches))
+        own, coded = pair_summed(keep, send)
+        parts = [own] + from_peers(coded, "seq", seq_size)
         mine = pl.pallas_call(
             attended_kernel,
             out_shape=shape((count, heads // 2 * HD), BF),
@@ -727,18 +837,15 @@
             in_specs=[SMEM] + [VMEM] * 3,
             out_specs=VMEM,
             compiler_params=limit(16),
-        )(meta, mine, other, output_weight.T)
+        )(place, mine, other, output_weight.T)
         parts = [part] + from_peers(part, "kv", kv_size)
+        near_gate, _ = held_near(part, (gate_weight, 0, width))
 
     with jax.named_scope("gate_up"):
         hidden_units = gate_weight.shape[1]
         unit_block = hidden_units // (2 * seq_size)
         share_width = 2 * unit_block + LANES
-        const2 = lambda i, *_: (0, 0)
-        small = pl.BlockSpec((count, width), const2)
-        gain_block = pl.BlockSpec((1, width), const2)
-        weight_block = pl.BlockSpec((width, unit_block), lambda i, *_: (0, i))
-        share_block = pl.BlockSpec((seq_size, 2 * count, share_width), lambda i, *_: (0, 0, 0))
+        steps = 2 * seq_size
         keep, send, branch = pl.pallas_call(
             lambda *refs: gate_up_kernel(seq_size, *refs),
             out_shape=(
@@ -746,18 +853,12 @@
                 shape((seq_size, 2 * count, share_width), BF),
                 shape((count, width), F32),
             ),
-            grid_spec=pltpu.PrefetchScalarGridSpec(
-                num_scalar_prefetch=1,
-                grid=(2 * seq_size,),
-                in_specs=[small, gain_block, gain_block] + [small] * kv_size + [weight_block] * 2,
-                out_specs=(share_block, share_block, small),
-                scratch_shapes=[
-                    pltpu.VMEM((2 * count, width), BF),
-                    pltpu.VMEM((count, LANES), F32),
-                ],
-            ),
-            compiler_params=limit(24),
-        )(meta, rows, row(post_attn_gain), row(pre_ffw_gain), *parts, gate_weight, up_weight)
+            in_specs=[SMEM] + [VMEM] * (4 + kv_size) + [ANY],
+            out_specs=(VMEM,) * 3,
+            scratch_shapes=[pltpu.VMEM((steps, width, unit_block), BF)]
+            + [pltpu.SemaphoreType.DMA((steps,))],
+            compiler_params=limit(16),
+        )(place, rows, post_attn_gain, pre_ffw_gain, *parts, near_gate, in_hbm(up_weight))
         got = from_peers(send, "guide", 2)[0]
         own, *shares = pl.pallas_call(
             share_kernel,
@@ -768,34 +869,30 @@
             compiler_params=limit(16),
         )(keep, got)
         parts = from_peers(shares, "seq", seq_size)
+        quarter = embedding.shape[0] // 4
+        near_down, near_low, token = held_near(
+            shares[0], (down_weight.T, 0, width), (embedding, 0, 2 * quarter)
+        )
         active, scales = pl.pallas_call(
-            active_kernel,
+            lambda token_ref, *refs: active_kernel(*refs),
             out_shape=(shape((count, unit_block), BF), shape((count, LANES), F32)),
-            in_specs=[VMEM] * (1 + seq_size),
+            in_specs=[VMEM] * (2 + seq_size),
             out_specs=(VMEM,) * 2,
             compiler_params=limit(16),
-        )(squares, own, *parts)
+        )(token, squares, own, *parts)
 
     with jax.named_scope("down"):
         mine = [active] + from_peers(active, "seq", seq_size)
         other = [from_peers(value, "guide", 2)[0] for value in mine]
-
-        def weight_place(i, meta_ref):
-            side = jnp.where(i < seq_size, meta_ref[0], 1 - meta_ref[0])
-            return (0, side * seq_size + lax.bitwise_xor(lax.rem(i, seq_size), meta_ref[2]))
+        near_high, _ = held_near(active, (embedding, 2 * quarter, quarter))
 
         part = pl.pallas_call(
             lambda *refs: down_kernel(seq_size, *refs),
             out_shape=shape((count, width), F32),
-            grid_spec=pltpu.PrefetchScalarGridSpec(
-                num_scalar_prefetch=1,
-                grid=(2 * seq_size,),
-                in_specs=[pl.BlockSpec((count, unit_block), const2)] * (2 * seq_size)
-                + [pl.BlockSpec((width, unit_block), weight_place)],
-                out_specs=small,
-            ),
-            compiler_params=limit(16),
-        )(meta, *mine, *other, down_weight.T)
+            in_specs=[SMEM] + [VMEM] * (1 + steps),
+            out_specs=VMEM,
+            compiler_params=limit(8),
+        )(place, *mine, *other, near_down)
         parts = [part] + from_peers(part, "kv", kv_size)
 
     with jax.named_scope("head"):
@@ -805,25 +902,21 @@
             in_specs=[VMEM] * (5 + kv_size),
             out_specs=VMEM,
             compiler_params=limit(16),
-        )(rows, branch, scales, row(post_ffw_gain), row(final_gain), *parts)
+        )(rows, branch, scales, post_ffw_gain, final_gain, *parts)
         parts = [mine] + from_peers(mine, "seq", seq_size)
         table_rows, table_width = embedding.shape
-        step_rows = min(512, table_rows)
-        piece_block = pl.BlockSpec((3 * count, width), const2)
-        logit_block = pl.BlockSpec((count, table_rows + LANES), const2)
         keep, send = pl.pallas_call(
             lambda *refs: table_kernel(seq_size, *refs),
             out_shape=(shape((count, table_rows + LANES), F32),) * 2,
-            grid_spec=pltpu.PrefetchScalarGridSpec(
-                num_scalar_prefetch=1,
-                grid=(table_rows // step_rows,),
-                in_specs=[piece_block] * seq_size
-                + [pl.BlockSpec((step_rows, table_width), lambda i, *_: (i, 0))],
-                out_specs=(logit_block,) * 2,
-                scratch_shapes=[pltpu.VMEM((2 * count, table_width), F32)],
-            ),
-            compiler_params=limit(24),
-        )(meta, *parts, embedding)
+            in_specs=[SMEM] + [VMEM] * (seq_size + 2) + [ANY],
+            out_specs=(VMEM,) * 2,
+            scratch_shapes=[
+                pltpu.VMEM((quarter, table_width), BF),
+                pltpu.VMEM((2 * count, table_width), F32),
+                pltpu.SemaphoreType.DMA((1,)),
+            ],
+            compiler_params=limit(14),
+        )(place, *parts, near_low, near_high, in_hbm(embedding))
         got = from_peers(send, "guide", 2)[0]
         allowed = allowed_ids.shape[0]
         places = allowed_ids - (kv_index * seq_size + seq_index) * table_rows

time: 152 us -> 111 us (0.73)
  local copies, waits for them, and re-layouts: 25.4 us -> 2.01 us
  waiting for transfers between devices: 43.7 us -> 21.5 us
  Pallas kernels: 47.9 us -> 54.8 us
    unnamed x44 -> x14, local copies, waits for them, and re-layouts: 24.3 us -> 0.04 us
    ppermute x31, waiting for transfers between devices: 43.7 us -> 21.5 us  [from_peers(): lax.ppermute(values[k - 1], axis, [(i, i ^ k) for i in range(size)])]
    pallas_call x1 -> x6, Pallas kernels: 0.4 us -> 19.2 us  [the longest x3 18.7 us: held_near(): pl.pallas_call(lambda *refs: hold_kernel(starts, *refs), out_shape=[pltpu...]
    pallas_call x1, Pallas kernels: 22.1 us -> 10.7 us  [fast_layer(): pl.pallas_call(lambda *refs: table_kernel(seq_size, *refs), out_shape=(sh...]
    pallas_call x1, Pallas kernels: 5.43 us -> 3.42 us  [fast_layer(): pl.pallas_call(lambda *refs: down_kernel(seq_size, *refs), out_shape=shap...]
  transfers between devices with their start and end apart: 31 -> 31, of which waited for: 21 -> 18; matrix products, arithmetic and copies ran while one was open for 1% -> 3% of each run, Pallas kernels for 0% -> 17%
where the time goes in v2:
time: 111 us
  Pallas kernels  54.8 us (49%)
  starting transfers between devices  31.3 us (28%)
  waiting for transfers between devices  21.5 us (19%)
  local copies, waits for them, and re-layouts  2.01 us (2%)
    ppermute x31, starting transfers between devices, from_peers(): lax.ppermute(values[k - 1], axis, [(i, i ^ k) for i in range(size)])  31.3 us
    ppermute x31, waiting for transfers between devices, from_peers(): lax.ppermute(values[k - 1], axis, [(i, i ^ k) for i in range(size)])  21.5 us
    pallas_call x3, Pallas kernels, held_near(): pl.pallas_call(lambda *refs: hold_kernel(starts, *refs), out_shape=[pltpu...  18.7 us
    pallas_call x1, Pallas kernels, fast_layer(): pl.pallas_call(lambda *refs: table_kernel(seq_size, *refs), out_shape=(sh...  10.7 us
    pallas_call x1, Pallas kernels, fast_layer(): pl.pallas_call(attend_kernel, out_shape=(shape((count, attend_width), F32...  8.63 us
    pallas_call x1, Pallas kernels, fast_layer(): pl.pallas_call(lambda *refs: gate_up_kernel(seq_size, *refs), out_shape=(...  6.3 us
    pallas_call x1, Pallas kernels, fast_layer(): pl.pallas_call(lambda *refs: down_kernel(seq_size, *refs), out_shape=shap...  3.42 us
    pallas_call x1, Pallas kernels, fast_layer(): pl.pallas_call(project_kernel, out_shape=(shape((count, width), BF), shap...  2.55 us
  transfers between devices with their start and end apart: 31, of which 18 were waited for; matrix products, arithmetic and copies ran while one was open for 3% of the time, Pallas kernels for 17%

profile of v2, /device:TPU:0, one launch (start us, length us, event | category | flops | bytes accessed | tf_op | source)
XLA Modules:
  0.0 111.0 jit_solution(9697584367842085310)
XLA Ops:
  0.1 2.6 %project.3 = (bf16[16,576]{1,0:T(8,128)(2,1)S(1)}, f32[16,1152]{1,0:T(8,128)S(1)}, f32[16,1152]{1,0:T(8,128)S(1)}) custom-call(s32[3]{0:T(128)S(1)} %pad_add_fusion.meta.refs_0_, bf16[16,576]{1,0:T(8,128)(2,1)} %bitcast.9, f32[576]{0:T(1024)} %refs_1_.4, bf16[576,1024]{1,0:T(8,128)(2,1)} %refs_2_.4, bf16[576,512]{1,0:T(8,128)(2,1)} %refs_3_.3, ...), custom_call_target="tpu_custom_call" | custom-call | tf_op jit(solution)/shard_map/project/pallas_call | solution.py:780
  2.6 0.5 collective-permute-start
  3.2 0.7 convert_element_type.3
  4.2 4.9 %collective-permute-start.3 = (bf16[16,1152]{1,0:T(8,128)(2,1)S(1)}, bf16[16,1152]{1,0:T(8,128)(2,1)S(1)}, u32[]{:S(2)}, u32[]{:S(2)}) collective-permute-start(bf16[16,1152]{1,0:T(8,128)(2,1)S(1)} %get-tuple-element.36), channel_id=1, source_target_pairs={{0,3},{1,2},{2,1},{3,0},{4,7},{5,6},{6,5},{7,4},{8,11},{9,10},{10,... | collective-permute-start | bytes 110600 | tf_op jit(solution)/shard_map/project/ppermute | solution.py:704
  9.1 0.6 collective-permute-start.1
  9.8 1.3 %collective-permute-done.3.refs_5_ = bf16[16,1152]{1,0:T(8,128)(2,1)S(1)} collective-permute-done((bf16[16,1152]{1,0:T(8,128)(2,1)S(1)}, bf16[16,1152]{1,0:T(8,128)(2,1)S(1)}, u32[]{:S(2)}, u32[]{:S(2)}) %collective-permute-start.3) | collective-permute-done | bytes 36896 | tf_op jit(solution)/shard_map/project/ppermute | solution.py:704
  11.1 2.9 %collective-permute-done.2.refs_4_ = bf16[16,1152]{1,0:T(8,128)(2,1)S(1)} collective-permute-done((bf16[16,1152]{1,0:T(8,128)(2,1)S(1)}, bf16[16,1152]{1,0:T(8,128)(2,1)S(1)}, u32[]{:S(2)}, u32[]{:S(2)}) %collective-permute-start.2) | collective-permute-done | bytes 36896 | tf_op jit(solution)/shard_map/project/ppermute | solution.py:704
  14.3 0.8 reshape.28
  15.1 0.8 reshape.29
  15.9 8.6 %attend.5 = (f32[16,640]{1,0:T(8,128)S(1)}, f32[16,640]{1,0:T(8,128)S(1)}) custom-call(s32[35]{0:T(128)S(1)} %concatenate.14.meta, bf16[16,1024]{1,0:T(8,128)(2,1)S(1)} %get-tuple-element.37.mine, bf16[16,1024]{1,0:T(8,128)(2,1)S(1)} %collective-permute-done.4.other, bf16[8,1024,512]{2,1,0:T(8,128)(2,1)} %refs_0_.1, bf16[8,1024,512]{2,1,0:T(8,128)(2,1)} %refs_1_.5, ...), custom_call_target="tpu_custom_call" | custom-call | tf_op jit(solution)/shard_map/attend/pallas_call | solution.py:810
  24.6 0.6 collective-permute-start.5
  25.1 0.9 collective-permute-done.5.got
  26.1 1.7 %collective-permute-start.8 = (bf16[16,640]{1,0:T(8,128)(2,1)S(1)}, bf16[16,640]{1,0:T(8,128)(2,1)S(1)}, u32[]{:S(2)}, u32[]{:S(2)}) collective-permute-start(bf16[16,640]{1,0:T(8,128)(2,1)S(1)} %get-tuple-element.41), channel_id=1, source_target_pairs={{0,3},{1,2},{2,1},{3,0},{4,7},{5,6},{6,5},{7,4},{8,11},{9,10},{10,... | collective-permute-start | bytes 61448 | tf_op jit(solution)/shard_map/attend/ppermute | solution.py:704
  28.2 2.3 %collective-permute-start.6 = (bf16[16,640]{1,0:T(8,128)(2,1)S(1)}, bf16[16,640]{1,0:T(8,128)(2,1)S(1)}, u32[]{:S(2)}, u32[]{:S(2)}) collective-permute-start(bf16[16,640]{1,0:T(8,128)(2,1)S(1)} %get-tuple-element.41), channel_id=1, source_target_pairs={{0,1},{1,0},{2,3},{3,2},{4,5},{5,4},{6,7},{7,6},{8,9},{9,8},{10,11... | collective-permute-start | bytes 61448 | tf_op jit(solution)/shard_map/attend/ppermute | solution.py:704
  30.5 1.3 %collective-permute-done.8.refs_3_ = bf16[16,640]{1,0:T(8,128)(2,1)S(1)} collective-permute-done((bf16[16,640]{1,0:T(8,128)(2,1)S(1)}, bf16[16,640]{1,0:T(8,128)(2,1)S(1)}, u32[]{:S(2)}, u32[]{:S(2)}) %collective-permute-start.8) | collective-permute-done | bytes 20512 | tf_op jit(solution)/shard_map/attend/ppermute | solution.py:704
  31.8 0.7 collective-permute-done.7.refs_2_
  32.7 1.2 %collective-permute-done.9.other = bf16[16,512]{1,0:T(8,128)(2,1)S(1)} collective-permute-done((bf16[16,512]{1,0:T(8,128)(2,1)S(1)}, bf16[16,512]{1,0:T(8,128)(2,1)S(1)}, u32[]{:S(2)}, u32[]{:S(2)}) %collective-permute-start.9) | collective-permute-done | bytes 16416 | tf_op jit(solution)/shard_map/attend/ppermute | solution.py:704
  33.9 0.9 attend.8.refs_0_.refs_4_
  34.8 2.5 %collective-permute-start.12 = (f32[16,576]{1,0:T(8,128)S(1)}, f32[16,576]{1,0:T(8,128)S(1)}, u32[]{:S(2)}, u32[]{:S(2)}) collective-permute-start(f32[16,576]{1,0:T(8,128)S(1)} %attend.8.refs_0_.refs_4_), channel_id=1, source_target_pairs={{0,12},{4,8},{8,4},{12,0},{1,13},{5,9},{9,5},{13,1},{2,14},{6,10},... | collective-permute-start | bytes 110600 | tf_op jit(solution)/shard_map/attend/ppermute | solution.py:704
  37.4 0.5 collective-permute-start.11
  37.9 0.5 collective-permute-start.10
  38.3 4.7 %attend.9 = (bf16[576,9216]{1,0:T(8,128)(2,1)S(1)}, f32[8,128]{1,0:T(8,128)}) custom-call(f32[16,576]{1,0:T(8,128)S(1)} %attend.8.refs_0_.refs_4_, bf16[576,9216]{1,0:T(8,128)(2,1)} %refs_1_.6), custom_call_target="tpu_custom_call" | custom-call | bytes 21233664 | tf_op jit(solution)/shard_map/attend/pallas_call | solution.py:331
  43.1 6.3 %gate_up.4 = (f32[4,32,2432]{2,1,0:T(8,128)S(1)}, bf16[4,32,2432]{2,1,0:T(8,128)(2,1)S(1)}, f32[16,576]{1,0:T(8,128)S(1)}) custom-call(s32[3]{0:T(128)S(1)} %pad_add_fusion.meta.refs_0_, bf16[16,576]{1,0:T(8,128)(2,1)S(1)} %get-tuple-element.32.refs_1_.hidden, f32[576]{0:T(1024)S(1)} %copy-done.3, f32[576]{0:T(1024)S(1)} %copy-done.4, ...), custom_call_target="tpu_custom_call" | custom-call | tf_op jit(solution)/shard_map/gate_up/pallas_call | solution.py:849
  49.5 2.0 %collective-permute-done.13.got = bf16[4,32,2432]{2,1,0:T(8,128)(2,1)S(1)} collective-permute-done((bf16[4,32,2432]{2,1,0:T(8,128)(2,1)S(1)}, bf16[4,32,2432]{2,1,0:T(8,128)(2,1)S(1)}, u32[]{:S(2)}, u32[]{:S(2)}) %collective-permute-start.13) | collective-permute-done | bytes 622624 | tf_op jit(solution)/shard_map/gate_up/ppermute | solution.py:704
  51.7 2.1 %collective-permute-start.15 = (bf16[32,2432]{1,0:T(8,128)(2,1)S(1)}, bf16[32,2432]{1,0:T(8,128)(2,1)S(1)}, u32[]{:S(2)}, u32[]{:S(2)}) collective-permute-start(bf16[32,2432]{1,0:T(8,128)(2,1)S(1)} %get-tuple-element.50), channel_id=1, source_target_pairs={{0,2},{1,3},{2,0},{3,1},{4,6},{5,7},{6,4},{7,5},{8,10},{9,11},{10,... | collective-permute-start | bytes 466952 | tf_op jit(solution)/shard_map/gate_up/ppermute | solution.py:704
  53.8 2.2 %collective-permute-start.16 = (bf16[32,2432]{1,0:T(8,128)(2,1)S(1)}, bf16[32,2432]{1,0:T(8,128)(2,1)S(1)}, u32[]{:S(2)}, u32[]{:S(2)}) collective-permute-start(bf16[32,2432]{1,0:T(8,128)(2,1)S(1)} %get-tuple-element.51), channel_id=1, source_target_pairs={{0,3},{1,2},{2,1},{3,0},{4,7},{5,6},{6,5},{7,4},{8,11},{9,10},{10,... | collective-permute-start | bytes 466952 | tf_op jit(solution)/shard_map/gate_up/ppermute | solution.py:704
  56.0 9.5 %gate_up.6 = (bf16[576,9216]{1,0:T(8,128)(2,1)S(1)}, bf16[4096,2304]{1,0:T(8,128)(2,1)S(1)}, f32[8,128]{1,0:T(8,128)S(1)}) custom-call(bf16[32,2432]{1,0:T(8,128)(2,1)S(1)} %get-tuple-element.46.refs_0_, bf16[576,9216]{1,0:T(8,128)(2,1)} %bitcast.8, bf16[8192,2304]{1,0:T(8,128)(2,1)} %refs_7_.1), custom_call_target="tpu_custom_call" | custom-call | bytes 58982400 | tf_op jit(solution)/shard_map/gate_up/pallas_call | solution.py:331
  65.5 0.7 collective-permute-done.15.refs_3_
  66.3 0.5 collective-permute-done.14.refs_2_
  67.2 2.4 %collective-permute-start.19 = (bf16[16,1152]{1,0:T(8,128)(2,1)S(1)}, bf16[16,1152]{1,0:T(8,128)(2,1)S(1)}, u32[]{:S(2)}, u32[]{:S(2)}) collective-permute-start(bf16[16,1152]{1,0:T(8,128)(2,1)S(1)} %get-tuple-element.53.refs_1_.refs_0_), channel_id=1, source_target_pairs={{0,3},{1,2},{2,1},{3,0},{4,7},{5,6},{6,5},{7,4},{8,11},{9,10},{10,... | collective-permute-start | bytes 110600 | tf_op jit(solution)/shard_map/down/ppermute | solution.py:704
  69.6 1.7 %collective-permute-start.18 = (bf16[16,1152]{1,0:T(8,128)(2,1)S(1)}, bf16[16,1152]{1,0:T(8,128)(2,1)S(1)}, u32[]{:S(2)}, u32[]{:S(2)}) collective-permute-start(bf16[16,1152]{1,0:T(8,128)(2,1)S(1)} %get-tuple-element.53.refs_1_.refs_0_), channel_id=1, source_target_pairs={{0,2},{1,3},{2,0},{3,1},{4,6},{5,7},{6,4},{7,5},{8,10},{9,11},{10,... | collective-permute-start | bytes 110600 | tf_op jit(solution)/shard_map/down/ppermute | solution.py:704
  71.7 1.4 %collective-permute-done.19.refs_4_ = bf16[16,1152]{1,0:T(8,128)(2,1)S(1)} collective-permute-done((bf16[16,1152]{1,0:T(8,128)(2,1)S(1)}, bf16[16,1152]{1,0:T(8,128)(2,1)S(1)}, u32[]{:S(2)}, u32[]{:S(2)}) %collective-permute-start.19) | collective-permute-done | bytes 36896 | tf_op jit(solution)/shard_map/down/ppermute | solution.py:704
  73.1 1.4 %collective-permute-done.18.refs_3_ = bf16[16,1152]{1,0:T(8,128)(2,1)S(1)} collective-permute-done((bf16[16,1152]{1,0:T(8,128)(2,1)S(1)}, bf16[16,1152]{1,0:T(8,128)(2,1)S(1)}, u32[]{:S(2)}, u32[]{:S(2)}) %collective-permute-start.18) | collective-permute-done | bytes 36896 | tf_op jit(solution)/shard_map/down/ppermute | solution.py:704
  74.5 0.8 collective-permute-done.17.refs_2_
  75.7 0.8 collective-permute-done.21.refs_6_
  76.5 3.4 %down.2.refs_0_ = f32[16,576]{1,0:T(8,128)S(1)} custom-call(s32[3]{0:T(128)S(1)} %pad_add_fusion.meta.refs_0_, bf16[16,1152]{1,0:T(8,128)(2,1)S(1)} %get-tuple-element.53.refs_1_.refs_0_, bf16[16,1152]{1,0:T(8,128)(2,1)S(1)} %collective-permute-done.17.refs_2_, bf16[16,1152]{1,0:T(8,128)(2,1)S(1)} %collective-permute-done.18.refs_3_, ...), custom_call_target="tpu_custom_call" | custom-call | tf_op jit(solution)/shard_map/down/pallas_call | solution.py:889
  79.9 2.5 %collective-permute-start.26 = (f32[16,576]{1,0:T(8,128)S(1)}, f32[16,576]{1,0:T(8,128)S(1)}, u32[]{:S(2)}, u32[]{:S(2)}) collective-permute-start(f32[16,576]{1,0:T(8,128)S(1)} %down.2.refs_0_), channel_id=1, source_target_pairs={{0,12},{4,8},{8,4},{12,0},{1,13},{5,9},{9,5},{13,1},{2,14},{6,10},... | collective-permute-start | bytes 110600 | tf_op jit(solution)/shard_map/down/ppermute | solution.py:704
  82.5 0.5 collective-permute-start.25
  83.0 0.5 collective-permute-start.24
  83.4 1.4 %collective-permute-done.26.refs_3_ = f32[16,576]{1,0:T(8,128)S(1)} collective-permute-done((f32[16,576]{1,0:T(8,128)S(1)}, f32[16,576]{1,0:T(8,128)S(1)}, u32[]{:S(2)}, u32[]{:S(2)}) %collective-permute-start.26) | collective-permute-done | bytes 36896 | tf_op jit(solution)/shard_map/down/ppermute | solution.py:704
  84.8 1.6 %collective-permute-done.25.refs_2_ = f32[16,576]{1,0:T(8,128)S(1)} collective-permute-done((f32[16,576]{1,0:T(8,128)S(1)}, f32[16,576]{1,0:T(8,128)S(1)}, u32[]{:S(2)}, u32[]{:S(2)}) %collective-permute-start.25) | collective-permute-done | bytes 36896 | tf_op jit(solution)/shard_map/down/ppermute | solution.py:704
  86.5 0.5 collective-permute-done.24.refs_1_
  87.2 2.3 %collective-permute-start.29 = (bf16[48,576]{1,0:T(8,128)(2,1)S(1)}, bf16[48,576]{1,0:T(8,128)(2,1)S(1)}, u32[]{:S(2)}, u32[]{:S(2)}) collective-permute-start(bf16[48,576]{1,0:T(8,128)(2,1)S(1)} %head.3.refs_1_), channel_id=1, source_target_pairs={{0,3},{1,2},{2,1},{3,0},{4,7},{5,6},{6,5},{7,4},{8,11},{9,10},{10,... | collective-permute-start | bytes 165896 | tf_op jit(solution)/shard_map/head/ppermute | solution.py:704
  89.7 1.9 %collective-permute-start.27 = (bf16[48,576]{1,0:T(8,128)(2,1)S(1)}, bf16[48,576]{1,0:T(8,128)(2,1)S(1)}, u32[]{:S(2)}, u32[]{:S(2)}) collective-permute-start(bf16[48,576]{1,0:T(8,128)(2,1)S(1)} %head.3.refs_1_), channel_id=1, source_target_pairs={{0,1},{1,0},{2,3},{3,2},{4,5},{5,4},{6,7},{7,6},{8,9},{9,8},{10,11... | collective-permute-start | bytes 165896 | tf_op jit(solution)/shard_map/head/ppermute | solution.py:704
  91.6 4.4 %down.3 = (bf16[2048,2304]{1,0:T(8,128)(2,1)S(1)}, f32[8,128]{1,0:T(8,128)}) custom-call(bf16[16,1152]{1,0:T(8,128)(2,1)S(1)} %get-tuple-element.53.refs_1_.refs_0_, bf16[8192,2304]{1,0:T(8,128)(2,1)} %refs_7_.1), custom_call_target="tpu_custom_call" | custom-call | bytes 18874368 | tf_op jit(solution)/shard_map/down/pallas_call | solution.py:331
  96.1 10.7 %head.4 = (f32[16,8320]{1,0:T(8,128)S(1)}, f32[16,8320]{1,0:T(8,128)S(1)}) custom-call(s32[3]{0:T(128)S(1)} %pad_add_fusion.meta.refs_0_, bf16[48,576]{1,0:T(8,128)(2,1)S(1)} %head.3.refs_1_, bf16[48,576]{1,0:T(8,128)(2,1)S(1)} %collective-permute-done.27.refs_2_, bf16[48,576]{1,0:T(8,128)(2,1)S(1)} %collective-permute-done.28.refs_3_, ...), custom_call_target="tpu_custom_call" | custom-call | tf_op jit(solution)/shard_map/head/pallas_call | solution.py:908
  107.1 1.6 %collective-permute-done.30.got = f32[16,8320]{1,0:T(8,128)S(1)} collective-permute-done((f32[16,8320]{1,0:T(8,128)S(1)}, f32[16,8320]{1,0:T(8,128)S(1)}, u32[]{:S(2)}, u32[]{:S(2)}) %collective-permute-start.30) | collective-permute-done | bytes 532512 | tf_op jit(solution)/shard_map/head/ppermute | solution.py:704
  108.8 2.2 %head.5 = f32[4,4096]{1,0:T(4,128)} custom-call(s32[8,2048]{1,0:T(8,128)S(1)} %reshape.26.places, f32[8,128]{1,0:T(8,128)S(1)} %broadcast_in_dim.5.weights, f32[16,8320]{1,0:T(8,128)S(1)} %get-tuple-element.57.keep, f32[16,8320]{1,0:T(8,128)S(1)} %collective-permute-done.30.got), custom_call_target="tpu_custom_call" | custom-call | tf_op jit(solution)/shard_map/head/pallas_call | solution.py:926
  (63 shorter events, 4.0 us)
Async XLA Ops:
  2.6 1.5 %collective-permute-start = (f32[16,1152]{1,0:T(8,128)S(1)}, f32[16,1152]{1,0:T(8,128)S(1)}, u32[]{:S(2)}, u32[]{:S(2)}) collective-permute-start(f32[16,1152]{1,0:T(8,128)S(1)} %get-tuple-element.34), channel_id=1, source_target_pairs={{0,16},{16,0},{1,17},{17,1},{2,18},{18,2},{3,19},{19,3},{4,20},{20... | collective-permute-start | bytes 221192 | tf_op jit(solution)/shard_map/project/ppermute | solution.py:704
  4.2 6.9 %collective-permute-start.3 = (bf16[16,1152]{1,0:T(8,128)(2,1)S(1)}, bf16[16,1152]{1,0:T(8,128)(2,1)S(1)}, u32[]{:S(2)}, u32[]{:S(2)}) collective-permute-start(bf16[16,1152]{1,0:T(8,128)(2,1)S(1)} %get-tuple-element.36), channel_id=1, source_target_pairs={{0,3},{1,2},{2,1},{3,0},{4,7},{5,6},{6,5},{7,4},{8,11},{9,10},{10,... | collective-permute-start | bytes 110600 | tf_op jit(solution)/shard_map/project/ppermute | solution.py:704
  9.1 4.9 %collective-permute-start.2 = (bf16[16,1152]{1,0:T(8,128)(2,1)S(1)}, bf16[16,1152]{1,0:T(8,128)(2,1)S(1)}, u32[]{:S(2)}, u32[]{:S(2)}) collective-permute-start(bf16[16,1152]{1,0:T(8,128)(2,1)S(1)} %get-tuple-element.36), channel_id=1, source_target_pairs={{0,2},{1,3},{2,0},{3,1},{4,6},{5,7},{6,4},{7,5},{8,10},{9,11},{10,... | collective-permute-start | bytes 110600 | tf_op jit(solution)/shard_map/project/ppermute | solution.py:704
  9.1 4.9 %collective-permute-start.1 = (bf16[16,1152]{1,0:T(8,128)(2,1)S(1)}, bf16[16,1152]{1,0:T(8,128)(2,1)S(1)}, u32[]{:S(2)}, u32[]{:S(2)}) collective-permute-start(bf16[16,1152]{1,0:T(8,128)(2,1)S(1)} %get-tuple-element.36), channel_id=1, source_target_pairs={{0,1},{1,0},{2,3},{3,2},{4,5},{5,4},{6,7},{7,6},{8,9},{9,8},{10,11... | collective-permute-start | bytes 110600 | tf_op jit(solution)/shard_map/project/ppermute | solution.py:704
  14.2 1.7 %collective-permute-start.4 = (bf16[16,1024]{1,0:T(8,128)(2,1)S(1)}, bf16[16,1024]{1,0:T(8,128)(2,1)S(1)}, u32[]{:S(2)}, u32[]{:S(2)}) collective-permute-start(bf16[16,1024]{1,0:T(8,128)(2,1)S(1)} %get-tuple-element.37.mine), channel_id=1, source_target_pairs={{0,16},{16,0},{1,17},{17,1},{2,18},{18,2},{3,19},{19,3},{4,20},{20... | collective-permute-start | bytes 98312 | tf_op jit(solution)/shard_map/project/ppermute | solution.py:704
  15.9 18.0 %copy-start = (bf16[1024,576]{0,1:T(8,128)(2,1)S(1)}, bf16[1024,576]{0,1:T(8,128)(2,1)}, u32[]{:S(2)}) copy-start(bf16[1024,576]{0,1:T(8,128)(2,1)} %param.35) | copy-start | bytes 3538948
  24.5 18.5 %copy-start.3 = (f32[576]{0:T(1024)S(1)}, f32[576]{0:T(1024)}, u32[]{:S(2)}) copy-start(f32[576]{0:T(1024)} %refs_2_.6) | copy-start | bytes 6916
  24.5 18.5 %copy-start.4 = (f32[576]{0:T(1024)S(1)}, f32[576]{0:T(1024)}, u32[]{:S(2)}) copy-start(f32[576]{0:T(1024)} %refs_3_.5) | copy-start | bytes 6916
  24.6 1.4 %collective-permute-start.5 = (f32[16,640]{1,0:T(8,128)S(1)}, f32[16,640]{1,0:T(8,128)S(1)}, u32[]{:S(2)}, u32[]{:S(2)}) collective-permute-start(f32[16,640]{1,0:T(8,128)S(1)} %get-tuple-element.39), channel_id=1, source_target_pairs={{0,16},{16,0},{1,17},{17,1},{2,18},{18,2},{3,19},{19,3},{4,20},{20... | collective-permute-start | bytes 122888 | tf_op jit(solution)/shard_map/attend/ppermute | solution.py:704
  26.1 5.7 %collective-permute-start.8 = (bf16[16,640]{1,0:T(8,128)(2,1)S(1)}, bf16[16,640]{1,0:T(8,128)(2,1)S(1)}, u32[]{:S(2)}, u32[]{:S(2)}) collective-permute-start(bf16[16,640]{1,0:T(8,128)(2,1)S(1)} %get-tuple-element.41), channel_id=1, source_target_pairs={{0,3},{1,2},{2,1},{3,0},{4,7},{5,6},{6,5},{7,4},{8,11},{9,10},{10,... | collective-permute-start | bytes 61448 | tf_op jit(solution)/shard_map/attend/ppermute | solution.py:704
  27.7 4.7 %collective-permute-start.7 = (bf16[16,640]{1,0:T(8,128)(2,1)S(1)}, bf16[16,640]{1,0:T(8,128)(2,1)S(1)}, u32[]{:S(2)}, u32[]{:S(2)}) collective-permute-start(bf16[16,640]{1,0:T(8,128)(2,1)S(1)} %get-tuple-element.41), channel_id=1, source_target_pairs={{0,2},{1,3},{2,0},{3,1},{4,6},{5,7},{6,4},{7,5},{8,10},{9,11},{10,... | collective-permute-start | bytes 61448 | tf_op jit(solution)/shard_map/attend/ppermute | solution.py:704
  28.2 4.3 %collective-permute-start.6 = (bf16[16,640]{1,0:T(8,128)(2,1)S(1)}, bf16[16,640]{1,0:T(8,128)(2,1)S(1)}, u32[]{:S(2)}, u32[]{:S(2)}) collective-permute-start(bf16[16,640]{1,0:T(8,128)(2,1)S(1)} %get-tuple-element.41), channel_id=1, source_target_pairs={{0,1},{1,0},{2,3},{3,2},{4,5},{5,4},{6,7},{7,6},{8,9},{9,8},{10,11... | collective-permute-start | bytes 61448 | tf_op jit(solution)/shard_map/attend/ppermute | solution.py:704
  32.6 1.2 %collective-permute-start.9 = (bf16[16,512]{1,0:T(8,128)(2,1)S(1)}, bf16[16,512]{1,0:T(8,128)(2,1)S(1)}, u32[]{:S(2)}, u32[]{:S(2)}) collective-permute-start(bf16[16,512]{1,0:T(8,128)(2,1)S(1)} %attend.7.mine), channel_id=1, source_target_pairs={{0,16},{16,0},{1,17},{17,1},{2,18},{18,2},{3,19},{19,3},{4,20},{20... | collective-permute-start | bytes 49160 | tf_op jit(solution)/shard_map/attend/ppermute | solution.py:704
  34.8 8.2 %collective-permute-start.12 = (f32[16,576]{1,0:T(8,128)S(1)}, f32[16,576]{1,0:T(8,128)S(1)}, u32[]{:S(2)}, u32[]{:S(2)}) collective-permute-start(f32[16,576]{1,0:T(8,128)S(1)} %attend.8.refs_0_.refs_4_), channel_id=1, source_target_pairs={{0,12},{4,8},{8,4},{12,0},{1,13},{5,9},{9,5},{13,1},{2,14},{6,10},... | collective-permute-start | bytes 110600 | tf_op jit(solution)/shard_map/attend/ppermute | solution.py:704
  37.4 5.7 %collective-permute-start.11 = (f32[16,576]{1,0:T(8,128)S(1)}, f32[16,576]{1,0:T(8,128)S(1)}, u32[]{:S(2)}, u32[]{:S(2)}) collective-permute-start(f32[16,576]{1,0:T(8,128)S(1)} %attend.8.refs_0_.refs_4_), channel_id=1, source_target_pairs={{0,8},{4,12},{8,0},{12,4},{1,9},{5,13},{9,1},{13,5},{2,10},{6,14},... | collective-permute-start | bytes 110600 | tf_op jit(solution)/shard_map/attend/ppermute | solution.py:704
  37.9 5.2 %collective-permute-start.10 = (f32[16,576]{1,0:T(8,128)S(1)}, f32[16,576]{1,0:T(8,128)S(1)}, u32[]{:S(2)}, u32[]{:S(2)}) collective-permute-start(f32[16,576]{1,0:T(8,128)S(1)} %attend.8.refs_0_.refs_4_), channel_id=1, source_target_pairs={{0,4},{4,0},{8,12},{12,8},{1,5},{5,1},{9,13},{13,9},{2,6},{6,2},{1... | collective-permute-start | bytes 110600 | tf_op jit(solution)/shard_map/attend/ppermute | solution.py:704
  49.4 2.1 %collective-permute-start.13 = (bf16[4,32,2432]{2,1,0:T(8,128)(2,1)S(1)}, bf16[4,32,2432]{2,1,0:T(8,128)(2,1)S(1)}, u32[]{:S(2)}, u32[]{:S(2)}) collective-permute-start(bf16[4,32,2432]{2,1,0:T(8,128)(2,1)S(1)} %get-tuple-element.45), channel_id=1, source_target_pairs={{0,16},{16,0},{1,17},{17,1},{2,18},{18,2},{3,19},{19,3},{4,20},{20... | collective-permute-start | bytes 1867784 | tf_op jit(solution)/shard_map/gate_up/ppermute | solution.py:704
  51.7 14.5 %collective-permute-start.15 = (bf16[32,2432]{1,0:T(8,128)(2,1)S(1)}, bf16[32,2432]{1,0:T(8,128)(2,1)S(1)}, u32[]{:S(2)}, u32[]{:S(2)}) collective-permute-start(bf16[32,2432]{1,0:T(8,128)(2,1)S(1)} %get-tuple-element.50), channel_id=1, source_target_pairs={{0,2},{1,3},{2,0},{3,1},{4,6},{5,7},{6,4},{7,5},{8,10},{9,11},{10,... | collective-permute-start | bytes 466952 | tf_op jit(solution)/shard_map/gate_up/ppermute | solution.py:704
  53.8 12.5 %collective-permute-start.16 = (bf16[32,2432]{1,0:T(8,128)(2,1)S(1)}, bf16[32,2432]{1,0:T(8,128)(2,1)S(1)}, u32[]{:S(2)}, u32[]{:S(2)}) collective-permute-start(bf16[32,2432]{1,0:T(8,128)(2,1)S(1)} %get-tuple-element.51), channel_id=1, source_target_pairs={{0,3},{1,2},{2,1},{3,0},{4,7},{5,6},{6,5},{7,4},{8,11},{9,10},{10,... | collective-permute-start | bytes 466952 | tf_op jit(solution)/shard_map/gate_up/ppermute | solution.py:704
  56.0 10.8 %collective-permute-start.14 = (bf16[32,2432]{1,0:T(8,128)(2,1)S(1)}, bf16[32,2432]{1,0:T(8,128)(2,1)S(1)}, u32[]{:S(2)}, u32[]{:S(2)}) collective-permute-start(bf16[32,2432]{1,0:T(8,128)(2,1)S(1)} %get-tuple-element.46.refs_0_), channel_id=1, source_target_pairs={{0,1},{1,0},{2,3},{3,2},{4,5},{5,4},{6,7},{7,6},{8,9},{9,8},{10,11... | collective-permute-start | bytes 466952 | tf_op jit(solution)/shard_map/gate_up/ppermute | solution.py:704
  65.5 21.5 %copy-start.1 = (f32[576]{0:T(1024)S(1)}, f32[576]{0:T(1024)}, u32[]{:S(2)}) copy-start(f32[576]{0:T(1024)} %post_gain.1) | copy-start | bytes 6916
  65.5 21.4 %copy-start.2 = (f32[576]{0:T(1024)S(1)}, f32[576]{0:T(1024)}, u32[]{:S(2)}) copy-start(f32[576]{0:T(1024)} %final_gain.1) | copy-start | bytes 6916
  67.2 5.9 %collective-permute-start.19 = (bf16[16,1152]{1,0:T(8,128)(2,1)S(1)}, bf16[16,1152]{1,0:T(8,128)(2,1)S(1)}, u32[]{:S(2)}, u32[]{:S(2)}) collective-permute-start(bf16[16,1152]{1,0:T(8,128)(2,1)S(1)} %get-tuple-element.53.refs_1_.refs_0_), channel_id=1, source_target_pairs={{0,3},{1,2},{2,1},{3,0},{4,7},{5,6},{6,5},{7,4},{8,11},{9,10},{10,... | collective-permute-start | bytes 110600 | tf_op jit(solution)/shard_map/down/ppermute | solution.py:704
  69.6 4.9 %collective-permute-start.18 = (bf16[16,1152]{1,0:T(8,128)(2,1)S(1)}, bf16[16,1152]{1,0:T(8,128)(2,1)S(1)}, u32[]{:S(2)}, u32[]{:S(2)}) collective-permute-start(bf16[16,1152]{1,0:T(8,128)(2,1)S(1)} %get-tuple-element.53.refs_1_.refs_0_), channel_id=1, source_target_pairs={{0,2},{1,3},{2,0},{3,1},{4,6},{5,7},{6,4},{7,5},{8,10},{9,11},{10,... | collective-permute-start | bytes 110600 | tf_op jit(solution)/shard_map/down/ppermute | solution.py:704
  71.3 4.0 %collective-permute-start.17 = (bf16[16,1152]{1,0:T(8,128)(2,1)S(1)}, bf16[16,1152]{1,0:T(8,128)(2,1)S(1)}, u32[]{:S(2)}, u32[]{:S(2)}) collective-permute-start(bf16[16,1152]{1,0:T(8,128)(2,1)S(1)} %get-tuple-element.53.refs_1_.refs_0_), channel_id=1, source_target_pairs={{0,1},{1,0},{2,3},{3,2},{4,5},{5,4},{6,7},{7,6},{8,9},{9,8},{10,11... | collective-permute-start | bytes 110600 | tf_op jit(solution)/shard_map/down/ppermute | solution.py:704
  71.7 3.6 %collective-permute-start.20 = (bf16[16,1152]{1,0:T(8,128)(2,1)S(1)}, bf16[16,1152]{1,0:T(8,128)(2,1)S(1)}, u32[]{:S(2)}, u32[]{:S(2)}) collective-permute-start(bf16[16,1152]{1,0:T(8,128)(2,1)S(1)} %get-tuple-element.53.refs_1_.refs_0_), channel_id=1, source_target_pairs={{0,16},{16,0},{1,17},{17,1},{2,18},{18,2},{3,19},{19,3},{4,20},{20... | collective-permute-start | bytes 110600 | tf_op jit(solution)/shard_map/down/ppermute | solution.py:704
  73.1 2.2 %collective-permute-start.23 = (bf16[16,1152]{1,0:T(8,128)(2,1)S(1)}, bf16[16,1152]{1,0:T(8,128)(2,1)S(1)}, u32[]{:S(2)}, u32[]{:S(2)}) collective-permute-start(bf16[16,1152]{1,0:T(8,128)(2,1)S(1)} %collective-permute-done.19.refs_4_), channel_id=1, source_target_pairs={{0,16},{16,0},{1,17},{17,1},{2,18},{18,2},{3,19},{19,3},{4,20},{20... | collective-permute-start | bytes 110600 | tf_op jit(solution)/shard_map/down/ppermute | solution.py:704
  74.5 1.2 %collective-permute-start.22 = (bf16[16,1152]{1,0:T(8,128)(2,1)S(1)}, bf16[16,1152]{1,0:T(8,128)(2,1)S(1)}, u32[]{:S(2)}, u32[]{:S(2)}) collective-permute-start(bf16[16,1152]{1,0:T(8,128)(2,1)S(1)} %collective-permute-done.18.refs_3_), channel_id=1, source_target_pairs={{0,16},{16,0},{1,17},{17,1},{2,18},{18,2},{3,19},{19,3},{4,20},{20... | collective-permute-start | bytes 110600 | tf_op jit(solution)/shard_map/down/ppermute | solution.py:704
  75.3 1.2 %collective-permute-start.21 = (bf16[16,1152]{1,0:T(8,128)(2,1)S(1)}, bf16[16,1152]{1,0:T(8,128)(2,1)S(1)}, u32[]{:S(2)}, u32[]{:S(2)}) collective-permute-start(bf16[16,1152]{1,0:T(8,128)(2,1)S(1)} %collective-permute-done.17.refs_2_), channel_id=1, source_target_pairs={{0,16},{16,0},{1,17},{17,1},{2,18},{18,2},{3,19},{19,3},{4,20},{20... | collective-permute-start | bytes 110600 | tf_op jit(solution)/shard_map/down/ppermute | solution.py:704
  79.9 4.9 %collective-permute-start.26 = (f32[16,576]{1,0:T(8,128)S(1)}, f32[16,576]{1,0:T(8,128)S(1)}, u32[]{:S(2)}, u32[]{:S(2)}) collective-permute-start(f32[16,576]{1,0:T(8,128)S(1)} %down.2.refs_0_), channel_id=1, source_target_pairs={{0,12},{4,8},{8,4},{12,0},{1,13},{5,9},{9,5},{13,1},{2,14},{6,10},... | collective-permute-start | bytes 110600 | tf_op jit(solution)/shard_map/down/ppermute | solution.py:704
  82.5 4.0 %collective-permute-start.25 = (f32[16,576]{1,0:T(8,128)S(1)}, f32[16,576]{1,0:T(8,128)S(1)}, u32[]{:S(2)}, u32[]{:S(2)}) collective-permute-start(f32[16,576]{1,0:T(8,128)S(1)} %down.2.refs_0_), channel_id=1, source_target_pairs={{0,8},{4,12},{8,0},{12,4},{1,9},{5,13},{9,1},{13,5},{2,10},{6,14},... | collective-permute-start | bytes 110600 | tf_op jit(solution)/shard_map/down/ppermute | solution.py:704
  83.0 4.0 %collective-permute-start.24 = (f32[16,576]{1,0:T(8,128)S(1)}, f32[16,576]{1,0:T(8,128)S(1)}, u32[]{:S(2)}, u32[]{:S(2)}) collective-permute-start(f32[16,576]{1,0:T(8,128)S(1)} %down.2.refs_0_), channel_id=1, source_target_pairs={{0,4},{4,0},{8,12},{12,8},{1,5},{5,1},{9,13},{13,9},{2,6},{6,2},{1... | collective-permute-start | bytes 110600 | tf_op jit(solution)/shard_map/down/ppermute | solution.py:704
  87.2 8.8 %collective-permute-start.29 = (bf16[48,576]{1,0:T(8,128)(2,1)S(1)}, bf16[48,576]{1,0:T(8,128)(2,1)S(1)}, u32[]{:S(2)}, u32[]{:S(2)}) collective-permute-start(bf16[48,576]{1,0:T(8,128)(2,1)S(1)} %head.3.refs_1_), channel_id=1, source_target_pairs={{0,3},{1,2},{2,1},{3,0},{4,7},{5,6},{6,5},{7,4},{8,11},{9,10},{10,... | collective-permute-start | bytes 165896 | tf_op jit(solution)/shard_map/head/ppermute | solution.py:704
  89.5 6.5 %collective-permute-start.28 = (bf16[48,576]{1,0:T(8,128)(2,1)S(1)}, bf16[48,576]{1,0:T(8,128)(2,1)S(1)}, u32[]{:S(2)}, u32[]{:S(2)}) collective-permute-start(bf16[48,576]{1,0:T(8,128)(2,1)S(1)} %head.3.refs_1_), channel_id=1, source_target_pairs={{0,2},{1,3},{2,0},{3,1},{4,6},{5,7},{6,4},{7,5},{8,10},{9,11},{10,... | collective-permute-start | bytes 165896 | tf_op jit(solution)/shard_map/head/ppermute | solution.py:704
  89.7 6.4 %collective-permute-start.27 = (bf16[48,576]{1,0:T(8,128)(2,1)S(1)}, bf16[48,576]{1,0:T(8,128)(2,1)S(1)}, u32[]{:S(2)}, u32[]{:S(2)}) collective-permute-start(bf16[48,576]{1,0:T(8,128)(2,1)S(1)} %head.3.refs_1_), channel_id=1, source_target_pairs={{0,1},{1,0},{2,3},{3,2},{4,5},{5,4},{6,7},{7,6},{8,9},{9,8},{10,11... | collective-permute-start | bytes 165896 | tf_op jit(solution)/shard_map/head/ppermute | solution.py:704
  96.0 10.8 %copy-start.5 = (s32[4096]{0:T(1024)S(1)}, s32[4096]{0:T(1024)}, u32[]{:S(2)}) copy-start(s32[4096]{0:T(1024)} %param.25) | copy-start | bytes 49156
  96.0 10.9 %copy-start.6 = (f32[8]{0:T(128)S(1)}, f32[8]{0:T(128)}, u32[]{:S(2)}) copy-start(f32[8]{0:T(128)} %param.26) | copy-start | bytes 100
  106.8 2.0 %collective-permute-start.30 = (f32[16,8320]{1,0:T(8,128)S(1)}, f32[16,8320]{1,0:T(8,128)S(1)}, u32[]{:S(2)}, u32[]{:S(2)}) collective-permute-start(f32[16,8320]{1,0:T(8,128)S(1)} %get-tuple-element.58), channel_id=1, source_target_pairs={{0,16},{16,0},{1,17},{17,1},{2,18},{18,2},{3,19},{19,3},{4,20},{20... | collective-permute-start | bytes 1597448 | tf_op jit(solution)/shard_map/head/ppermute | solution.py:704

commit v3 on v2

--- a/solution.py
+++ b/solution.py
@@ -225,6 +225,7 @@
 SMEM = pl.BlockSpec(memory_space=pltpu.SMEM)
 MIB = 1 << 20
 COPIES = 4
+AHEAD = 5
 
 
 def nt_dot(a, b):
@@ -314,6 +315,8 @@
     token[...] = jnp.zeros_like(token)
     pieces = []
     for start, source, target in zip(starts, sources, targets):
+        if source.shape[1:] != target.shape[1:]:
+            source = source.at[:, pl.ds(0, target.shape[1])]
         size = target.shape[0] // COPIES
         pieces += [
             (source.at[pl.ds(start + at * size, size)], target.at[pl.ds(at * size, size)])
@@ -323,11 +326,13 @@
         copy.wait()
 
 
-def held_near(after, *values):
+def held_near(after, *values, columns=None):
     arrays = [array for array, _, _ in values]
     starts = [start for _, start, _ in values]
-    shapes = [(rows,) + array.shape[1:] for array, _, rows in values]
-    size = sum(rows * array.shape[-1] * 2 for array, _, rows in values)
+    shapes = [
+        (rows,) + ((columns,) if columns else array.shape[1:]) for array, _, rows in values
+    ]
+    size = sum(2 * rows * held[-1] for (_, _, rows), held in zip(values, shapes))
     return pl.pallas_call(
         lambda *refs: hold_kernel(starts, *refs),
         out_shape=[pltpu.VMEM(held, array.dtype) for held, array in zip(shapes, arrays)]
@@ -489,16 +494,22 @@
 
 
 def gate_up_kernel(pieces, meta, hidden, post_gain, pre_gain, *refs):
-    parts, (gate_weight, up_weight, keep, send, branch, ups, done) = refs[:-7], refs[-7:]
+    parts, (near_gate, gate_weight, up_weight, keep, send, branch, held, done) = refs[:-8], refs[-8:]
     count = hidden.shape[0]
-    width = ups.shape[2]
+    width = held.shape[2]
     guide, place = meta[0], meta[2]
-    blocks = [pl.ds(step * width, width) for step in range(2 * pieces)]
-    copies = started(
-        [up_weight.at[:, block] for block in blocks],
-        [ups.at[step] for step in range(2 * pieces)],
-        done,
-    )
+    steps = 2 * pieces
+    near = near_gate.shape[1] // width
+    far = [(gate_weight, step) for step in range(near, steps)]
+    far += [(up_weight, step) for step in range(steps)]
+    copies = [
+        pltpu.make_async_copy(
+            weight.at[:, pl.ds(step * width, width)], held.at[at], done.at[at]
+        )
+        for at, (weight, step) in enumerate(far)
+    ]
+    for copy in copies[:AHEAD]:
+        copy.start()
     projected = parts[0][...]
     for part in parts[1:]:
         projected = projected + part[...]
@@ -521,15 +532,17 @@
         keep[slot, count:, 2 * width :] = jnp.zeros_like(tile)
         send[slot, :count, 2 * width :] = coded
         send[slot, count:, 2 * width :] = jnp.zeros_like(coded)
-    for part in range(4 * pieces):
-        step, offset = part % (2 * pieces), part // (2 * pieces) * width
+    for part in range(2 * steps):
+        step, offset = part % steps, part // steps * width
         slot = lax.bitwise_xor(place, step % pieces)
         mine = guide == step // pieces
-        if offset:
-            copies[step].wait()
-            product = nn_dot(operand, ups[step])
+        if part < near:
+            product = nn_dot(operand, near_gate[:, step * width : (step + 1) * width])
         else:
-            product = nn_dot(operand, gate_weight[:, step * width : (step + 1) * width])
+            copies[part - near].wait()
+            if part - near + AHEAD < len(copies):
+                copies[part - near + AHEAD].start()
+            product = nn_dot(operand, held[part - near])
 
         @pl.when(mine)
         def _(product=product, slot=slot, offset=offset):
@@ -583,8 +596,13 @@
     out[...] = (jax.nn.gelu(gate, approximate=True) * up).astype(BF)
 
 
+def by_distance(parts):
+    return parts[:1] + parts[:0:-1]
+
+
 def down_kernel(pieces, meta, *refs):
-    parts, (weight, out) = refs[: 2 * pieces], refs[2 * pieces :]
+    parts = by_distance(refs[:pieces]) + by_distance(refs[pieces : 2 * pieces])
+    weight, out = refs[2 * pieces :]
     units = parts[0].shape[1]
     guide, place = meta[0], meta[2]
     total = jnp.zeros(out.shape, F32)
@@ -621,7 +639,8 @@
 
 
 def table_kernel(pieces, meta, *refs):
-    parts, (lower, upper, table, keep, send, last, rows, done) = refs[:pieces], refs[pieces:]
+    parts, (lower, middle, upper, table, keep, send, last, rows, done) = refs[:pieces], refs[pieces:]
+    parts = by_distance(parts)
     quarter = last.shape[0]
     copies = started([table.at[pl.ds(3 * quarter, quarter)]], [last], done)
     count = parts[0].shape[0] // 3
@@ -650,7 +669,9 @@
     operand = rows[...].astype(BF)
     step_rows = quarter // 2
     for block in range(8):
-        ref, first_row = ((lower, 0), (upper, 4), (last, 6))[(block >= 4) + (block >= 6)]
+        ref, first_row = ((lower, 0), (middle, 4), (upper, 5), (last, 6))[
+            (block >= 4) + (block >= 5) + (block >= 6)
+        ]
         if block == 6:
             copies[0].wait()
         start = (block - first_row) * step_rows
@@ -702,7 +723,7 @@
     values = value if isinstance(value, (list, tuple)) else [value] * (size - 1)
     return [
         lax.ppermute(values[k - 1], axis, [(i, i ^ k) for i in range(size)])
-        for k in range(1, size)
+        for k in range(size - 1, 0, -1)
     ]
 
 
@@ -839,7 +860,9 @@
             compiler_params=limit(16),
         )(place, mine, other, output_weight.T)
         parts = [part] + from_peers(part, "kv", kv_size)
-        near_gate, _ = held_near(part, (gate_weight, 0, width))
+        near_gate, _ = held_near(
+            part, (gate_weight, 0, width), columns=3 * gate_weight.shape[1] // 4
+        )
 
     with jax.named_scope("gate_up"):
         hidden_units = gate_weight.shape[1]
@@ -853,12 +876,14 @@
                 shape((seq_size, 2 * count, share_width), BF),
                 shape((count, width), F32),
             ),
-            in_specs=[SMEM] + [VMEM] * (4 + kv_size) + [ANY],
+            in_specs=[SMEM] + [VMEM] * (4 + kv_size) + [ANY] * 2,
             out_specs=(VMEM,) * 3,
-            scratch_shapes=[pltpu.VMEM((steps, width, unit_block), BF)]
-            + [pltpu.SemaphoreType.DMA((steps,))],
-            compiler_params=limit(16),
-        )(place, rows, post_attn_gain, pre_ffw_gain, *parts, near_gate, in_hbm(up_weight))
+            scratch_shapes=[
+                pltpu.VMEM((steps * 5 // 4, width, unit_block), BF),
+                pltpu.SemaphoreType.DMA((steps * 5 // 4,)),
+            ],
+            compiler_params=limit(18),
+        )(place, rows, post_attn_gain, pre_ffw_gain, *parts, near_gate, in_hbm(gate_weight), in_hbm(up_weight))
         got = from_peers(send, "guide", 2)[0]
         own, *shares = pl.pallas_call(
             share_kernel,
@@ -869,6 +894,7 @@
             compiler_params=limit(16),
         )(keep, got)
         parts = from_peers(shares, "seq", seq_size)
+        parts = parts[1:2] + parts[:1] + parts[2:]
         quarter = embedding.shape[0] // 4
         near_down, near_low, token = held_near(
             shares[0], (down_weight.T, 0, width), (embedding, 0, 2 * quarter)
@@ -884,7 +910,6 @@
     with jax.named_scope("down"):
         mine = [active] + from_peers(active, "seq", seq_size)
         other = [from_peers(value, "guide", 2)[0] for value in mine]
-        near_high, _ = held_near(active, (embedding, 2 * quarter, quarter))
 
         part = pl.pallas_call(
             lambda *refs: down_kernel(seq_size, *refs),
@@ -894,21 +919,23 @@
             compiler_params=limit(8),
         )(place, *mine, *other, near_down)
         parts = [part] + from_peers(part, "kv", kv_size)
+        near_middle, token = held_near(part, (embedding, 2 * quarter, quarter // 2))
 
     with jax.named_scope("head"):
         mine = pl.pallas_call(
-            last_kernel,
+            lambda token_ref, *refs: last_kernel(*refs),
             out_shape=shape((3 * count, width), BF),
-            in_specs=[VMEM] * (5 + kv_size),
+            in_specs=[VMEM] * (6 + kv_size),
             out_specs=VMEM,
             compiler_params=limit(16),
-        )(rows, branch, scales, post_ffw_gain, final_gain, *parts)
+        )(token, rows, branch, scales, post_ffw_gain, final_gain, *parts)
         parts = [mine] + from_peers(mine, "seq", seq_size)
+        near_high, _ = held_near(mine, (embedding, 5 * quarter // 2, quarter // 2))
         table_rows, table_width = embedding.shape
         keep, send = pl.pallas_call(
             lambda *refs: table_kernel(seq_size, *refs),
             out_shape=(shape((count, table_rows + LANES), F32),) * 2,
-            in_specs=[SMEM] + [VMEM] * (seq_size + 2) + [ANY],
+            in_specs=[SMEM] + [VMEM] * (seq_size + 3) + [ANY],
             out_specs=(VMEM,) * 2,
             scratch_shapes=[
                 pltpu.VMEM((quarter, table_width), BF),
@@ -916,7 +943,7 @@
                 pltpu.SemaphoreType.DMA((1,)),
             ],
             compiler_params=limit(14),
-        )(place, *parts, near_low, near_high, in_hbm(embedding))
+        )(place, *parts, near_low, near_middle, near_high, in_hbm(embedding))
         got = from_peers(send, "guide", 2)[0]
         allowed = allowed_ids.shape[0]
         places = allowed_ids - (kv_index * seq_size + seq_index) * table_rows

time: 111 us -> 110 us (level)
  waiting for transfers between devices: 21.5 us -> 19.5 us
    ppermute x31, waiting for transfers between devices: 21.5 us -> 19.5 us  [from_peers(): lax.ppermute(values[k - 1], axis, [(i, i ^ k) for i in range(size)])]
    pallas_call x3 -> x4, Pallas kernels: 18.7 us -> 18.8 us  [held_near(): pl.pallas_call(lambda *refs: hold_kernel(starts, *refs), out_shape=[pltpu...]
where the time goes in v3:
time: 110 us; the launch traced here: 109 us
  Pallas kernels  55.1 us (50%)
  starting transfers between devices  31.4 us (29%)
  waiting for transfers between devices  19.5 us (18%)
  local copies, waits for them, and re-layouts  2 us (2%)
    ppermute x31, starting transfers between devices, from_peers(): lax.ppermute(values[k - 1], axis, [(i, i ^ k) for i in range(size)])  31.4 us
    ppermute x31, waiting for transfers between devices, from_peers(): lax.ppermute(values[k - 1], axis, [(i, i ^ k) for i in range(size)])  19.5 us
    pallas_call x4, Pallas kernels, held_near(): pl.pallas_call(lambda *refs: hold_kernel(starts, *refs), out_shape=[pltpu...  18.8 us
    pallas_call x1, Pallas kernels, fast_layer(): pl.pallas_call(lambda *refs: table_kernel(seq_size, *refs), out_shape=(sh...  10.7 us
    pallas_call x1, Pallas kernels, fast_layer(): pl.pallas_call(attend_kernel, out_shape=(shape((count, attend_width), F32...  8.63 us
    pallas_call x1, Pallas kernels, fast_layer(): pl.pallas_call(lambda *refs: gate_up_kernel(seq_size, *refs), out_shape=(...  6.35 us
    pallas_call x1, Pallas kernels, fast_layer(): pl.pallas_call(lambda *refs: down_kernel(seq_size, *refs), out_shape=shap...  3.42 us
    pallas_call x1, Pallas kernels, fast_layer(): pl.pallas_call(project_kernel, out_shape=(shape((count, width), BF), shap...  2.55 us
  transfers between devices with their start and end apart: 31, of which 18 were waited for; matrix products, arithmetic and copies ran while one was open for 3% of the time, Pallas kernels for 17%

profile of v3, /device:TPU:0, one launch (start us, length us, event | category | flops | bytes accessed | tf_op | source)
XLA Modules:
  0.0 109.3 jit_solution(2714524325919125619)
XLA Ops:
  0.1 2.6 %project.3 = (bf16[16,576]{1,0:T(8,128)(2,1)S(1)}, f32[16,1152]{1,0:T(8,128)S(1)}, f32[16,1152]{1,0:T(8,128)S(1)}) custom-call(s32[3]{0:T(128)S(1)} %pad_add_fusion.meta.refs_0_, bf16[16,576]{1,0:T(8,128)(2,1)} %bitcast.9, f32[576]{0:T(1024)} %refs_1_.5, bf16[576,1024]{1,0:T(8,128)(2,1)} %refs_2_.4, bf16[576,512]{1,0:T(8,128)(2,1)} %refs_3_.4, ...), custom_call_target="tpu_custom_call" | custom-call | tf_op jit(solution)/shard_map/project/pallas_call | solution.py:801
  2.6 0.5 collective-permute-start
  3.2 0.7 convert_element_type.3
  4.2 4.9 %collective-permute-start.1 = (bf16[16,1152]{1,0:T(8,128)(2,1)S(1)}, bf16[16,1152]{1,0:T(8,128)(2,1)S(1)}, u32[]{:S(2)}, u32[]{:S(2)}) collective-permute-start(bf16[16,1152]{1,0:T(8,128)(2,1)S(1)} %get-tuple-element.38), channel_id=1, source_target_pairs={{0,3},{1,2},{2,1},{3,0},{4,7},{5,6},{6,5},{7,4},{8,11},{9,10},{10,... | collective-permute-start | bytes 110600 | tf_op jit(solution)/shard_map/project/ppermute | solution.py:725
  9.1 0.6 collective-permute-start.3
  9.8 1.3 %collective-permute-done.1.refs_3_ = bf16[16,1152]{1,0:T(8,128)(2,1)S(1)} collective-permute-done((bf16[16,1152]{1,0:T(8,128)(2,1)S(1)}, bf16[16,1152]{1,0:T(8,128)(2,1)S(1)}, u32[]{:S(2)}, u32[]{:S(2)}) %collective-permute-start.1) | collective-permute-done | bytes 36896 | tf_op jit(solution)/shard_map/project/ppermute | solution.py:725
  11.1 2.9 %collective-permute-done.2.refs_4_ = bf16[16,1152]{1,0:T(8,128)(2,1)S(1)} collective-permute-done((bf16[16,1152]{1,0:T(8,128)(2,1)S(1)}, bf16[16,1152]{1,0:T(8,128)(2,1)S(1)}, u32[]{:S(2)}, u32[]{:S(2)}) %collective-permute-start.2) | collective-permute-done | bytes 36896 | tf_op jit(solution)/shard_map/project/ppermute | solution.py:725
  14.3 0.8 reshape.28
  15.1 0.8 reshape.29
  15.9 8.6 %attend.5 = (f32[16,640]{1,0:T(8,128)S(1)}, f32[16,640]{1,0:T(8,128)S(1)}) custom-call(s32[35]{0:T(128)S(1)} %concatenate.14.meta, bf16[16,1024]{1,0:T(8,128)(2,1)S(1)} %get-tuple-element.39.mine, bf16[16,1024]{1,0:T(8,128)(2,1)S(1)} %collective-permute-done.4.other, bf16[8,1024,512]{2,1,0:T(8,128)(2,1)} %refs_0_.1, bf16[8,1024,512]{2,1,0:T(8,128)(2,1)} %refs_1_.6, ...), custom_call_target="tpu_custom_call" | custom-call | tf_op jit(solution)/shard_map/attend/pallas_call | solution.py:831
  24.6 0.6 collective-permute-start.5
  25.1 0.9 collective-permute-done.5.got
  26.1 1.7 %collective-permute-start.6 = (bf16[16,640]{1,0:T(8,128)(2,1)S(1)}, bf16[16,640]{1,0:T(8,128)(2,1)S(1)}, u32[]{:S(2)}, u32[]{:S(2)}) collective-permute-start(bf16[16,640]{1,0:T(8,128)(2,1)S(1)} %get-tuple-element.43), channel_id=1, source_target_pairs={{0,3},{1,2},{2,1},{3,0},{4,7},{5,6},{6,5},{7,4},{8,11},{9,10},{10,... | collective-permute-start | bytes 61448 | tf_op jit(solution)/shard_map/attend/ppermute | solution.py:725
  28.2 2.3 %collective-permute-start.8 = (bf16[16,640]{1,0:T(8,128)(2,1)S(1)}, bf16[16,640]{1,0:T(8,128)(2,1)S(1)}, u32[]{:S(2)}, u32[]{:S(2)}) collective-permute-start(bf16[16,640]{1,0:T(8,128)(2,1)S(1)} %get-tuple-element.43), channel_id=1, source_target_pairs={{0,1},{1,0},{2,3},{3,2},{4,5},{5,4},{6,7},{7,6},{8,9},{9,8},{10,11... | collective-permute-start | bytes 61448 | tf_op jit(solution)/shard_map/attend/ppermute | solution.py:725
  30.5 1.3 %collective-permute-done.6.refs_1_ = bf16[16,640]{1,0:T(8,128)(2,1)S(1)} collective-permute-done((bf16[16,640]{1,0:T(8,128)(2,1)S(1)}, bf16[16,640]{1,0:T(8,128)(2,1)S(1)}, u32[]{:S(2)}, u32[]{:S(2)}) %collective-permute-start.6) | collective-permute-done | bytes 20512 | tf_op jit(solution)/shard_map/attend/ppermute | solution.py:725
  31.8 0.7 collective-permute-done.7.refs_2_
  32.7 1.2 %collective-permute-done.9.other = bf16[16,512]{1,0:T(8,128)(2,1)S(1)} collective-permute-done((bf16[16,512]{1,0:T(8,128)(2,1)S(1)}, bf16[16,512]{1,0:T(8,128)(2,1)S(1)}, u32[]{:S(2)}, u32[]{:S(2)}) %collective-permute-start.9) | collective-permute-done | bytes 16416 | tf_op jit(solution)/shard_map/attend/ppermute | solution.py:725
  33.9 0.9 attend.8.refs_0_.refs_4_
  34.8 2.5 %collective-permute-start.10 = (f32[16,576]{1,0:T(8,128)S(1)}, f32[16,576]{1,0:T(8,128)S(1)}, u32[]{:S(2)}, u32[]{:S(2)}) collective-permute-start(f32[16,576]{1,0:T(8,128)S(1)} %attend.8.refs_0_.refs_4_), channel_id=1, source_target_pairs={{0,12},{4,8},{8,4},{12,0},{1,13},{5,9},{9,5},{13,1},{2,14},{6,10},... | collective-permute-start | bytes 110600 | tf_op jit(solution)/shard_map/attend/ppermute | solution.py:725
  37.4 0.5 collective-permute-start.11
  37.9 0.5 collective-permute-start.12
  38.3 4.0 %attend.9 = (bf16[576,6912]{1,0:T(8,128)(2,1)S(1)}, f32[8,128]{1,0:T(8,128)}) custom-call(f32[16,576]{1,0:T(8,128)S(1)} %attend.8.refs_0_.refs_4_, bf16[576,9216]{1,0:T(8,128)(2,1)} %refs_9_.1), custom_call_target="tpu_custom_call" | custom-call | bytes 15925248 | tf_op jit(solution)/shard_map/attend/pallas_call | solution.py:336
  42.3 6.3 %gate_up.4 = (f32[4,32,2432]{2,1,0:T(8,128)S(1)}, bf16[4,32,2432]{2,1,0:T(8,128)(2,1)S(1)}, f32[16,576]{1,0:T(8,128)S(1)}) custom-call(s32[3]{0:T(128)S(1)} %pad_add_fusion.meta.refs_0_, bf16[16,576]{1,0:T(8,128)(2,1)S(1)} %get-tuple-element.34.refs_1_.refs_0_, f32[576]{0:T(1024)S(1)} %copy-done.1, f32[576]{0:T(1024)S(1)} %copy-done.2, ...), custom_call_target="tpu_custom_call" | custom-call | tf_op jit(solution)/shard_map/gate_up/pallas_call | solution.py:872
  48.8 2.0 %collective-permute-done.13.got = bf16[4,32,2432]{2,1,0:T(8,128)(2,1)S(1)} collective-permute-done((bf16[4,32,2432]{2,1,0:T(8,128)(2,1)S(1)}, bf16[4,32,2432]{2,1,0:T(8,128)(2,1)S(1)}, u32[]{:S(2)}, u32[]{:S(2)}) %collective-permute-start.13) | collective-permute-done | bytes 622624 | tf_op jit(solution)/shard_map/gate_up/ppermute | solution.py:725
  51.0 2.1 %collective-permute-start.14 = (bf16[32,2432]{1,0:T(8,128)(2,1)S(1)}, bf16[32,2432]{1,0:T(8,128)(2,1)S(1)}, u32[]{:S(2)}, u32[]{:S(2)}) collective-permute-start(bf16[32,2432]{1,0:T(8,128)(2,1)S(1)} %get-tuple-element.51), channel_id=1, source_target_pairs={{0,2},{1,3},{2,0},{3,1},{4,6},{5,7},{6,4},{7,5},{8,10},{9,11},{10,... | collective-permute-start | bytes 466952 | tf_op jit(solution)/shard_map/gate_up/ppermute | solution.py:725
  53.1 2.2 %collective-permute-start.15 = (bf16[32,2432]{1,0:T(8,128)(2,1)S(1)}, bf16[32,2432]{1,0:T(8,128)(2,1)S(1)}, u32[]{:S(2)}, u32[]{:S(2)}) collective-permute-start(bf16[32,2432]{1,0:T(8,128)(2,1)S(1)} %get-tuple-element.52), channel_id=1, source_target_pairs={{0,3},{1,2},{2,1},{3,0},{4,7},{5,6},{6,5},{7,4},{8,11},{9,10},{10,... | collective-permute-start | bytes 466952 | tf_op jit(solution)/shard_map/gate_up/ppermute | solution.py:725
  55.3 9.5 %gate_up.6 = (bf16[576,9216]{1,0:T(8,128)(2,1)S(1)}, bf16[4096,2304]{1,0:T(8,128)(2,1)S(1)}, f32[8,128]{1,0:T(8,128)S(1)}) custom-call(bf16[32,2432]{1,0:T(8,128)(2,1)S(1)} %get-tuple-element.47.refs_0_, bf16[576,9216]{1,0:T(8,128)(2,1)} %bitcast.8, bf16[8192,2304]{1,0:T(8,128)(2,1)} %refs_8_.1), custom_call_target="tpu_custom_call" | custom-call | bytes 58982400 | tf_op jit(solution)/shard_map/gate_up/pallas_call | solution.py:336
  64.8 0.8 collective-permute-done.14.refs_2_
  65.6 0.5 collective-permute-done.16.refs_4_
  66.5 2.4 %collective-permute-start.17 = (bf16[16,1152]{1,0:T(8,128)(2,1)S(1)}, bf16[16,1152]{1,0:T(8,128)(2,1)S(1)}, u32[]{:S(2)}, u32[]{:S(2)}) collective-permute-start(bf16[16,1152]{1,0:T(8,128)(2,1)S(1)} %get-tuple-element.53.refs_1_), channel_id=1, source_target_pairs={{0,3},{1,2},{2,1},{3,0},{4,7},{5,6},{6,5},{7,4},{8,11},{9,10},{10,... | collective-permute-start | bytes 110600 | tf_op jit(solution)/shard_map/down/ppermute | solution.py:725
  68.9 1.7 %collective-permute-start.18 = (bf16[16,1152]{1,0:T(8,128)(2,1)S(1)}, bf16[16,1152]{1,0:T(8,128)(2,1)S(1)}, u32[]{:S(2)}, u32[]{:S(2)}) collective-permute-start(bf16[16,1152]{1,0:T(8,128)(2,1)S(1)} %get-tuple-element.53.refs_1_), channel_id=1, source_target_pairs={{0,2},{1,3},{2,0},{3,1},{4,6},{5,7},{6,4},{7,5},{8,10},{9,11},{10,... | collective-permute-start | bytes 110600 | tf_op jit(solution)/shard_map/down/ppermute | solution.py:725
  71.0 1.4 %collective-permute-done.17.refs_2_ = bf16[16,1152]{1,0:T(8,128)(2,1)S(1)} collective-permute-done((bf16[16,1152]{1,0:T(8,128)(2,1)S(1)}, bf16[16,1152]{1,0:T(8,128)(2,1)S(1)}, u32[]{:S(2)}, u32[]{:S(2)}) %collective-permute-start.17) | collective-permute-done | bytes 36896 | tf_op jit(solution)/shard_map/down/ppermute | solution.py:725
  72.4 1.4 %collective-permute-done.18.refs_3_ = bf16[16,1152]{1,0:T(8,128)(2,1)S(1)} collective-permute-done((bf16[16,1152]{1,0:T(8,128)(2,1)S(1)}, bf16[16,1152]{1,0:T(8,128)(2,1)S(1)}, u32[]{:S(2)}, u32[]{:S(2)}) %collective-permute-start.18) | collective-permute-done | bytes 36896 | tf_op jit(solution)/shard_map/down/ppermute | solution.py:725
  73.8 0.8 collective-permute-done.19.refs_4_
  75.0 0.8 collective-permute-done.23.refs_8_
  75.8 3.4 %down.2.refs_0_.refs_5_ = f32[16,576]{1,0:T(8,128)S(1)} custom-call(s32[3]{0:T(128)S(1)} %pad_add_fusion.meta.refs_0_, bf16[16,1152]{1,0:T(8,128)(2,1)S(1)} %get-tuple-element.53.refs_1_, bf16[16,1152]{1,0:T(8,128)(2,1)S(1)} %collective-permute-done.17.refs_2_, bf16[16,1152]{1,0:T(8,128)(2,1)S(1)} %collective-permute-done.18.refs_3_, ...), custom_call_target="tpu_custom_call" | custom-call | tf_op jit(solution)/shard_map/down/pallas_call | solution.py:914
  79.2 2.6 %collective-permute-start.24 = (f32[16,576]{1,0:T(8,128)S(1)}, f32[16,576]{1,0:T(8,128)S(1)}, u32[]{:S(2)}, u32[]{:S(2)}) collective-permute-start(f32[16,576]{1,0:T(8,128)S(1)} %down.2.refs_0_.refs_5_), channel_id=1, source_target_pairs={{0,12},{4,8},{8,4},{12,0},{1,13},{5,9},{9,5},{13,1},{2,14},{6,10},... | collective-permute-start | bytes 110600 | tf_op jit(solution)/shard_map/down/ppermute | solution.py:725
  81.8 0.5 collective-permute-start.25
  82.3 0.5 collective-permute-start.26
  82.7 2.4 %down.3 = (bf16[1024,2304]{1,0:T(8,128)(2,1)S(1)}, f32[8,128]{1,0:T(8,128)S(1)}) custom-call(f32[16,576]{1,0:T(8,128)S(1)} %down.2.refs_0_.refs_5_, bf16[8192,2304]{1,0:T(8,128)(2,1)} %refs_8_.1), custom_call_target="tpu_custom_call" | custom-call | bytes 9437184 | tf_op jit(solution)/shard_map/down/pallas_call | solution.py:336
  85.1 0.7 collective-permute-done.25.refs_7_
  85.8 0.5 collective-permute-done.26.refs_8_
  86.5 2.3 %collective-permute-start.27 = (bf16[48,576]{1,0:T(8,128)(2,1)S(1)}, bf16[48,576]{1,0:T(8,128)(2,1)S(1)}, u32[]{:S(2)}, u32[]{:S(2)}) collective-permute-start(bf16[48,576]{1,0:T(8,128)(2,1)S(1)} %head.4.refs_0_.refs_1_), channel_id=1, source_target_pairs={{0,3},{1,2},{2,1},{3,0},{4,7},{5,6},{6,5},{7,4},{8,11},{9,10},{10,... | collective-permute-start | bytes 165896 | tf_op jit(solution)/shard_map/head/ppermute | solution.py:725
  89.0 1.9 %collective-permute-start.29 = (bf16[48,576]{1,0:T(8,128)(2,1)S(1)}, bf16[48,576]{1,0:T(8,128)(2,1)S(1)}, u32[]{:S(2)}, u32[]{:S(2)}) collective-permute-start(bf16[48,576]{1,0:T(8,128)(2,1)S(1)} %head.4.refs_0_.refs_1_), channel_id=1, source_target_pairs={{0,1},{1,0},{2,3},{3,2},{4,5},{5,4},{6,7},{7,6},{8,9},{9,8},{10,11... | collective-permute-start | bytes 165896 | tf_op jit(solution)/shard_map/head/ppermute | solution.py:725
  90.9 3.0 %head.5 = (bf16[1024,2304]{1,0:T(8,128)(2,1)S(1)}, f32[8,128]{1,0:T(8,128)}) custom-call(bf16[48,576]{1,0:T(8,128)(2,1)S(1)} %head.4.refs_0_.refs_1_, bf16[8192,2304]{1,0:T(8,128)(2,1)} %refs_8_.1), custom_call_target="tpu_custom_call" | custom-call | bytes 9437184 | tf_op jit(solution)/shard_map/head/pallas_call | solution.py:336
  94.3 10.7 %head.6 = (f32[16,8320]{1,0:T(8,128)S(1)}, f32[16,8320]{1,0:T(8,128)S(1)}) custom-call(s32[3]{0:T(128)S(1)} %pad_add_fusion.meta.refs_0_, bf16[48,576]{1,0:T(8,128)(2,1)S(1)} %head.4.refs_0_.refs_1_, bf16[48,576]{1,0:T(8,128)(2,1)S(1)} %collective-permute-done.27.refs_2_, bf16[48,576]{1,0:T(8,128)(2,1)S(1)} %collective-permute-done.28.refs_3_, ...), custom_call_target="tpu_custom_call" | custom-call | tf_op jit(solution)/shard_map/head/pallas_call | solution.py:935
  105.4 1.6 %collective-permute-done.30.got = f32[16,8320]{1,0:T(8,128)S(1)} collective-permute-done((f32[16,8320]{1,0:T(8,128)S(1)}, f32[16,8320]{1,0:T(8,128)S(1)}, u32[]{:S(2)}, u32[]{:S(2)}) %collective-permute-start.30) | collective-permute-done | bytes 532512 | tf_op jit(solution)/shard_map/head/ppermute | solution.py:725
  107.1 2.2 %head.7 = f32[4,4096]{1,0:T(4,128)} custom-call(s32[8,2048]{1,0:T(8,128)S(1)} %reshape.26.places, f32[8,128]{1,0:T(8,128)S(1)} %broadcast_in_dim.5.weights, f32[16,8320]{1,0:T(8,128)S(1)} %get-tuple-element.61.keep, f32[16,8320]{1,0:T(8,128)S(1)} %collective-permute-done.30.got), custom_call_target="tpu_custom_call" | custom-call | tf_op jit(solution)/shard_map/head/pallas_call | solution.py:953
  (64 shorter events, 4.4 us)
Async XLA Ops:
  2.6 1.5 %collective-permute-start = (f32[16,1152]{1,0:T(8,128)S(1)}, f32[16,1152]{1,0:T(8,128)S(1)}, u32[]{:S(2)}, u32[]{:S(2)}) collective-permute-start(f32[16,1152]{1,0:T(8,128)S(1)} %get-tuple-element.36), channel_id=1, source_target_pairs={{0,16},{16,0},{1,17},{17,1},{2,18},{18,2},{3,19},{19,3},{4,20},{20... | collective-permute-start | bytes 221192 | tf_op jit(solution)/shard_map/project/ppermute | solution.py:725
  4.2 6.9 %collective-permute-start.1 = (bf16[16,1152]{1,0:T(8,128)(2,1)S(1)}, bf16[16,1152]{1,0:T(8,128)(2,1)S(1)}, u32[]{:S(2)}, u32[]{:S(2)}) collective-permute-start(bf16[16,1152]{1,0:T(8,128)(2,1)S(1)} %get-tuple-element.38), channel_id=1, source_target_pairs={{0,3},{1,2},{2,1},{3,0},{4,7},{5,6},{6,5},{7,4},{8,11},{9,10},{10,... | collective-permute-start | bytes 110600 | tf_op jit(solution)/shard_map/project/ppermute | solution.py:725
  9.1 4.9 %collective-permute-start.2 = (bf16[16,1152]{1,0:T(8,128)(2,1)S(1)}, bf16[16,1152]{1,0:T(8,128)(2,1)S(1)}, u32[]{:S(2)}, u32[]{:S(2)}) collective-permute-start(bf16[16,1152]{1,0:T(8,128)(2,1)S(1)} %get-tuple-element.38), channel_id=1, source_target_pairs={{0,2},{1,3},{2,0},{3,1},{4,6},{5,7},{6,4},{7,5},{8,10},{9,11},{10,... | collective-permute-start | bytes 110600 | tf_op jit(solution)/shard_map/project/ppermute | solution.py:725
  9.1 4.9 %collective-permute-start.3 = (bf16[16,1152]{1,0:T(8,128)(2,1)S(1)}, bf16[16,1152]{1,0:T(8,128)(2,1)S(1)}, u32[]{:S(2)}, u32[]{:S(2)}) collective-permute-start(bf16[16,1152]{1,0:T(8,128)(2,1)S(1)} %get-tuple-element.38), channel_id=1, source_target_pairs={{0,1},{1,0},{2,3},{3,2},{4,5},{5,4},{6,7},{7,6},{8,9},{9,8},{10,11... | collective-permute-start | bytes 110600 | tf_op jit(solution)/shard_map/project/ppermute | solution.py:725
  14.2 1.7 %collective-permute-start.4 = (bf16[16,1024]{1,0:T(8,128)(2,1)S(1)}, bf16[16,1024]{1,0:T(8,128)(2,1)S(1)}, u32[]{:S(2)}, u32[]{:S(2)}) collective-permute-start(bf16[16,1024]{1,0:T(8,128)(2,1)S(1)} %get-tuple-element.39.mine), channel_id=1, source_target_pairs={{0,16},{16,0},{1,17},{17,1},{2,18},{18,2},{3,19},{19,3},{4,20},{20... | collective-permute-start | bytes 98312 | tf_op jit(solution)/shard_map/project/ppermute | solution.py:725
  15.9 18.0 %copy-start = (bf16[1024,576]{0,1:T(8,128)(2,1)S(1)}, bf16[1024,576]{0,1:T(8,128)(2,1)}, u32[]{:S(2)}) copy-start(bf16[1024,576]{0,1:T(8,128)(2,1)} %param.35) | copy-start | bytes 3538948
  24.5 17.8 %copy-start.1 = (f32[576]{0:T(1024)S(1)}, f32[576]{0:T(1024)}, u32[]{:S(2)}) copy-start(f32[576]{0:T(1024)} %refs_2_.6) | copy-start | bytes 6916
  24.6 17.8 %copy-start.2 = (f32[576]{0:T(1024)S(1)}, f32[576]{0:T(1024)}, u32[]{:S(2)}) copy-start(f32[576]{0:T(1024)} %refs_3_.6) | copy-start | bytes 6916
  24.6 1.4 %collective-permute-start.5 = (f32[16,640]{1,0:T(8,128)S(1)}, f32[16,640]{1,0:T(8,128)S(1)}, u32[]{:S(2)}, u32[]{:S(2)}) collective-permute-start(f32[16,640]{1,0:T(8,128)S(1)} %get-tuple-element.41), channel_id=1, source_target_pairs={{0,16},{16,0},{1,17},{17,1},{2,18},{18,2},{3,19},{19,3},{4,20},{20... | collective-permute-start | bytes 122888 | tf_op jit(solution)/shard_map/attend/ppermute | solution.py:725
  26.1 5.7 %collective-permute-start.6 = (bf16[16,640]{1,0:T(8,128)(2,1)S(1)}, bf16[16,640]{1,0:T(8,128)(2,1)S(1)}, u32[]{:S(2)}, u32[]{:S(2)}) collective-permute-start(bf16[16,640]{1,0:T(8,128)(2,1)S(1)} %get-tuple-element.43), channel_id=1, source_target_pairs={{0,3},{1,2},{2,1},{3,0},{4,7},{5,6},{6,5},{7,4},{8,11},{9,10},{10,... | collective-permute-start | bytes 61448 | tf_op jit(solution)/shard_map/attend/ppermute | solution.py:725
  27.7 4.7 %collective-permute-start.7 = (bf16[16,640]{1,0:T(8,128)(2,1)S(1)}, bf16[16,640]{1,0:T(8,128)(2,1)S(1)}, u32[]{:S(2)}, u32[]{:S(2)}) collective-permute-start(bf16[16,640]{1,0:T(8,128)(2,1)S(1)} %get-tuple-element.43), channel_id=1, source_target_pairs={{0,2},{1,3},{2,0},{3,1},{4,6},{5,7},{6,4},{7,5},{8,10},{9,11},{10,... | collective-permute-start | bytes 61448 | tf_op jit(solution)/shard_map/attend/ppermute | solution.py:725
  28.2 4.3 %collective-permute-start.8 = (bf16[16,640]{1,0:T(8,128)(2,1)S(1)}, bf16[16,640]{1,0:T(8,128)(2,1)S(1)}, u32[]{:S(2)}, u32[]{:S(2)}) collective-permute-start(bf16[16,640]{1,0:T(8,128)(2,1)S(1)} %get-tuple-element.43), channel_id=1, source_target_pairs={{0,1},{1,0},{2,3},{3,2},{4,5},{5,4},{6,7},{7,6},{8,9},{9,8},{10,11... | collective-permute-start | bytes 61448 | tf_op jit(solution)/shard_map/attend/ppermute | solution.py:725
  32.6 1.2 %collective-permute-start.9 = (bf16[16,512]{1,0:T(8,128)(2,1)S(1)}, bf16[16,512]{1,0:T(8,128)(2,1)S(1)}, u32[]{:S(2)}, u32[]{:S(2)}) collective-permute-start(bf16[16,512]{1,0:T(8,128)(2,1)S(1)} %attend.7.mine), channel_id=1, source_target_pairs={{0,16},{16,0},{1,17},{17,1},{2,18},{18,2},{3,19},{19,3},{4,20},{20... | collective-permute-start | bytes 49160 | tf_op jit(solution)/shard_map/attend/ppermute | solution.py:725
  34.8 7.5 %collective-permute-start.10 = (f32[16,576]{1,0:T(8,128)S(1)}, f32[16,576]{1,0:T(8,128)S(1)}, u32[]{:S(2)}, u32[]{:S(2)}) collective-permute-start(f32[16,576]{1,0:T(8,128)S(1)} %attend.8.refs_0_.refs_4_), channel_id=1, source_target_pairs={{0,12},{4,8},{8,4},{12,0},{1,13},{5,9},{9,5},{13,1},{2,14},{6,10},... | collective-permute-start | bytes 110600 | tf_op jit(solution)/shard_map/attend/ppermute | solution.py:725
  37.4 4.9 %collective-permute-start.11 = (f32[16,576]{1,0:T(8,128)S(1)}, f32[16,576]{1,0:T(8,128)S(1)}, u32[]{:S(2)}, u32[]{:S(2)}) collective-permute-start(f32[16,576]{1,0:T(8,128)S(1)} %attend.8.refs_0_.refs_4_), channel_id=1, source_target_pairs={{0,8},{4,12},{8,0},{12,4},{1,9},{5,13},{9,1},{13,5},{2,10},{6,14},... | collective-permute-start | bytes 110600 | tf_op jit(solution)/shard_map/attend/ppermute | solution.py:725
  37.9 4.5 %collective-permute-start.12 = (f32[16,576]{1,0:T(8,128)S(1)}, f32[16,576]{1,0:T(8,128)S(1)}, u32[]{:S(2)}, u32[]{:S(2)}) collective-permute-start(f32[16,576]{1,0:T(8,128)S(1)} %attend.8.refs_0_.refs_4_), channel_id=1, source_target_pairs={{0,4},{4,0},{8,12},{12,8},{1,5},{5,1},{9,13},{13,9},{2,6},{6,2},{1... | collective-permute-start | bytes 110600 | tf_op jit(solution)/shard_map/attend/ppermute | solution.py:725
  48.7 2.1 %collective-permute-start.13 = (bf16[4,32,2432]{2,1,0:T(8,128)(2,1)S(1)}, bf16[4,32,2432]{2,1,0:T(8,128)(2,1)S(1)}, u32[]{:S(2)}, u32[]{:S(2)}) collective-permute-start(bf16[4,32,2432]{2,1,0:T(8,128)(2,1)S(1)} %get-tuple-element.46), channel_id=1, source_target_pairs={{0,16},{16,0},{1,17},{17,1},{2,18},{18,2},{3,19},{19,3},{4,20},{20... | collective-permute-start | bytes 1867784 | tf_op jit(solution)/shard_map/gate_up/ppermute | solution.py:725
  51.0 14.5 %collective-permute-start.14 = (bf16[32,2432]{1,0:T(8,128)(2,1)S(1)}, bf16[32,2432]{1,0:T(8,128)(2,1)S(1)}, u32[]{:S(2)}, u32[]{:S(2)}) collective-permute-start(bf16[32,2432]{1,0:T(8,128)(2,1)S(1)} %get-tuple-element.51), channel_id=1, source_target_pairs={{0,2},{1,3},{2,0},{3,1},{4,6},{5,7},{6,4},{7,5},{8,10},{9,11},{10,... | collective-permute-start | bytes 466952 | tf_op jit(solution)/shard_map/gate_up/ppermute | solution.py:725
  53.1 12.5 %collective-permute-start.15 = (bf16[32,2432]{1,0:T(8,128)(2,1)S(1)}, bf16[32,2432]{1,0:T(8,128)(2,1)S(1)}, u32[]{:S(2)}, u32[]{:S(2)}) collective-permute-start(bf16[32,2432]{1,0:T(8,128)(2,1)S(1)} %get-tuple-element.52), channel_id=1, source_target_pairs={{0,3},{1,2},{2,1},{3,0},{4,7},{5,6},{6,5},{7,4},{8,11},{9,10},{10,... | collective-permute-start | bytes 466952 | tf_op jit(solution)/shard_map/gate_up/ppermute | solution.py:725
  55.3 10.8 %collective-permute-start.16 = (bf16[32,2432]{1,0:T(8,128)(2,1)S(1)}, bf16[32,2432]{1,0:T(8,128)(2,1)S(1)}, u32[]{:S(2)}, u32[]{:S(2)}) collective-permute-start(bf16[32,2432]{1,0:T(8,128)(2,1)S(1)} %get-tuple-element.47.refs_0_), channel_id=1, source_target_pairs={{0,1},{1,0},{2,3},{3,2},{4,5},{5,4},{6,7},{7,6},{8,9},{9,8},{10,11... | collective-permute-start | bytes 466952 | tf_op jit(solution)/shard_map/gate_up/ppermute | solution.py:725
  66.5 5.9 %collective-permute-start.17 = (bf16[16,1152]{1,0:T(8,128)(2,1)S(1)}, bf16[16,1152]{1,0:T(8,128)(2,1)S(1)}, u32[]{:S(2)}, u32[]{:S(2)}) collective-permute-start(bf16[16,1152]{1,0:T(8,128)(2,1)S(1)} %get-tuple-element.53.refs_1_), channel_id=1, source_target_pairs={{0,3},{1,2},{2,1},{3,0},{4,7},{5,6},{6,5},{7,4},{8,11},{9,10},{10,... | collective-permute-start | bytes 110600 | tf_op jit(solution)/shard_map/down/ppermute | solution.py:725
  68.9 4.9 %collective-permute-start.18 = (bf16[16,1152]{1,0:T(8,128)(2,1)S(1)}, bf16[16,1152]{1,0:T(8,128)(2,1)S(1)}, u32[]{:S(2)}, u32[]{:S(2)}) collective-permute-start(bf16[16,1152]{1,0:T(8,128)(2,1)S(1)} %get-tuple-element.53.refs_1_), channel_id=1, source_target_pairs={{0,2},{1,3},{2,0},{3,1},{4,6},{5,7},{6,4},{7,5},{8,10},{9,11},{10,... | collective-permute-start | bytes 110600 | tf_op jit(solution)/shard_map/down/ppermute | solution.py:725
  70.6 4.0 %collective-permute-start.19 = (bf16[16,1152]{1,0:T(8,128)(2,1)S(1)}, bf16[16,1152]{1,0:T(8,128)(2,1)S(1)}, u32[]{:S(2)}, u32[]{:S(2)}) collective-permute-start(bf16[16,1152]{1,0:T(8,128)(2,1)S(1)} %get-tuple-element.53.refs_1_), channel_id=1, source_target_pairs={{0,1},{1,0},{2,3},{3,2},{4,5},{5,4},{6,7},{7,6},{8,9},{9,8},{10,11... | collective-permute-start | bytes 110600 | tf_op jit(solution)/shard_map/down/ppermute | solution.py:725
  71.0 3.6 %collective-permute-start.20 = (bf16[16,1152]{1,0:T(8,128)(2,1)S(1)}, bf16[16,1152]{1,0:T(8,128)(2,1)S(1)}, u32[]{:S(2)}, u32[]{:S(2)}) collective-permute-start(bf16[16,1152]{1,0:T(8,128)(2,1)S(1)} %get-tuple-element.53.refs_1_), channel_id=1, source_target_pairs={{0,16},{16,0},{1,17},{17,1},{2,18},{18,2},{3,19},{19,3},{4,20},{20... | collective-permute-start | bytes 110600 | tf_op jit(solution)/shard_map/down/ppermute | solution.py:725
  72.4 2.2 %collective-permute-start.21 = (bf16[16,1152]{1,0:T(8,128)(2,1)S(1)}, bf16[16,1152]{1,0:T(8,128)(2,1)S(1)}, u32[]{:S(2)}, u32[]{:S(2)}) collective-permute-start(bf16[16,1152]{1,0:T(8,128)(2,1)S(1)} %collective-permute-done.17.refs_2_), channel_id=1, source_target_pairs={{0,16},{16,0},{1,17},{17,1},{2,18},{18,2},{3,19},{19,3},{4,20},{20... | collective-permute-start | bytes 110600 | tf_op jit(solution)/shard_map/down/ppermute | solution.py:725
  73.8 1.2 %collective-permute-start.22 = (bf16[16,1152]{1,0:T(8,128)(2,1)S(1)}, bf16[16,1152]{1,0:T(8,128)(2,1)S(1)}, u32[]{:S(2)}, u32[]{:S(2)}) collective-permute-start(bf16[16,1152]{1,0:T(8,128)(2,1)S(1)} %collective-permute-done.18.refs_3_), channel_id=1, source_target_pairs={{0,16},{16,0},{1,17},{17,1},{2,18},{18,2},{3,19},{19,3},{4,20},{20... | collective-permute-start | bytes 110600 | tf_op jit(solution)/shard_map/down/ppermute | solution.py:725
  74.6 1.2 %collective-permute-start.23 = (bf16[16,1152]{1,0:T(8,128)(2,1)S(1)}, bf16[16,1152]{1,0:T(8,128)(2,1)S(1)}, u32[]{:S(2)}, u32[]{:S(2)}) collective-permute-start(bf16[16,1152]{1,0:T(8,128)(2,1)S(1)} %collective-permute-done.19.refs_4_), channel_id=1, source_target_pairs={{0,16},{16,0},{1,17},{17,1},{2,18},{18,2},{3,19},{19,3},{4,20},{20... | collective-permute-start | bytes 110600 | tf_op jit(solution)/shard_map/down/ppermute | solution.py:725
  79.2 7.1 %copy-start.3 = (f32[576]{0:T(1024)S(1)}, f32[576]{0:T(1024)}, u32[]{:S(2)}) copy-start(f32[576]{0:T(1024)} %refs_3_.7) | copy-start | bytes 6916
  79.2 7.1 %copy-start.4 = (f32[576]{0:T(1024)S(1)}, f32[576]{0:T(1024)}, u32[]{:S(2)}) copy-start(f32[576]{0:T(1024)} %refs_4_.3) | copy-start | bytes 6916
  79.2 5.9 %collective-permute-start.24 = (f32[16,576]{1,0:T(8,128)S(1)}, f32[16,576]{1,0:T(8,128)S(1)}, u32[]{:S(2)}, u32[]{:S(2)}) collective-permute-start(f32[16,576]{1,0:T(8,128)S(1)} %down.2.refs_0_.refs_5_), channel_id=1, source_target_pairs={{0,12},{4,8},{8,4},{12,0},{1,13},{5,9},{9,5},{13,1},{2,14},{6,10},... | collective-permute-start | bytes 110600 | tf_op jit(solution)/shard_map/down/ppermute | solution.py:725
  81.8 4.0 %collective-permute-start.25 = (f32[16,576]{1,0:T(8,128)S(1)}, f32[16,576]{1,0:T(8,128)S(1)}, u32[]{:S(2)}, u32[]{:S(2)}) collective-permute-start(f32[16,576]{1,0:T(8,128)S(1)} %down.2.refs_0_.refs_5_), channel_id=1, source_target_pairs={{0,8},{4,12},{8,0},{12,4},{1,9},{5,13},{9,1},{13,5},{2,10},{6,14},... | collective-permute-start | bytes 110600 | tf_op jit(solution)/shard_map/down/ppermute | solution.py:725
  82.3 4.0 %collective-permute-start.26 = (f32[16,576]{1,0:T(8,128)S(1)}, f32[16,576]{1,0:T(8,128)S(1)}, u32[]{:S(2)}, u32[]{:S(2)}) collective-permute-start(f32[16,576]{1,0:T(8,128)S(1)} %down.2.refs_0_.refs_5_), channel_id=1, source_target_pairs={{0,4},{4,0},{8,12},{12,8},{1,5},{5,1},{9,13},{13,9},{2,6},{6,2},{1... | collective-permute-start | bytes 110600 | tf_op jit(solution)/shard_map/down/ppermute | solution.py:725
  86.5 7.4 %collective-permute-start.27 = (bf16[48,576]{1,0:T(8,128)(2,1)S(1)}, bf16[48,576]{1,0:T(8,128)(2,1)S(1)}, u32[]{:S(2)}, u32[]{:S(2)}) collective-permute-start(bf16[48,576]{1,0:T(8,128)(2,1)S(1)} %head.4.refs_0_.refs_1_), channel_id=1, source_target_pairs={{0,3},{1,2},{2,1},{3,0},{4,7},{5,6},{6,5},{7,4},{8,11},{9,10},{10,... | collective-permute-start | bytes 165896 | tf_op jit(solution)/shard_map/head/ppermute | solution.py:725
  88.8 5.5 %collective-permute-start.28 = (bf16[48,576]{1,0:T(8,128)(2,1)S(1)}, bf16[48,576]{1,0:T(8,128)(2,1)S(1)}, u32[]{:S(2)}, u32[]{:S(2)}) collective-permute-start(bf16[48,576]{1,0:T(8,128)(2,1)S(1)} %head.4.refs_0_.refs_1_), channel_id=1, source_target_pairs={{0,2},{1,3},{2,0},{3,1},{4,6},{5,7},{6,4},{7,5},{8,10},{9,11},{10,... | collective-permute-start | bytes 165896 | tf_op jit(solution)/shard_map/head/ppermute | solution.py:725
  89.0 5.3 %collective-permute-start.29 = (bf16[48,576]{1,0:T(8,128)(2,1)S(1)}, bf16[48,576]{1,0:T(8,128)(2,1)S(1)}, u32[]{:S(2)}, u32[]{:S(2)}) collective-permute-start(bf16[48,576]{1,0:T(8,128)(2,1)S(1)} %head.4.refs_0_.refs_1_), channel_id=1, source_target_pairs={{0,1},{1,0},{2,3},{3,2},{4,5},{5,4},{6,7},{7,6},{8,9},{9,8},{10,11... | collective-permute-start | bytes 165896 | tf_op jit(solution)/shard_map/head/ppermute | solution.py:725
  94.3 10.8 %copy-start.5 = (s32[4096]{0:T(1024)S(1)}, s32[4096]{0:T(1024)}, u32[]{:S(2)}) copy-start(s32[4096]{0:T(1024)} %param.25) | copy-start | bytes 49156
  94.3 10.9 %copy-start.6 = (f32[8]{0:T(128)S(1)}, f32[8]{0:T(128)}, u32[]{:S(2)}) copy-start(f32[8]{0:T(128)} %param.26) | copy-start | bytes 100
  105.0 2.0 %collective-permute-start.30 = (f32[16,8320]{1,0:T(8,128)S(1)}, f32[16,8320]{1,0:T(8,128)S(1)}, u32[]{:S(2)}, u32[]{:S(2)}) collective-permute-start(f32[16,8320]{1,0:T(8,128)S(1)} %get-tuple-element.62), channel_id=1, source_target_pairs={{0,16},{16,0},{1,17},{17,1},{2,18},{18,2},{3,19},{19,3},{4,20},{20... | collective-permute-start | bytes 1597448 | tf_op jit(solution)/shard_map/head/ppermute | solution.py:725

commit v4 on v3

--- a/solution.py
+++ b/solution.py
@@ -860,8 +860,10 @@
             compiler_params=limit(16),
         )(place, mine, other, output_weight.T)
         parts = [part] + from_peers(part, "kv", kv_size)
+        steps = 2 * seq_size
+        near_steps = 5 * steps // 8
         near_gate, _ = held_near(
-            part, (gate_weight, 0, width), columns=3 * gate_weight.shape[1] // 4
+            part, (gate_weight, 0, width), columns=near_steps * (gate_weight.shape[1] // steps)
         )
 
     with jax.named_scope("gate_up"):
@@ -879,8 +881,8 @@
             in_specs=[SMEM] + [VMEM] * (4 + kv_size) + [ANY] * 2,
             out_specs=(VMEM,) * 3,
             scratch_shapes=[
-                pltpu.VMEM((steps * 5 // 4, width, unit_block), BF),
-                pltpu.SemaphoreType.DMA((steps * 5 // 4,)),
+                pltpu.VMEM((2 * steps - near_steps, width, unit_block), BF),
+                pltpu.SemaphoreType.DMA((2 * steps - near_steps,)),
             ],
             compiler_params=limit(18),
         )(place, rows, post_attn_gain, pre_ffw_gain, *parts, near_gate, in_hbm(gate_weight), in_hbm(up_weight))

time: 110 us -> 109 us (level)
  no operation moved by 1% of the time
where the time goes in v4:
time: 109 us
  Pallas kernels  55 us (50%)
  starting transfers between devices  31.4 us (29%)
  waiting for transfers between devices  19.5 us (18%)
  local copies, waits for them, and re-layouts  2 us (2%)
    ppermute x31, starting transfers between devices, from_peers(): lax.ppermute(values[k - 1], axis, [(i, i ^ k) for i in range(size)])  31.4 us
    ppermute x31, waiting for transfers between devices, from_peers(): lax.ppermute(values[k - 1], axis, [(i, i ^ k) for i in range(size)])  19.5 us
    pallas_call x4, Pallas kernels, held_near(): pl.pallas_call(lambda *refs: hold_kernel(starts, *refs), out_shape=[pltpu...  18.4 us
    pallas_call x1, Pallas kernels, fast_layer(): pl.pallas_call(lambda *refs: table_kernel(seq_size, *refs), out_shape=(sh...  10.7 us
    pallas_call x1, Pallas kernels, fast_layer(): pl.pallas_call(attend_kernel, out_shape=(shape((count, attend_width), F32...  8.63 us
    pallas_call x1, Pallas kernels, fast_layer(): pl.pallas_call(lambda *refs: gate_up_kernel(seq_size, *refs), out_shape=(...  6.69 us
    pallas_call x1, Pallas kernels, fast_layer(): pl.pallas_call(lambda *refs: down_kernel(seq_size, *refs), out_shape=shap...  3.42 us
    pallas_call x1, Pallas kernels, fast_layer(): pl.pallas_call(project_kernel, out_shape=(shape((count, width), BF), shap...  2.55 us
  transfers between devices with their start and end apart: 31, of which 18 were waited for; matrix products, arithmetic and copies ran while one was open for 3% of the time, Pallas kernels for 17%

profile of v4, /device:TPU:0, one launch (start us, length us, event | category | flops | bytes accessed | tf_op | source)
XLA Modules:
  0.0 109.2 jit_solution(16664423640732122941)
XLA Ops:
  0.1 2.6 %project.3 = (bf16[16,576]{1,0:T(8,128)(2,1)S(1)}, f32[16,1152]{1,0:T(8,128)S(1)}, f32[16,1152]{1,0:T(8,128)S(1)}) custom-call(s32[3]{0:T(128)S(1)} %pad_add_fusion.meta.refs_0_, bf16[16,576]{1,0:T(8,128)(2,1)} %bitcast.9, f32[576]{0:T(1024)} %refs_1_.5, bf16[576,1024]{1,0:T(8,128)(2,1)} %refs_2_.4, bf16[576,512]{1,0:T(8,128)(2,1)} %refs_3_.4, ...), custom_call_target="tpu_custom_call" | custom-call | tf_op jit(solution)/shard_map/project/pallas_call | solution.py:801
  2.6 0.5 collective-permute-start
  3.2 0.7 convert_element_type.3
  4.2 4.9 %collective-permute-start.1 = (bf16[16,1152]{1,0:T(8,128)(2,1)S(1)}, bf16[16,1152]{1,0:T(8,128)(2,1)S(1)}, u32[]{:S(2)}, u32[]{:S(2)}) collective-permute-start(bf16[16,1152]{1,0:T(8,128)(2,1)S(1)} %get-tuple-element.38), channel_id=1, source_target_pairs={{0,3},{1,2},{2,1},{3,0},{4,7},{5,6},{6,5},{7,4},{8,11},{9,10},{10,... | collective-permute-start | bytes 110600 | tf_op jit(solution)/shard_map/project/ppermute | solution.py:725
  9.1 0.6 collective-permute-start.3
  9.8 1.3 %collective-permute-done.1.refs_3_ = bf16[16,1152]{1,0:T(8,128)(2,1)S(1)} collective-permute-done((bf16[16,1152]{1,0:T(8,128)(2,1)S(1)}, bf16[16,1152]{1,0:T(8,128)(2,1)S(1)}, u32[]{:S(2)}, u32[]{:S(2)}) %collective-permute-start.1) | collective-permute-done | bytes 36896 | tf_op jit(solution)/shard_map/project/ppermute | solution.py:725
  11.1 2.9 %collective-permute-done.2.refs_4_ = bf16[16,1152]{1,0:T(8,128)(2,1)S(1)} collective-permute-done((bf16[16,1152]{1,0:T(8,128)(2,1)S(1)}, bf16[16,1152]{1,0:T(8,128)(2,1)S(1)}, u32[]{:S(2)}, u32[]{:S(2)}) %collective-permute-start.2) | collective-permute-done | bytes 36896 | tf_op jit(solution)/shard_map/project/ppermute | solution.py:725
  14.3 0.8 reshape.28
  15.1 0.8 reshape.29
  15.9 8.6 %attend.5 = (f32[16,640]{1,0:T(8,128)S(1)}, f32[16,640]{1,0:T(8,128)S(1)}) custom-call(s32[35]{0:T(128)S(1)} %concatenate.14.meta, bf16[16,1024]{1,0:T(8,128)(2,1)S(1)} %get-tuple-element.39.mine, bf16[16,1024]{1,0:T(8,128)(2,1)S(1)} %collective-permute-done.4.other, bf16[8,1024,512]{2,1,0:T(8,128)(2,1)} %refs_0_.1, bf16[8,1024,512]{2,1,0:T(8,128)(2,1)} %refs_1_.6, ...), custom_call_target="tpu_custom_call" | custom-call | tf_op jit(solution)/shard_map/attend/pallas_call | solution.py:831
  24.6 0.6 collective-permute-start.5
  25.1 0.9 collective-permute-done.5.got
  26.1 1.7 %collective-permute-start.6 = (bf16[16,640]{1,0:T(8,128)(2,1)S(1)}, bf16[16,640]{1,0:T(8,128)(2,1)S(1)}, u32[]{:S(2)}, u32[]{:S(2)}) collective-permute-start(bf16[16,640]{1,0:T(8,128)(2,1)S(1)} %get-tuple-element.43), channel_id=1, source_target_pairs={{0,3},{1,2},{2,1},{3,0},{4,7},{5,6},{6,5},{7,4},{8,11},{9,10},{10,... | collective-permute-start | bytes 61448 | tf_op jit(solution)/shard_map/attend/ppermute | solution.py:725
  28.2 2.3 %collective-permute-start.8 = (bf16[16,640]{1,0:T(8,128)(2,1)S(1)}, bf16[16,640]{1,0:T(8,128)(2,1)S(1)}, u32[]{:S(2)}, u32[]{:S(2)}) collective-permute-start(bf16[16,640]{1,0:T(8,128)(2,1)S(1)} %get-tuple-element.43), channel_id=1, source_target_pairs={{0,1},{1,0},{2,3},{3,2},{4,5},{5,4},{6,7},{7,6},{8,9},{9,8},{10,11... | collective-permute-start | bytes 61448 | tf_op jit(solution)/shard_map/attend/ppermute | solution.py:725
  30.5 1.3 %collective-permute-done.6.refs_1_ = bf16[16,640]{1,0:T(8,128)(2,1)S(1)} collective-permute-done((bf16[16,640]{1,0:T(8,128)(2,1)S(1)}, bf16[16,640]{1,0:T(8,128)(2,1)S(1)}, u32[]{:S(2)}, u32[]{:S(2)}) %collective-permute-start.6) | collective-permute-done | bytes 20512 | tf_op jit(solution)/shard_map/attend/ppermute | solution.py:725
  31.8 0.7 collective-permute-done.7.refs_2_
  32.7 1.2 %collective-permute-done.9.other = bf16[16,512]{1,0:T(8,128)(2,1)S(1)} collective-permute-done((bf16[16,512]{1,0:T(8,128)(2,1)S(1)}, bf16[16,512]{1,0:T(8,128)(2,1)S(1)}, u32[]{:S(2)}, u32[]{:S(2)}) %collective-permute-start.9) | collective-permute-done | bytes 16416 | tf_op jit(solution)/shard_map/attend/ppermute | solution.py:725
  33.9 0.9 attend.8.refs_0_.refs_4_
  34.8 2.5 %collective-permute-start.10 = (f32[16,576]{1,0:T(8,128)S(1)}, f32[16,576]{1,0:T(8,128)S(1)}, u32[]{:S(2)}, u32[]{:S(2)}) collective-permute-start(f32[16,576]{1,0:T(8,128)S(1)} %attend.8.refs_0_.refs_4_), channel_id=1, source_target_pairs={{0,12},{4,8},{8,4},{12,0},{1,13},{5,9},{9,5},{13,1},{2,14},{6,10},... | collective-permute-start | bytes 110600 | tf_op jit(solution)/shard_map/attend/ppermute | solution.py:725
  37.4 0.5 collective-permute-start.11
  37.9 0.5 collective-permute-start.12
  38.3 3.6 %attend.9 = (bf16[576,5760]{1,0:T(8,128)(2,1)S(1)}, f32[8,128]{1,0:T(8,128)}) custom-call(f32[16,576]{1,0:T(8,128)S(1)} %attend.8.refs_0_.refs_4_, bf16[576,9216]{1,0:T(8,128)(2,1)} %refs_9_.1), custom_call_target="tpu_custom_call" | custom-call | bytes 13271040 | tf_op jit(solution)/shard_map/attend/pallas_call | solution.py:336
  41.9 6.7 %gate_up.4 = (f32[4,32,2432]{2,1,0:T(8,128)S(1)}, bf16[4,32,2432]{2,1,0:T(8,128)(2,1)S(1)}, f32[16,576]{1,0:T(8,128)S(1)}) custom-call(s32[3]{0:T(128)S(1)} %pad_add_fusion.meta.refs_0_, bf16[16,576]{1,0:T(8,128)(2,1)S(1)} %get-tuple-element.34.refs_1_.refs_0_, f32[576]{0:T(1024)S(1)} %copy-done.1, f32[576]{0:T(1024)S(1)} %copy-done.2, ...), custom_call_target="tpu_custom_call" | custom-call | tf_op jit(solution)/shard_map/gate_up/pallas_call | solution.py:874
  48.7 2.0 %collective-permute-done.13.got = bf16[4,32,2432]{2,1,0:T(8,128)(2,1)S(1)} collective-permute-done((bf16[4,32,2432]{2,1,0:T(8,128)(2,1)S(1)}, bf16[4,32,2432]{2,1,0:T(8,128)(2,1)S(1)}, u32[]{:S(2)}, u32[]{:S(2)}) %collective-permute-start.13) | collective-permute-done | bytes 622624 | tf_op jit(solution)/shard_map/gate_up/ppermute | solution.py:725
  51.0 2.1 %collective-permute-start.14 = (bf16[32,2432]{1,0:T(8,128)(2,1)S(1)}, bf16[32,2432]{1,0:T(8,128)(2,1)S(1)}, u32[]{:S(2)}, u32[]{:S(2)}) collective-permute-start(bf16[32,2432]{1,0:T(8,128)(2,1)S(1)} %get-tuple-element.51), channel_id=1, source_target_pairs={{0,2},{1,3},{2,0},{3,1},{4,6},{5,7},{6,4},{7,5},{8,10},{9,11},{10,... | collective-permute-start | bytes 466952 | tf_op jit(solution)/shard_map/gate_up/ppermute | solution.py:725
  53.0 2.2 %collective-permute-start.15 = (bf16[32,2432]{1,0:T(8,128)(2,1)S(1)}, bf16[32,2432]{1,0:T(8,128)(2,1)S(1)}, u32[]{:S(2)}, u32[]{:S(2)}) collective-permute-start(bf16[32,2432]{1,0:T(8,128)(2,1)S(1)} %get-tuple-element.52), channel_id=1, source_target_pairs={{0,3},{1,2},{2,1},{3,0},{4,7},{5,6},{6,5},{7,4},{8,11},{9,10},{10,... | collective-permute-start | bytes 466952 | tf_op jit(solution)/shard_map/gate_up/ppermute | solution.py:725
  55.2 9.5 %gate_up.6 = (bf16[576,9216]{1,0:T(8,128)(2,1)S(1)}, bf16[4096,2304]{1,0:T(8,128)(2,1)S(1)}, f32[8,128]{1,0:T(8,128)S(1)}) custom-call(bf16[32,2432]{1,0:T(8,128)(2,1)S(1)} %get-tuple-element.47.refs_0_, bf16[576,9216]{1,0:T(8,128)(2,1)} %bitcast.8, bf16[8192,2304]{1,0:T(8,128)(2,1)} %refs_8_.1), custom_call_target="tpu_custom_call" | custom-call | bytes 58982400 | tf_op jit(solution)/shard_map/gate_up/pallas_call | solution.py:336
  64.7 0.8 collective-permute-done.14.refs_2_
  65.5 0.5 collective-permute-done.16.refs_4_
  66.4 2.4 %collective-permute-start.17 = (bf16[16,1152]{1,0:T(8,128)(2,1)S(1)}, bf16[16,1152]{1,0:T(8,128)(2,1)S(1)}, u32[]{:S(2)}, u32[]{:S(2)}) collective-permute-start(bf16[16,1152]{1,0:T(8,128)(2,1)S(1)} %get-tuple-element.53.refs_1_), channel_id=1, source_target_pairs={{0,3},{1,2},{2,1},{3,0},{4,7},{5,6},{6,5},{7,4},{8,11},{9,10},{10,... | collective-permute-start | bytes 110600 | tf_op jit(solution)/shard_map/down/ppermute | solution.py:725
  68.9 1.7 %collective-permute-start.18 = (bf16[16,1152]{1,0:T(8,128)(2,1)S(1)}, bf16[16,1152]{1,0:T(8,128)(2,1)S(1)}, u32[]{:S(2)}, u32[]{:S(2)}) collective-permute-start(bf16[16,1152]{1,0:T(8,128)(2,1)S(1)} %get-tuple-element.53.refs_1_), channel_id=1, source_target_pairs={{0,2},{1,3},{2,0},{3,1},{4,6},{5,7},{6,4},{7,5},{8,10},{9,11},{10,... | collective-permute-start | bytes 110600 | tf_op jit(solution)/shard_map/down/ppermute | solution.py:725
  70.9 1.4 %collective-permute-done.17.refs_2_ = bf16[16,1152]{1,0:T(8,128)(2,1)S(1)} collective-permute-done((bf16[16,1152]{1,0:T(8,128)(2,1)S(1)}, bf16[16,1152]{1,0:T(8,128)(2,1)S(1)}, u32[]{:S(2)}, u32[]{:S(2)}) %collective-permute-start.17) | collective-permute-done | bytes 36896 | tf_op jit(solution)/shard_map/down/ppermute | solution.py:725
  72.3 1.4 %collective-permute-done.18.refs_3_ = bf16[16,1152]{1,0:T(8,128)(2,1)S(1)} collective-permute-done((bf16[16,1152]{1,0:T(8,128)(2,1)S(1)}, bf16[16,1152]{1,0:T(8,128)(2,1)S(1)}, u32[]{:S(2)}, u32[]{:S(2)}) %collective-permute-start.18) | collective-permute-done | bytes 36896 | tf_op jit(solution)/shard_map/down/ppermute | solution.py:725
  73.7 0.8 collective-permute-done.19.refs_4_
  74.9 0.8 collective-permute-done.23.refs_8_
  75.7 3.4 %down.2.refs_0_.refs_5_ = f32[16,576]{1,0:T(8,128)S(1)} custom-call(s32[3]{0:T(128)S(1)} %pad_add_fusion.meta.refs_0_, bf16[16,1152]{1,0:T(8,128)(2,1)S(1)} %get-tuple-element.53.refs_1_, bf16[16,1152]{1,0:T(8,128)(2,1)S(1)} %collective-permute-done.17.refs_2_, bf16[16,1152]{1,0:T(8,128)(2,1)S(1)} %collective-permute-done.18.refs_3_, ...), custom_call_target="tpu_custom_call" | custom-call | tf_op jit(solution)/shard_map/down/pallas_call | solution.py:916
  79.2 2.6 %collective-permute-start.24 = (f32[16,576]{1,0:T(8,128)S(1)}, f32[16,576]{1,0:T(8,128)S(1)}, u32[]{:S(2)}, u32[]{:S(2)}) collective-permute-start(f32[16,576]{1,0:T(8,128)S(1)} %down.2.refs_0_.refs_5_), channel_id=1, source_target_pairs={{0,12},{4,8},{8,4},{12,0},{1,13},{5,9},{9,5},{13,1},{2,14},{6,10},... | collective-permute-start | bytes 110600 | tf_op jit(solution)/shard_map/down/ppermute | solution.py:725
  81.7 0.5 collective-permute-start.25
  82.2 0.5 collective-permute-start.26
  82.7 2.4 %down.3 = (bf16[1024,2304]{1,0:T(8,128)(2,1)S(1)}, f32[8,128]{1,0:T(8,128)S(1)}) custom-call(f32[16,576]{1,0:T(8,128)S(1)} %down.2.refs_0_.refs_5_, bf16[8192,2304]{1,0:T(8,128)(2,1)} %refs_8_.1), custom_call_target="tpu_custom_call" | custom-call | bytes 9437184 | tf_op jit(solution)/shard_map/down/pallas_call | solution.py:336
  85.1 0.7 collective-permute-done.25.refs_7_
  85.7 0.5 collective-permute-done.26.refs_8_
  86.5 2.3 %collective-permute-start.27 = (bf16[48,576]{1,0:T(8,128)(2,1)S(1)}, bf16[48,576]{1,0:T(8,128)(2,1)S(1)}, u32[]{:S(2)}, u32[]{:S(2)}) collective-permute-start(bf16[48,576]{1,0:T(8,128)(2,1)S(1)} %head.4.refs_0_.refs_1_), channel_id=1, source_target_pairs={{0,3},{1,2},{2,1},{3,0},{4,7},{5,6},{6,5},{7,4},{8,11},{9,10},{10,... | collective-permute-start | bytes 165896 | tf_op jit(solution)/shard_map/head/ppermute | solution.py:725
  88.9 1.9 %collective-permute-start.29 = (bf16[48,576]{1,0:T(8,128)(2,1)S(1)}, bf16[48,576]{1,0:T(8,128)(2,1)S(1)}, u32[]{:S(2)}, u32[]{:S(2)}) collective-permute-start(bf16[48,576]{1,0:T(8,128)(2,1)S(1)} %head.4.refs_0_.refs_1_), channel_id=1, source_target_pairs={{0,1},{1,0},{2,3},{3,2},{4,5},{5,4},{6,7},{7,6},{8,9},{9,8},{10,11... | collective-permute-start | bytes 165896 | tf_op jit(solution)/shard_map/head/ppermute | solution.py:725
  90.9 3.0 %head.5 = (bf16[1024,2304]{1,0:T(8,128)(2,1)S(1)}, f32[8,128]{1,0:T(8,128)}) custom-call(bf16[48,576]{1,0:T(8,128)(2,1)S(1)} %head.4.refs_0_.refs_1_, bf16[8192,2304]{1,0:T(8,128)(2,1)} %refs_8_.1), custom_call_target="tpu_custom_call" | custom-call | bytes 9437184 | tf_op jit(solution)/shard_map/head/pallas_call | solution.py:336
  94.3 10.7 %head.6 = (f32[16,8320]{1,0:T(8,128)S(1)}, f32[16,8320]{1,0:T(8,128)S(1)}) custom-call(s32[3]{0:T(128)S(1)} %pad_add_fusion.meta.refs_0_, bf16[48,576]{1,0:T(8,128)(2,1)S(1)} %head.4.refs_0_.refs_1_, bf16[48,576]{1,0:T(8,128)(2,1)S(1)} %collective-permute-done.27.refs_2_, bf16[48,576]{1,0:T(8,128)(2,1)S(1)} %collective-permute-done.28.refs_3_, ...), custom_call_target="tpu_custom_call" | custom-call | tf_op jit(solution)/shard_map/head/pallas_call | solution.py:937
  105.3 1.6 %collective-permute-done.30.got = f32[16,8320]{1,0:T(8,128)S(1)} collective-permute-done((f32[16,8320]{1,0:T(8,128)S(1)}, f32[16,8320]{1,0:T(8,128)S(1)}, u32[]{:S(2)}, u32[]{:S(2)}) %collective-permute-start.30) | collective-permute-done | bytes 532512 | tf_op jit(solution)/shard_map/head/ppermute | solution.py:725
  107.0 2.2 %head.7 = f32[4,4096]{1,0:T(4,128)} custom-call(s32[8,2048]{1,0:T(8,128)S(1)} %reshape.26.places, f32[8,128]{1,0:T(8,128)S(1)} %broadcast_in_dim.5.weights, f32[16,8320]{1,0:T(8,128)S(1)} %get-tuple-element.61.keep, f32[16,8320]{1,0:T(8,128)S(1)} %collective-permute-done.30.got), custom_call_target="tpu_custom_call" | custom-call | tf_op jit(solution)/shard_map/head/pallas_call | solution.py:955
  (64 shorter events, 4.4 us)
Async XLA Ops:
  2.6 1.5 %collective-permute-start = (f32[16,1152]{1,0:T(8,128)S(1)}, f32[16,1152]{1,0:T(8,128)S(1)}, u32[]{:S(2)}, u32[]{:S(2)}) collective-permute-start(f32[16,1152]{1,0:T(8,128)S(1)} %get-tuple-element.36), channel_id=1, source_target_pairs={{0,16},{16,0},{1,17},{17,1},{2,18},{18,2},{3,19},{19,3},{4,20},{20... | collective-permute-start | bytes 221192 | tf_op jit(solution)/shard_map/project/ppermute | solution.py:725
  4.2 6.9 %collective-permute-start.1 = (bf16[16,1152]{1,0:T(8,128)(2,1)S(1)}, bf16[16,1152]{1,0:T(8,128)(2,1)S(1)}, u32[]{:S(2)}, u32[]{:S(2)}) collective-permute-start(bf16[16,1152]{1,0:T(8,128)(2,1)S(1)} %get-tuple-element.38), channel_id=1, source_target_pairs={{0,3},{1,2},{2,1},{3,0},{4,7},{5,6},{6,5},{7,4},{8,11},{9,10},{10,... | collective-permute-start | bytes 110600 | tf_op jit(solution)/shard_map/project/ppermute | solution.py:725
  9.1 4.9 %collective-permute-start.2 = (bf16[16,1152]{1,0:T(8,128)(2,1)S(1)}, bf16[16,1152]{1,0:T(8,128)(2,1)S(1)}, u32[]{:S(2)}, u32[]{:S(2)}) collective-permute-start(bf16[16,1152]{1,0:T(8,128)(2,1)S(1)} %get-tuple-element.38), channel_id=1, source_target_pairs={{0,2},{1,3},{2,0},{3,1},{4,6},{5,7},{6,4},{7,5},{8,10},{9,11},{10,... | collective-permute-start | bytes 110600 | tf_op jit(solution)/shard_map/project/ppermute | solution.py:725
  9.1 4.9 %collective-permute-start.3 = (bf16[16,1152]{1,0:T(8,128)(2,1)S(1)}, bf16[16,1152]{1,0:T(8,128)(2,1)S(1)}, u32[]{:S(2)}, u32[]{:S(2)}) collective-permute-start(bf16[16,1152]{1,0:T(8,128)(2,1)S(1)} %get-tuple-element.38), channel_id=1, source_target_pairs={{0,1},{1,0},{2,3},{3,2},{4,5},{5,4},{6,7},{7,6},{8,9},{9,8},{10,11... | collective-permute-start | bytes 110600 | tf_op jit(solution)/shard_map/project/ppermute | solution.py:725
  14.2 1.7 %collective-permute-start.4 = (bf16[16,1024]{1,0:T(8,128)(2,1)S(1)}, bf16[16,1024]{1,0:T(8,128)(2,1)S(1)}, u32[]{:S(2)}, u32[]{:S(2)}) collective-permute-start(bf16[16,1024]{1,0:T(8,128)(2,1)S(1)} %get-tuple-element.39.mine), channel_id=1, source_target_pairs={{0,16},{16,0},{1,17},{17,1},{2,18},{18,2},{3,19},{19,3},{4,20},{20... | collective-permute-start | bytes 98312 | tf_op jit(solution)/shard_map/project/ppermute | solution.py:725
  15.9 18.0 %copy-start = (bf16[1024,576]{0,1:T(8,128)(2,1)S(1)}, bf16[1024,576]{0,1:T(8,128)(2,1)}, u32[]{:S(2)}) copy-start(bf16[1024,576]{0,1:T(8,128)(2,1)} %param.35) | copy-start | bytes 3538948
  24.5 17.4 %copy-start.1 = (f32[576]{0:T(1024)S(1)}, f32[576]{0:T(1024)}, u32[]{:S(2)}) copy-start(f32[576]{0:T(1024)} %refs_2_.6) | copy-start | bytes 6916
  24.5 17.4 %copy-start.2 = (f32[576]{0:T(1024)S(1)}, f32[576]{0:T(1024)}, u32[]{:S(2)}) copy-start(f32[576]{0:T(1024)} %refs_3_.6) | copy-start | bytes 6916
  24.6 1.4 %collective-permute-start.5 = (f32[16,640]{1,0:T(8,128)S(1)}, f32[16,640]{1,0:T(8,128)S(1)}, u32[]{:S(2)}, u32[]{:S(2)}) collective-permute-start(f32[16,640]{1,0:T(8,128)S(1)} %get-tuple-element.41), channel_id=1, source_target_pairs={{0,16},{16,0},{1,17},{17,1},{2,18},{18,2},{3,19},{19,3},{4,20},{20... | collective-permute-start | bytes 122888 | tf_op jit(solution)/shard_map/attend/ppermute | solution.py:725
  26.1 5.7 %collective-permute-start.6 = (bf16[16,640]{1,0:T(8,128)(2,1)S(1)}, bf16[16,640]{1,0:T(8,128)(2,1)S(1)}, u32[]{:S(2)}, u32[]{:S(2)}) collective-permute-start(bf16[16,640]{1,0:T(8,128)(2,1)S(1)} %get-tuple-element.43), channel_id=1, source_target_pairs={{0,3},{1,2},{2,1},{3,0},{4,7},{5,6},{6,5},{7,4},{8,11},{9,10},{10,... | collective-permute-start | bytes 61448 | tf_op jit(solution)/shard_map/attend/ppermute | solution.py:725
  27.7 4.7 %collective-permute-start.7 = (bf16[16,640]{1,0:T(8,128)(2,1)S(1)}, bf16[16,640]{1,0:T(8,128)(2,1)S(1)}, u32[]{:S(2)}, u32[]{:S(2)}) collective-permute-start(bf16[16,640]{1,0:T(8,128)(2,1)S(1)} %get-tuple-element.43), channel_id=1, source_target_pairs={{0,2},{1,3},{2,0},{3,1},{4,6},{5,7},{6,4},{7,5},{8,10},{9,11},{10,... | collective-permute-start | bytes 61448 | tf_op jit(solution)/shard_map/attend/ppermute | solution.py:725
  28.2 4.3 %collective-permute-start.8 = (bf16[16,640]{1,0:T(8,128)(2,1)S(1)}, bf16[16,640]{1,0:T(8,128)(2,1)S(1)}, u32[]{:S(2)}, u32[]{:S(2)}) collective-permute-start(bf16[16,640]{1,0:T(8,128)(2,1)S(1)} %get-tuple-element.43), channel_id=1, source_target_pairs={{0,1},{1,0},{2,3},{3,2},{4,5},{5,4},{6,7},{7,6},{8,9},{9,8},{10,11... | collective-permute-start | bytes 61448 | tf_op jit(solution)/shard_map/attend/ppermute | solution.py:725
  32.6 1.2 %collective-permute-start.9 = (bf16[16,512]{1,0:T(8,128)(2,1)S(1)}, bf16[16,512]{1,0:T(8,128)(2,1)S(1)}, u32[]{:S(2)}, u32[]{:S(2)}) collective-permute-start(bf16[16,512]{1,0:T(8,128)(2,1)S(1)} %attend.7.mine), channel_id=1, source_target_pairs={{0,16},{16,0},{1,17},{17,1},{2,18},{18,2},{3,19},{19,3},{4,20},{20... | collective-permute-start | bytes 49160 | tf_op jit(solution)/shard_map/attend/ppermute | solution.py:725
  34.8 7.1 %collective-permute-start.10 = (f32[16,576]{1,0:T(8,128)S(1)}, f32[16,576]{1,0:T(8,128)S(1)}, u32[]{:S(2)}, u32[]{:S(2)}) collective-permute-start(f32[16,576]{1,0:T(8,128)S(1)} %attend.8.refs_0_.refs_4_), channel_id=1, source_target_pairs={{0,12},{4,8},{8,4},{12,0},{1,13},{5,9},{9,5},{13,1},{2,14},{6,10},... | collective-permute-start | bytes 110600 | tf_op jit(solution)/shard_map/attend/ppermute | solution.py:725
  37.4 4.5 %collective-permute-start.11 = (f32[16,576]{1,0:T(8,128)S(1)}, f32[16,576]{1,0:T(8,128)S(1)}, u32[]{:S(2)}, u32[]{:S(2)}) collective-permute-start(f32[16,576]{1,0:T(8,128)S(1)} %attend.8.refs_0_.refs_4_), channel_id=1, source_target_pairs={{0,8},{4,12},{8,0},{12,4},{1,9},{5,13},{9,1},{13,5},{2,10},{6,14},... | collective-permute-start | bytes 110600 | tf_op jit(solution)/shard_map/attend/ppermute | solution.py:725
  37.9 4.0 %collective-permute-start.12 = (f32[16,576]{1,0:T(8,128)S(1)}, f32[16,576]{1,0:T(8,128)S(1)}, u32[]{:S(2)}, u32[]{:S(2)}) collective-permute-start(f32[16,576]{1,0:T(8,128)S(1)} %attend.8.refs_0_.refs_4_), channel_id=1, source_target_pairs={{0,4},{4,0},{8,12},{12,8},{1,5},{5,1},{9,13},{13,9},{2,6},{6,2},{1... | collective-permute-start | bytes 110600 | tf_op jit(solution)/shard_map/attend/ppermute | solution.py:725
  48.6 2.1 %collective-permute-start.13 = (bf16[4,32,2432]{2,1,0:T(8,128)(2,1)S(1)}, bf16[4,32,2432]{2,1,0:T(8,128)(2,1)S(1)}, u32[]{:S(2)}, u32[]{:S(2)}) collective-permute-start(bf16[4,32,2432]{2,1,0:T(8,128)(2,1)S(1)} %get-tuple-element.46), channel_id=1, source_target_pairs={{0,16},{16,0},{1,17},{17,1},{2,18},{18,2},{3,19},{19,3},{4,20},{20... | collective-permute-start | bytes 1867784 | tf_op jit(solution)/shard_map/gate_up/ppermute | solution.py:725
  51.0 14.5 %collective-permute-start.14 = (bf16[32,2432]{1,0:T(8,128)(2,1)S(1)}, bf16[32,2432]{1,0:T(8,128)(2,1)S(1)}, u32[]{:S(2)}, u32[]{:S(2)}) collective-permute-start(bf16[32,2432]{1,0:T(8,128)(2,1)S(1)} %get-tuple-element.51), channel_id=1, source_target_pairs={{0,2},{1,3},{2,0},{3,1},{4,6},{5,7},{6,4},{7,5},{8,10},{9,11},{10,... | collective-permute-start | bytes 466952 | tf_op jit(solution)/shard_map/gate_up/ppermute | solution.py:725
  53.0 12.5 %collective-permute-start.15 = (bf16[32,2432]{1,0:T(8,128)(2,1)S(1)}, bf16[32,2432]{1,0:T(8,128)(2,1)S(1)}, u32[]{:S(2)}, u32[]{:S(2)}) collective-permute-start(bf16[32,2432]{1,0:T(8,128)(2,1)S(1)} %get-tuple-element.52), channel_id=1, source_target_pairs={{0,3},{1,2},{2,1},{3,0},{4,7},{5,6},{6,5},{7,4},{8,11},{9,10},{10,... | collective-permute-start | bytes 466952 | tf_op jit(solution)/shard_map/gate_up/ppermute | solution.py:725
  55.2 10.8 %collective-permute-start.16 = (bf16[32,2432]{1,0:T(8,128)(2,1)S(1)}, bf16[32,2432]{1,0:T(8,128)(2,1)S(1)}, u32[]{:S(2)}, u32[]{:S(2)}) collective-permute-start(bf16[32,2432]{1,0:T(8,128)(2,1)S(1)} %get-tuple-element.47.refs_0_), channel_id=1, source_target_pairs={{0,1},{1,0},{2,3},{3,2},{4,5},{5,4},{6,7},{7,6},{8,9},{9,8},{10,11... | collective-permute-start | bytes 466952 | tf_op jit(solution)/shard_map/gate_up/ppermute | solution.py:725
  66.4 5.9 %collective-permute-start.17 = (bf16[16,1152]{1,0:T(8,128)(2,1)S(1)}, bf16[16,1152]{1,0:T(8,128)(2,1)S(1)}, u32[]{:S(2)}, u32[]{:S(2)}) collective-permute-start(bf16[16,1152]{1,0:T(8,128)(2,1)S(1)} %get-tuple-element.53.refs_1_), channel_id=1, source_target_pairs={{0,3},{1,2},{2,1},{3,0},{4,7},{5,6},{6,5},{7,4},{8,11},{9,10},{10,... | collective-permute-start | bytes 110600 | tf_op jit(solution)/shard_map/down/ppermute | solution.py:725
  68.9 4.9 %collective-permute-start.18 = (bf16[16,1152]{1,0:T(8,128)(2,1)S(1)}, bf16[16,1152]{1,0:T(8,128)(2,1)S(1)}, u32[]{:S(2)}, u32[]{:S(2)}) collective-permute-start(bf16[16,1152]{1,0:T(8,128)(2,1)S(1)} %get-tuple-element.53.refs_1_), channel_id=1, source_target_pairs={{0,2},{1,3},{2,0},{3,1},{4,6},{5,7},{6,4},{7,5},{8,10},{9,11},{10,... | collective-permute-start | bytes 110600 | tf_op jit(solution)/shard_map/down/ppermute | solution.py:725
  70.6 4.0 %collective-permute-start.19 = (bf16[16,1152]{1,0:T(8,128)(2,1)S(1)}, bf16[16,1152]{1,0:T(8,128)(2,1)S(1)}, u32[]{:S(2)}, u32[]{:S(2)}) collective-permute-start(bf16[16,1152]{1,0:T(8,128)(2,1)S(1)} %get-tuple-element.53.refs_1_), channel_id=1, source_target_pairs={{0,1},{1,0},{2,3},{3,2},{4,5},{5,4},{6,7},{7,6},{8,9},{9,8},{10,11... | collective-permute-start | bytes 110600 | tf_op jit(solution)/shard_map/down/ppermute | solution.py:725
  70.9 3.6 %collective-permute-start.20 = (bf16[16,1152]{1,0:T(8,128)(2,1)S(1)}, bf16[16,1152]{1,0:T(8,128)(2,1)S(1)}, u32[]{:S(2)}, u32[]{:S(2)}) collective-permute-start(bf16[16,1152]{1,0:T(8,128)(2,1)S(1)} %get-tuple-element.53.refs_1_), channel_id=1, source_target_pairs={{0,16},{16,0},{1,17},{17,1},{2,18},{18,2},{3,19},{19,3},{4,20},{20... | collective-permute-start | bytes 110600 | tf_op jit(solution)/shard_map/down/ppermute | solution.py:725
  72.3 2.2 %collective-permute-start.21 = (bf16[16,1152]{1,0:T(8,128)(2,1)S(1)}, bf16[16,1152]{1,0:T(8,128)(2,1)S(1)}, u32[]{:S(2)}, u32[]{:S(2)}) collective-permute-start(bf16[16,1152]{1,0:T(8,128)(2,1)S(1)} %collective-permute-done.17.refs_2_), channel_id=1, source_target_pairs={{0,16},{16,0},{1,17},{17,1},{2,18},{18,2},{3,19},{19,3},{4,20},{20... | collective-permute-start | bytes 110600 | tf_op jit(solution)/shard_map/down/ppermute | solution.py:725
  73.7 1.2 %collective-permute-start.22 = (bf16[16,1152]{1,0:T(8,128)(2,1)S(1)}, bf16[16,1152]{1,0:T(8,128)(2,1)S(1)}, u32[]{:S(2)}, u32[]{:S(2)}) collective-permute-start(bf16[16,1152]{1,0:T(8,128)(2,1)S(1)} %collective-permute-done.18.refs_3_), channel_id=1, source_target_pairs={{0,16},{16,0},{1,17},{17,1},{2,18},{18,2},{3,19},{19,3},{4,20},{20... | collective-permute-start | bytes 110600 | tf_op jit(solution)/shard_map/down/ppermute | solution.py:725
  74.5 1.2 %collective-permute-start.23 = (bf16[16,1152]{1,0:T(8,128)(2,1)S(1)}, bf16[16,1152]{1,0:T(8,128)(2,1)S(1)}, u32[]{:S(2)}, u32[]{:S(2)}) collective-permute-start(bf16[16,1152]{1,0:T(8,128)(2,1)S(1)} %collective-permute-done.19.refs_4_), channel_id=1, source_target_pairs={{0,16},{16,0},{1,17},{17,1},{2,18},{18,2},{3,19},{19,3},{4,20},{20... | collective-permute-start | bytes 110600 | tf_op jit(solution)/shard_map/down/ppermute | solution.py:725
  79.1 7.1 %copy-start.3 = (f32[576]{0:T(1024)S(1)}, f32[576]{0:T(1024)}, u32[]{:S(2)}) copy-start(f32[576]{0:T(1024)} %refs_3_.7) | copy-start | bytes 6916
  79.1 7.1 %copy-start.4 = (f32[576]{0:T(1024)S(1)}, f32[576]{0:T(1024)}, u32[]{:S(2)}) copy-start(f32[576]{0:T(1024)} %refs_4_.3) | copy-start | bytes 6916
  79.2 5.9 %collective-permute-start.24 = (f32[16,576]{1,0:T(8,128)S(1)}, f32[16,576]{1,0:T(8,128)S(1)}, u32[]{:S(2)}, u32[]{:S(2)}) collective-permute-start(f32[16,576]{1,0:T(8,128)S(1)} %down.2.refs_0_.refs_5_), channel_id=1, source_target_pairs={{0,12},{4,8},{8,4},{12,0},{1,13},{5,9},{9,5},{13,1},{2,14},{6,10},... | collective-permute-start | bytes 110600 | tf_op jit(solution)/shard_map/down/ppermute | solution.py:725
  81.7 4.0 %collective-permute-start.25 = (f32[16,576]{1,0:T(8,128)S(1)}, f32[16,576]{1,0:T(8,128)S(1)}, u32[]{:S(2)}, u32[]{:S(2)}) collective-permute-start(f32[16,576]{1,0:T(8,128)S(1)} %down.2.refs_0_.refs_5_), channel_id=1, source_target_pairs={{0,8},{4,12},{8,0},{12,4},{1,9},{5,13},{9,1},{13,5},{2,10},{6,14},... | collective-permute-start | bytes 110600 | tf_op jit(solution)/shard_map/down/ppermute | solution.py:725
  82.2 4.0 %collective-permute-start.26 = (f32[16,576]{1,0:T(8,128)S(1)}, f32[16,576]{1,0:T(8,128)S(1)}, u32[]{:S(2)}, u32[]{:S(2)}) collective-permute-start(f32[16,576]{1,0:T(8,128)S(1)} %down.2.refs_0_.refs_5_), channel_id=1, source_target_pairs={{0,4},{4,0},{8,12},{12,8},{1,5},{5,1},{9,13},{13,9},{2,6},{6,2},{1... | collective-permute-start | bytes 110600 | tf_op jit(solution)/shard_map/down/ppermute | solution.py:725
  86.5 7.4 %collective-permute-start.27 = (bf16[48,576]{1,0:T(8,128)(2,1)S(1)}, bf16[48,576]{1,0:T(8,128)(2,1)S(1)}, u32[]{:S(2)}, u32[]{:S(2)}) collective-permute-start(bf16[48,576]{1,0:T(8,128)(2,1)S(1)} %head.4.refs_0_.refs_1_), channel_id=1, source_target_pairs={{0,3},{1,2},{2,1},{3,0},{4,7},{5,6},{6,5},{7,4},{8,11},{9,10},{10,... | collective-permute-start | bytes 165896 | tf_op jit(solution)/shard_map/head/ppermute | solution.py:725
  88.8 5.5 %collective-permute-start.28 = (bf16[48,576]{1,0:T(8,128)(2,1)S(1)}, bf16[48,576]{1,0:T(8,128)(2,1)S(1)}, u32[]{:S(2)}, u32[]{:S(2)}) collective-permute-start(bf16[48,576]{1,0:T(8,128)(2,1)S(1)} %head.4.refs_0_.refs_1_), channel_id=1, source_target_pairs={{0,2},{1,3},{2,0},{3,1},{4,6},{5,7},{6,4},{7,5},{8,10},{9,11},{10,... | collective-permute-start | bytes 165896 | tf_op jit(solution)/shard_map/head/ppermute | solution.py:725
  88.9 5.3 %collective-permute-start.29 = (bf16[48,576]{1,0:T(8,128)(2,1)S(1)}, bf16[48,576]{1,0:T(8,128)(2,1)S(1)}, u32[]{:S(2)}, u32[]{:S(2)}) collective-permute-start(bf16[48,576]{1,0:T(8,128)(2,1)S(1)} %head.4.refs_0_.refs_1_), channel_id=1, source_target_pairs={{0,1},{1,0},{2,3},{3,2},{4,5},{5,4},{6,7},{7,6},{8,9},{9,8},{10,11... | collective-permute-start | bytes 165896 | tf_op jit(solution)/shard_map/head/ppermute | solution.py:725
  94.2 10.8 %copy-start.5 = (s32[4096]{0:T(1024)S(1)}, s32[4096]{0:T(1024)}, u32[]{:S(2)}) copy-start(s32[4096]{0:T(1024)} %param.25) | copy-start | bytes 49156
  94.2 10.9 %copy-start.6 = (f32[8]{0:T(128)S(1)}, f32[8]{0:T(128)}, u32[]{:S(2)}) copy-start(f32[8]{0:T(128)} %param.26) | copy-start | bytes 100
  105.0 2.0 %collective-permute-start.30 = (f32[16,8320]{1,0:T(8,128)S(1)}, f32[16,8320]{1,0:T(8,128)S(1)}, u32[]{:S(2)}, u32[]{:S(2)}) collective-permute-start(f32[16,8320]{1,0:T(8,128)S(1)} %get-tuple-element.62), channel_id=1, source_target_pairs={{0,16},{16,0},{1,17},{17,1},{2,18},{18,2},{3,19},{19,3},{4,20},{20... | collective-permute-start | bytes 1597448 | tf_op jit(solution)/shard_map/head/ppermute | solution.py:725
